TPU v7x, 32 devices: a whole 2x2x4 slice. The times are simulated.
32 devices in a mesh: mem: 4 (over y, x), col: 8 (over z, core).
Axes of the slice: x: 2, y: 2, z: 4, core: 2. Of those that a mesh axis runs over, the one named last changes fastest.
Arguments:
- adj_final: float32 [16, 137, 4096], P('mem', None, 'col'), parts along dimension 0, may hold values from -60 to 60
- inverses: float32 [8, 32, 137, 137], P('mem', 'col'), parts along dimension 0, may hold values from 0 to 1
- dep_lists: int32 [8, 32, 5], P('mem', 'col'), parts along dimension 0, may hold values from 0 to 31, as said below
- dep_points: int32 [8, 4, 4096], P('mem', None, 'col'), parts along dimension 0, may hold values from 0 to 639, as said below
- weights: float32 [8, 4, 4096], P('mem', None, 'col'), parts along dimension 0, may hold values from 0 to 1, as said below
Outputs:
- adj_mid: float32 [16, 137, 4096], P('mem', None, 'col'), parts along dimension 0
- lanczos: float32 [16, 137, 4096], P('mem', None, 'col'), parts along dimension 0
There are 4 independent parts, one for each index of `mem`. A program takes and returns all parts, laid end to end along the dimension named above; each array names one. Nothing has to cross between parts.
Inputs may be any that keep to these rules, and one draw needn't show every extreme that they name: `dep_lists`: every entry of a block's list is a block within 2 blocks of that block, counting cyclically over all 32 blocks; the list's first entries are distinct and the rest repeat the block itself. `dep_points`: the slot of every point indexes one of the first entries of its arrival block's list. The 4 weights of a column are bilinear weights and sum to one.
All inputs are finite; a program needn't handle non-finite values.
Results may differ from a plain program's by a relative error of at most 0.0003.
Values sent between devices are 32-bit elements; how exact they have to be, the bound alone decides.
No kernel may reach another device: no remote copies, remote signals or barrier semaphores. Data moves between devices by JAX's collectives and lax.ppermute only.
A program may use at most 64 MiB of HBM per device.

v0:
```python
import jax
import jax.numpy as jnp
from jax import lax
from jax.sharding import PartitionSpec as P

BCOLS = 128
REACH = 2
SLOTS = 5
POINTS = 4
STEPS = 2


eps_energy = 1e-06


def passed_along(value, axis, steps):
    count = lax.axis_size(axis)
    pairs = [(source, (source + steps) % count) for source in range(count)]
    return lax.ppermute(value, axis, pairs)


def slot_matrix(block_points, block_weights, slot_number):
    slot_ids = block_points // BCOLS
    within = block_points % BCOLS
    chosen = jnp.where(slot_ids == slot_number, block_weights, 0.0)
    columns = lax.broadcasted_iota(jnp.int32, (1, 1, BCOLS), 2)
    one_hot = (within[:, :, None] == columns).astype(jnp.float32)
    return jnp.sum(one_hot * chosen[:, :, None], axis=0)


def add_block(accumulated, block_rows, block_points, block_weights, route_row, locate, slot_limit):

    def one_slot(slot_number, current):
        matrix = slot_matrix(block_points, block_weights, slot_number)
        partial_block = jnp.dot(
            block_rows, matrix, precision=lax.Precision.HIGHEST, preferred_element_type=jnp.float32
        )
        position, inside = locate(route_row[slot_number])
        previous = lax.dynamic_slice_in_dim(current, position, 1, 1)
        return lax.dynamic_update_slice_in_dim(
            current, previous + inside * partial_block[:, None, :], position, 1
        )

    return lax.fori_loop(0, slot_limit, one_slot, accumulated)


def over_blocks(
    accumulated, rows_all, point_blocks, weight_blocks, route_table, block_total, locate
):

    def one_block(block_index, current):
        block_rows = lax.dynamic_index_in_dim(rows_all, block_index, 1, keepdims=False)
        block_points = lax.dynamic_index_in_dim(point_blocks, block_index, 1, keepdims=False)
        block_weights = lax.dynamic_index_in_dim(weight_blocks, block_index, 1, keepdims=False)
        route_row = lax.dynamic_index_in_dim(route_table, block_index, 0, keepdims=False)
        slot_limit = SLOTS
        return add_block(
            current, block_rows, block_points, block_weights, route_row, locate, slot_limit
        )

    return lax.fori_loop(0, block_total, one_block, accumulated)


def spread(adjoint, inverse, routes, points, weights):
    variables, levels, col_count = adjoint.shape
    block_count = col_count // BCOLS
    row_count = variables * levels
    all_blocks = lax.axis_size("col") * block_count
    first_block = lax.axis_index("col") * block_count
    blocked = adjoint.reshape(variables, levels, block_count, BCOLS)
    diffused = jnp.einsum("blk,vlbc->vkbc", inverse, blocked, precision=lax.Precision.HIGHEST)
    diffused = diffused.reshape(row_count, block_count, BCOLS)
    point_blocks = points.reshape(POINTS, block_count, BCOLS)
    weight_blocks = weights.reshape(POINTS, block_count, BCOLS)

    def locate_near(target):
        return ((target - first_block + REACH) % all_blocks, 1.0)

    extended = jnp.zeros((row_count, block_count + 2 * REACH, BCOLS), jnp.float32)
    extended = over_blocks(
        extended, diffused, point_blocks, weight_blocks, routes, block_count, locate_near
    )
    from_below = passed_along(extended[:, block_count + REACH :], "col", 1)
    from_above = passed_along(extended[:, :REACH], "col", -1)
    owned = extended[:, REACH : REACH + block_count]
    owned = owned.at[:, :REACH].add(from_below)
    owned = owned.at[:, block_count - REACH :].add(from_above)
    return owned.reshape(variables, levels, col_count)


def shards(adj_final, inverses, dep_lists, dep_points, weights):
    adjoint = adj_final
    adj_mid = adj_final
    for step_index in range(STEPS - 1, -1, -1):
        adjoint = spread(
            adjoint,
            inverses[step_index],
            dep_lists[step_index],
            dep_points[step_index],
            weights[step_index],
        )
        if step_index == STEPS - 1:
            adj_mid = adjoint
    local_sum = jnp.sum(adjoint * adjoint)
    energy = lax.psum(local_sum, "col")
    cell_count = adjoint.size * lax.axis_size("col")
    lanczos = adjoint / jnp.sqrt(energy / cell_count + eps_energy)
    return (adj_mid, lanczos)


def solution(mesh):
    in_specs = (
        P("mem", None, "col"),
        P("mem", "col", None, None),
        P("mem", "col", None),
        P("mem", None, "col"),
        P("mem", None, "col"),
    )
    out_specs = (P("mem", None, "col"), P("mem", None, "col"))
    return jax.shard_map(shards, mesh=mesh, in_specs=in_specs, out_specs=out_specs, check_vma=False)
```

profile of v0, /device:TPU:0, one launch (start us, length us, event | category | flops | bytes accessed | tf_op | source)
XLA Modules:
  0.0 172.8 jit_solution(14304932874438624361)
XLA Ops:
  2.9 1.9 %reshape.295 = f32[4,137,4,128]{3,2,0,1:T(4,128)S(1)} reshape(f32[4,137,512]{2,0,1:T(4,128)} %param.21) | data formatting | bytes 2244608 | tf_op jit(solution)/shard_map/reshape | solution.py:70
  5.3 1.5 convolution_bitcast_fusion.3
  6.9 1.7 copy.43
  8.8 47.3 %while.97 = (s32[]{:T(128)}, f32[548,8,128]{2,0,1:T(8,128)S(1)}, s32[4,4,128]{2,0,1:T(4,128)S(1)}, f32[4,4,128]{2,0,1:T(4,128)S(1)}, f32[548,4,128]{2,1,0:T(4,12...) while((s32[]{:T(128)}, f32[548,8,128]{2,0,1:T(8,128)S(1)}, ...), condition=%wide.region_4.5_spmd, body=%wide.region_0.4_spmd.sunk | while | flops 108005904 | bytes 2138801 | solution.py:61
  8.8 1.5 constant_dynamic-slice_fusion.6
  10.4 10.2 %while.100 = (s32[]{:T(128)}, f32[548,8,128]{2,0,1:T(8,128)S(1)}, s32[5]{0:T(128)S(1)}, s32[]{:T(128)}, s32[4,128]{1,0:T(4,128)S(1)}, /*index=5*/s32[4,128]{1,0:...) while((s32[]{:T(128)}, f32[548,8,128]{2,0,1:T(8,128)S(1)}, ...), condition=%wide.region_3.3_spmd, body=%wide.region_1.2_spmd.sunk | while | flops 108004368 | bytes 999768 | solution.py:44
  20.7 1.5 constant_dynamic-slice_fusion.6
  22.2 10.2 %while.100 = (s32[]{:T(128)}, f32[548,8,128]{2,0,1:T(8,128)S(1)}, s32[5]{0:T(128)S(1)}, s32[]{:T(128)}, s32[4,128]{1,0:T(4,128)S(1)}, /*index=5*/s32[4,128]{1,0:...) while((s32[]{:T(128)}, f32[548,8,128]{2,0,1:T(8,128)S(1)}, ...), condition=%wide.region_3.3_spmd, body=%wide.region_1.2_spmd.sunk | while | flops 108004368 | bytes 999768 | solution.py:44
  32.5 1.5 constant_dynamic-slice_fusion.6
  34.0 10.2 %while.100 = (s32[]{:T(128)}, f32[548,8,128]{2,0,1:T(8,128)S(1)}, s32[5]{0:T(128)S(1)}, s32[]{:T(128)}, s32[4,128]{1,0:T(4,128)S(1)}, /*index=5*/s32[4,128]{1,0:...) while((s32[]{:T(128)}, f32[548,8,128]{2,0,1:T(8,128)S(1)}, ...), condition=%wide.region_3.3_spmd, body=%wide.region_1.2_spmd.sunk | while | flops 108004368 | bytes 999768 | solution.py:44
  44.3 1.5 constant_dynamic-slice_fusion.6
  45.8 10.2 %while.100 = (s32[]{:T(128)}, f32[548,8,128]{2,0,1:T(8,128)S(1)}, s32[5]{0:T(128)S(1)}, s32[]{:T(128)}, s32[4,128]{1,0:T(4,128)S(1)}, /*index=5*/s32[4,128]{1,0:...) while((s32[]{:T(128)}, f32[548,8,128]{2,0,1:T(8,128)S(1)}, ...), condition=%wide.region_3.3_spmd, body=%wide.region_1.2_spmd.sunk | while | flops 108004368 | bytes 999768 | solution.py:44
  59.4 4.0 %collective-permute-start.1 = (f32[548,2,128]{2,1,0:T(2,128)S(1)}, f32[548,2,128]{2,1,0:T(2,128)S(1)}, u32[]{:S(2)}, u32[]{:S(2)}) collective-permute-start(f32[548,2,128]{2,1,0:T(2,128)S(1)} %get-tuple-element.1194), channel_id=1, source_target_pairs={{0,7},{1,0},{2,1},{3,2},{4,3},{5,4},{6,5},{7,6},{8,15},{9,8},{10,9... | collective-permute-start | bytes 1683464 | tf_op jit(solution)/shard_map/ppermute | solution.py:19
  63.5 1.9 %slice.158 = f32[548,4,128]{2,1,0:T(4,128)S(1)} slice(f32[548,8,128]{2,1,0:T(8,128)} %copy-done.2), slice={[0:548], [2:6], [0:128]} | slice | bytes 2244608 | tf_op jit(solution)/shard_map/slice | solution.py:85
  65.7 8.9 %collective-permute-done = f32[548,2,128]{2,1,0:T(2,128)} collective-permute-done((f32[548,2,128]{2,1,0:T(2,128)}, f32[548,2,128]{2,1,0:T(2,128)}, u32[]{:S(2)}, u32[]{:S(2)}) %collective-permute-start) | collective-permute-done | bytes 561184 | tf_op jit(solution)/shard_map/ppermute | solution.py:19
  74.6 2.3 %fusion.19 = f32[548,4,128]{2,1,0:T(4,128)S(1)} fusion(f32[548,4,128]{2,1,0:T(4,128)S(1)} %slice.158, f32[548,2,128]{2,1,0:T(2,128)} %collective-permute-done, f32[548,8,128]{2,1,0:T(8,128)} %copy-done.2), kind=kLoop, calls=%fused_computation.60 | loop fusion | flops 140288 | bytes 1683456 | tf_op jit(solution)/shard_map/scatter-add | solution.py:86
  78.8 1.7 copy.51
  80.7 49.3 %while.99 = (s32[]{:T(128)}, f32[548,8,128]{2,0,1:T(8,128)S(1)}, s32[4,4,128]{2,0,1:T(4,128)S(1)}, f32[4,4,128]{2,0,1:T(4,128)S(1)}, f32[548,4,128]{2,1,0:T(4,12...) while((s32[]{:T(128)}, f32[548,8,128]{2,0,1:T(8,128)S(1)}, ...), condition=%wide.region_9.10_spmd, body=%wide.region_5.9_spmd.sunk | while | flops 108005904 | bytes 2138801 | solution.py:61
  80.8 1.5 constant_dynamic-slice_fusion.7
  82.3 10.7 %while.101 = (s32[]{:T(128)}, f32[548,8,128]{2,0,1:T(8,128)S(1)}, s32[5]{0:T(128)S(1)}, s32[]{:T(128)}, s32[4,128]{1,0:T(4,128)S(1)}, /*index=5*/s32[4,128]{1,0:...) while((s32[]{:T(128)}, f32[548,8,128]{2,0,1:T(8,128)S(1)}, ...), condition=%wide.region_8.8_spmd, body=%wide.region_6.7_spmd.sunk | while | flops 108004368 | bytes 999768 | solution.py:44
  93.1 1.5 constant_dynamic-slice_fusion.7
  94.6 10.7 %while.101 = (s32[]{:T(128)}, f32[548,8,128]{2,0,1:T(8,128)S(1)}, s32[5]{0:T(128)S(1)}, s32[]{:T(128)}, s32[4,128]{1,0:T(4,128)S(1)}, /*index=5*/s32[4,128]{1,0:...) while((s32[]{:T(128)}, f32[548,8,128]{2,0,1:T(8,128)S(1)}, ...), condition=%wide.region_8.8_spmd, body=%wide.region_6.7_spmd.sunk | while | flops 108004368 | bytes 999768 | solution.py:44
  105.4 1.5 constant_dynamic-slice_fusion.7
  107.0 10.7 %while.101 = (s32[]{:T(128)}, f32[548,8,128]{2,0,1:T(8,128)S(1)}, s32[5]{0:T(128)S(1)}, s32[]{:T(128)}, s32[4,128]{1,0:T(4,128)S(1)}, /*index=5*/s32[4,128]{1,0:...) while((s32[]{:T(128)}, f32[548,8,128]{2,0,1:T(8,128)S(1)}, ...), condition=%wide.region_8.8_spmd, body=%wide.region_6.7_spmd.sunk | while | flops 108004368 | bytes 999768 | solution.py:44
  119.3 10.7 %while.101 = (s32[]{:T(128)}, f32[548,8,128]{2,0,1:T(8,128)S(1)}, s32[5]{0:T(128)S(1)}, s32[]{:T(128)}, s32[4,128]{1,0:T(4,128)S(1)}, /*index=5*/s32[4,128]{1,0:...) while((s32[]{:T(128)}, f32[548,8,128]{2,0,1:T(8,128)S(1)}, ...), condition=%wide.region_8.8_spmd, body=%wide.region_6.7_spmd.sunk | while | flops 108004368 | bytes 999768 | solution.py:44
  133.1 3.5 %collective-permute-start.3 = (f32[548,2,128]{2,1,0:T(2,128)}, f32[548,2,128]{2,1,0:T(2,128)}, u32[]{:S(2)}, u32[]{:S(2)}) collective-permute-start(f32[548,2,128]{2,1,0:T(2,128)} %get-tuple-element.1192), channel_id=1, source_target_pairs={{0,7},{1,0},{2,1},{3,2},{4,3},{5,4},{6,5},{7,6},{8,15},{9,8},{10,9... | collective-permute-start | bytes 1683464 | tf_op jit(solution)/shard_map/ppermute | solution.py:19
  138.4 8.5 %collective-permute-done.2 = f32[548,2,128]{2,1,0:T(2,128)} collective-permute-done((f32[548,2,128]{2,1,0:T(2,128)}, f32[548,2,128]{2,1,0:T(2,128)}, u32[]{:S(2)}, u32[]{:S(2)}) %collective-permute-start.2) | collective-permute-done | bytes 561184 | tf_op jit(solution)/shard_map/ppermute | solution.py:19
  146.9 1.7 fusion.17
  148.6 1.7 %fusion.16 = f32[548,4,128]{2,1,0:T(4,128)S(1)} fusion(f32[548,4,128]{2,1,0:T(4,128)S(1)} %fusion.17, f32[548,2,128]{2,1,0:T(2,128)} %collective-permute-done.3), kind=kLoop, calls=%fused_computation.54 | loop fusion | flops 140288 | bytes 1683456 | tf_op jit(solution)/shard_map/scatter-add | solution.py:87
  151.5 1.7 copy.57
  153.2 16.6 %psum.7 = f32[]{:T(128)} all-reduce(f32[]{:T(128)} %multiply_reduce_fusion), channel_id=1, replica_groups=mesh['mem'=4,'col'=8] {'col'}, use_global_device_ids=true, to_apply=%region_11.12 | all-reduce | flops 1 | bytes 8 | tf_op jit(solution)/shard_map/psum | solution.py:105
  171.1 1.7 copy.58
  (278 shorter events, 74.3 us)
Async XLA Ops:
  0.6 4.2 %copy-start.6 = (f32[2,4,137,137]{3,1,2,0:T(4,128)S(1)}, f32[2,4,137,137]{3,1,2,0:T(4,128)}, u32[]{:S(2)}) copy-start(f32[2,4,137,137]{3,1,2,0:T(4,128)} %param.22) | copy-start | bytes 1801828
  56.5 1.4 copy-start.2
  59.0 15.6 %collective-permute-start = (f32[548,2,128]{2,1,0:T(2,128)}, f32[548,2,128]{2,1,0:T(2,128)}, u32[]{:S(2)}, u32[]{:S(2)}) collective-permute-start(f32[548,2,128]{2,1,0:T(2,128)} %get-tuple-element.1195), channel_id=1, source_target_pairs={{0,1},{1,2},{2,3},{3,4},{4,5},{5,6},{6,7},{7,0},{8,9},{9,10},{10,1... | collective-permute-start | bytes 1683464 | tf_op jit(solution)/shard_map/ppermute | solution.py:19
  59.4 17.5 %collective-permute-start.1 = (f32[548,2,128]{2,1,0:T(2,128)S(1)}, f32[548,2,128]{2,1,0:T(2,128)S(1)}, u32[]{:S(2)}, u32[]{:S(2)}) collective-permute-start(f32[548,2,128]{2,1,0:T(2,128)S(1)} %get-tuple-element.1194), channel_id=1, source_target_pairs={{0,7},{1,0},{2,1},{3,2},{4,3},{5,4},{6,5},{7,6},{8,15},{9,8},{10,9... | collective-permute-start | bytes 1683464 | tf_op jit(solution)/shard_map/ppermute | solution.py:19
  77.6 1.2 copy-start
  130.4 1.4 copy-start.3
  131.8 4.9 %copy-start.1 = (f32[548,4,128]{2,1,0:T(4,128)S(1)}, f32[548,4,128]{2,1,0:T(4,128)}, u32[]{:S(2)}) copy-start(f32[548,4,128]{2,1,0:T(4,128)} %copy-done) | copy-start | bytes 3366916
  133.1 5.0 %copy-start.4 = (f32[548,8,128]{2,1,0:T(8,128)S(1)}, f32[548,8,128]{2,1,0:T(8,128)}, u32[]{:S(2)}) copy-start(f32[548,8,128]{2,1,0:T(8,128)} %copy-done.3) | copy-start | bytes 6733828
  133.1 13.8 %collective-permute-start.2 = (f32[548,2,128]{2,1,0:T(2,128)}, f32[548,2,128]{2,1,0:T(2,128)}, u32[]{:S(2)}, u32[]{:S(2)}) collective-permute-start(f32[548,2,128]{2,1,0:T(2,128)} %get-tuple-element.1193), channel_id=1, source_target_pairs={{0,1},{1,2},{2,3},{3,4},{4,5},{5,6},{6,7},{7,0},{8,9},{9,10},{10,1... | collective-permute-start | bytes 1683464 | tf_op jit(solution)/shard_map/ppermute | solution.py:19
  133.1 15.5 %collective-permute-start.3 = (f32[548,2,128]{2,1,0:T(2,128)}, f32[548,2,128]{2,1,0:T(2,128)}, u32[]{:S(2)}, u32[]{:S(2)}) collective-permute-start(f32[548,2,128]{2,1,0:T(2,128)} %get-tuple-element.1192), channel_id=1, source_target_pairs={{0,7},{1,0},{2,1},{3,2},{4,3},{5,4},{6,5},{7,6},{8,15},{9,8},{10,9... | collective-permute-start | bytes 1683464 | tf_op jit(solution)/shard_map/ppermute | solution.py:19
  148.6 2.9 %copy-start.5 = (f32[4,137,512]{2,1,0:T(8,128)S(1)}, f32[4,137,512]{2,1,0:T(8,128)}, u32[]{:S(2)}) copy-start(f32[4,137,512]{2,1,0:T(8,128)} %reshape.297) | copy-start | bytes 3366916
where the time goes:
time: 174 us; the launch traced here: 173 us
  local copies, waits for them, and re-layouts  58.9 us (34%)
  matrix products  26.9 us (15%)
  loops' own time  26.9 us (15%)
  waiting for transfers between devices  17.5 us (10%)
  other arithmetic  16.6 us (10%)
  blocking collectives  16.6 us (10%)
  starting transfers between devices  8.03 us (5%)
    another operation x8, loops' own time, add_block(): return lax.fori_loop(0, slot_limit, one_slot, accumulated)  26.4 us
    dynamic_slice x40, local copies, waits for them, and re-layouts, one_slot(): position, inside = locate(route_row[slot_number])  24.3 us
    dot_general x40, matrix products, one_slot(): jnp.dot(block_rows, matrix, precision=lax.Precision.HIGHEST, preferred_el...  24.1 us
    ppermute x4, waiting for transfers between devices, passed_along(): return lax.ppermute(value, axis, pairs)  17.5 us
    psum x1, blocking collectives, shards(): energy = lax.psum(local_sum, 'col')  16.6 us
    dynamic_slice x16, local copies, waits for them, and re-layouts, one_block(): lax.dynamic_index_in_dim(rows_all, block_index, 1, keepdims=False)  12.2 us
    ppermute x4, starting transfers between devices, passed_along(): return lax.ppermute(value, axis, pairs)  8.03 us
    reduce_sum x40, other arithmetic, slot_matrix(): return jnp.sum(one_hot * chosen[:, :, None], axis=0)  8 us
  transfers between devices with their start and end apart: 4, of which 2 were waited for; matrix products, arithmetic and copies ran while one was open for 5% of the time, Pallas kernels for 0%

commit v1 on v0

v1 whole, which is shorter than its diff:
```python
import functools

import jax
import jax.numpy as jnp
from jax import lax
from jax.experimental import pallas as pl
from jax.experimental.pallas import tpu as pltpu
from jax.sharding import PartitionSpec as P

BCOLS = 128
REACH = 2
SLOTS = 5
POINTS = 4
STEPS = 2
EDGE = REACH * BCOLS
CHUNKS = 2
VMEM_LIMIT = 32 * 1024 * 1024

eps_energy = 1e-06

F32 = jnp.float32
BF16 = jnp.bfloat16
ANY = pl.BlockSpec(memory_space=pl.ANY)


def padded(count):
    return -(-count // 8) * 8


def z_side(block_count):
    follows = lax.rem(lax.axis_index("col"), 2)
    first = follows * (block_count - REACH)
    return follows, first, follows * (block_count + REACH) - REACH


def core_side(block_count):
    follows = 1 - lax.rem(lax.axis_index("col"), 2)
    first = follows * (block_count - REACH)
    return follows, first, follows * (block_count + REACH) - REACH


def lanes(block, count):
    return pl.ds(pl.multiple_of(block * BCOLS, BCOLS), count * BCOLS)


def split(value):
    high = value.astype(BF16)
    return high, (value - high.astype(F32)).astype(BF16)


def dot3(left, right, dims):
    def one(a, b):
        return lax.dot_general(a, b, (dims, ((), ())), preferred_element_type=F32)

    return one(left[0], right[0]) + (one(left[0], right[1]) + one(left[1], right[0]))


def target_columns(points, routes, step, block, block_count, all_blocks):
    slots = points // BCOLS
    here = lax.axis_index("col") * block_count + block
    found = jnp.zeros_like(points)
    for slot in range(SLOTS):
        offset = lax.rem(routes[step, block, slot] - here + REACH + all_blocks, all_blocks) - REACH
        found = jnp.where(slots == slot, (block + offset) * BCOLS, found)
    return found + points % BCOLS


def spread_matrix(targets, weights, first_target, rows):
    row = lax.broadcasted_iota(jnp.int32, (rows, targets.shape[1]), 0) + first_target
    total = jnp.zeros(row.shape, F32)
    for point in range(POINTS):
        total += jnp.where(row == targets[point : point + 1], weights[point : point + 1], 0.0)
    return split(total)


def diffuse(inverse, fields):
    turned = split(inverse.T)
    return dot3(turned, split(jnp.concatenate(fields, axis=1)), ((1,), (0,)))


def pack(sums, variables, levels, tall, out):
    even = levels // 8 * 8
    rest = levels - even
    for number in range(variables * REACH):
        variable, block = divmod(number, REACH)
        cols = slice(block * BCOLS, (block + 1) * BCOLS)
        out[number * even : (number + 1) * even] = sums[variable * tall : variable * tall + even, cols]
        tail = variables * REACH * even + number * rest
        out[tail : tail + rest] = sums[variable * tall + even : variable * tall + levels, cols]


def add_packed(packed, variables, levels, where, first_variable, first_block):
    even = levels // 8 * 8
    rest = levels - even
    for number in range(variables * REACH):
        variable, block = divmod(number, REACH)
        cols = lanes(first_block + block, 1)
        tail = variables * REACH * even + number * rest
        at = first_variable + variable
        where[at, :even, cols] += packed[number * even : (number + 1) * even]
        where[at, even:, cols] += packed[tail : tail + rest]


def edge_kernel(step, chunk, all_blocks, has_halo, *refs):
    fields, inverses, routes, points, weights = refs[:5]
    halo = refs[5] if has_halo else None
    out, field, inverse, route, point, weight, tall, incoming, sems = refs[5 + has_halo :]
    variables, levels, _ = field.shape
    block_count = inverses.shape[1]
    _, first, first_target = z_side(block_count)
    copies = [
        pltpu.make_async_copy(routes, route, sems.at[0]),
        pltpu.make_async_copy(points.at[step, :, lanes(first, REACH)], point, sems.at[1]),
        pltpu.make_async_copy(weights.at[step, :, lanes(first, REACH)], weight, sems.at[2]),
        pltpu.make_async_copy(inverses.at[step, pl.ds(first, REACH)], inverse, sems.at[3]),
        pltpu.make_async_copy(
            fields.at[pl.ds(chunk * variables, variables), :, lanes(first, REACH)], field, sems.at[4]
        ),
    ]
    if has_halo:
        copies.append(pltpu.make_async_copy(halo, incoming, sems.at[5]))
    for copy in copies:
        copy.start()
    for copy in copies[:3]:
        copy.wait()
    targets = jnp.concatenate(
        [
            target_columns(
                point[:, j * BCOLS : (j + 1) * BCOLS], route, step, first + j, block_count, all_blocks
            )
            for j in range(REACH)
        ],
        axis=1,
    )
    matrix = spread_matrix(targets, weight[...], first_target * BCOLS, EDGE)
    for copy in copies[3:]:
        copy.wait()
    if has_halo:
        add_packed(incoming, variables, levels, field, 0, 0)
    tall[:, levels // 8 * 8 :, :] = jnp.zeros((variables, 8, EDGE), F32)
    for j in range(REACH):
        cols = slice(j * BCOLS, (j + 1) * BCOLS)
        diffused = diffuse(inverse[j], [field[v, :, cols] for v in range(variables)])
        for v in range(variables):
            tall[v, :levels, cols] = diffused[:, v * BCOLS : (v + 1) * BCOLS]
    high = tall.shape[1]
    sums = dot3(split(tall[...].reshape(variables * high, EDGE)), matrix, ((1,), (1,)))
    pack(sums, variables, levels, high, out)


def edge(step, chunk, all_blocks, fields, inverses, routes, points, weights, halo=None):
    variables = fields.shape[0] // CHUNKS
    levels = fields.shape[1]
    has_halo = halo is not None
    packed = jax.ShapeDtypeStruct((variables * REACH * levels, BCOLS), F32)
    operands = (fields, inverses, routes, points, weights) + ((halo,) if has_halo else ())
    return pl.pallas_call(
        functools.partial(edge_kernel, step, chunk, all_blocks, has_halo),
        out_shape=packed,
        in_specs=[ANY] * len(operands),
        out_specs=pl.BlockSpec(memory_space=pltpu.VMEM),
        scratch_shapes=[
            pltpu.VMEM((variables, levels, EDGE), F32),
            pltpu.VMEM((REACH, levels, levels), F32),
            pltpu.SMEM(routes.shape, jnp.int32),
            pltpu.VMEM((POINTS, EDGE), jnp.int32),
            pltpu.VMEM((POINTS, EDGE), F32),
            pltpu.VMEM((variables, padded(levels), EDGE), F32),
            pltpu.VMEM(packed.shape, F32),
            pltpu.SemaphoreType.DMA((6,)),
        ],
        compiler_params=pltpu.CompilerParams(vmem_limit_bytes=VMEM_LIMIT),
        cost_estimate=pl.CostEstimate(flops=400_000_000, bytes_accessed=2_000_000, transcendentals=0),
        name=f"edge_step{step}_chunk{chunk}",
    )(*operands)


def rest_kernel(step, all_blocks, has_halo, *refs):
    fields, inverses, routes, points, weights = refs[:5]
    count = (1 + CHUNKS) if has_halo else 0
    halos = refs[5 : 5 + count]
    refs = refs[5 + count :]
    own, core_out = refs[:2]
    mid = refs[2] if has_halo else None
    refs = refs[2 + has_halo :]
    field, inverse, route, point, weight, tall, core_in, z_in, sems = refs
    variables, levels, columns = field.shape
    block_count = inverses.shape[1]
    _, z_first, _ = z_side(block_count)
    _, core_first, core_target = core_side(block_count)
    copies = [
        pltpu.make_async_copy(routes, route, sems.at[0]),
        pltpu.make_async_copy(points.at[step], point, sems.at[1]),
        pltpu.make_async_copy(weights.at[step], weight, sems.at[2]),
        pltpu.make_async_copy(inverses.at[step], inverse, sems.at[3]),
        pltpu.make_async_copy(fields, field, sems.at[4]),
    ]
    if has_halo:
        copies.append(pltpu.make_async_copy(halos[0], core_in, sems.at[5]))
        for chunk in range(CHUNKS):
            copies.append(pltpu.make_async_copy(halos[1 + chunk], z_in.at[chunk], sems.at[6 + chunk]))
    for copy in copies:
        copy.start()
    for copy in copies[:3]:
        copy.wait()
    targets = jnp.concatenate(
        [
            target_columns(
                point[:, j * BCOLS : (j + 1) * BCOLS], route, step, j, block_count, all_blocks
            )
            for j in range(block_count)
        ],
        axis=1,
    )
    point[...] = targets
    inner = spread_matrix(targets, weight[...], 0, columns)
    side = lanes(core_first, REACH)
    outer = spread_matrix(point[:, side], weight[:, side], core_target * BCOLS, EDGE)
    for copy in copies[3:]:
        copy.wait()
    if has_halo:
        add_packed(core_in, variables, levels, field, 0, core_first)
        per = variables // CHUNKS
        for chunk in range(CHUNKS):
            add_packed(z_in.at[chunk], per, levels, field, chunk * per, z_first)
        mid_copy = pltpu.make_async_copy(field, mid, sems.at[8])
        mid_copy.start()
    tall[:, levels // 8 * 8 :, :] = jnp.zeros((variables, 8, columns), F32)
    for j in range(block_count):
        cols = slice(j * BCOLS, (j + 1) * BCOLS)
        diffused = diffuse(inverse[j], [field[v, :, cols] for v in range(variables)])
        for v in range(variables):
            tall[v, :levels, cols] = diffused[:, v * BCOLS : (v + 1) * BCOLS]
    high = tall.shape[1]
    edge_sums = dot3(split(tall[:, :, side].reshape(variables * high, EDGE)), outer, ((1,), (1,)))
    pack(edge_sums, variables, levels, high, core_out)
    sums = dot3(split(tall[...].reshape(variables * high, columns)), inner, ((1,), (1,)))
    for v in range(variables):
        own[v] = sums[v * high : v * high + levels]
    if has_halo:
        mid_copy.wait()


def rest(step, all_blocks, fields, inverses, routes, points, weights, halos=()):
    variables, levels, columns = fields.shape
    has_halo = bool(halos)
    whole = jax.ShapeDtypeStruct(fields.shape, F32)
    packed = jax.ShapeDtypeStruct((variables * REACH * levels, BCOLS), F32)
    part = jax.ShapeDtypeStruct((variables // CHUNKS * REACH * levels, BCOLS), F32)
    operands = (fields, inverses, routes, points, weights) + tuple(halos)
    vmem = pl.BlockSpec(memory_space=pltpu.VMEM)
    return pl.pallas_call(
        functools.partial(rest_kernel, step, all_blocks, has_halo),
        out_shape=(whole, packed) + ((whole,) if has_halo else ()),
        in_specs=[ANY] * len(operands),
        out_specs=(vmem, vmem) + ((ANY,) if has_halo else ()),
        scratch_shapes=[
            pltpu.VMEM(fields.shape, F32),
            pltpu.VMEM(inverses.shape[1:], F32),
            pltpu.SMEM(routes.shape, jnp.int32),
            pltpu.VMEM((POINTS, columns), jnp.int32),
            pltpu.VMEM((POINTS, columns), F32),
            pltpu.VMEM((variables, padded(levels), columns), F32),
            pltpu.VMEM(packed.shape, F32),
            pltpu.VMEM((CHUNKS,) + part.shape, F32),
            pltpu.SemaphoreType.DMA((9,)),
        ],
        compiler_params=pltpu.CompilerParams(vmem_limit_bytes=VMEM_LIMIT),
        cost_estimate=pl.CostEstimate(flops=2_000_000_000, bytes_accessed=5_000_000, transcendentals=0),
        name=f"rest_step{step}",
    )(*operands)


def total_kernel(count, own, core_in, *refs):
    z_in, (start, share) = refs[:CHUNKS], refs[CHUNKS:]
    variables, levels, columns = own.shape
    block_count = columns // BCOLS
    _, z_first, _ = z_side(block_count)
    _, core_first, _ = core_side(block_count)
    start[...] = own[...]
    add_packed(core_in, variables, levels, start, 0, core_first)
    per = variables // CHUNKS
    for chunk in range(CHUNKS):
        add_packed(z_in[chunk], per, levels, start, chunk * per, z_first)
    lane_sums = jnp.zeros((1, BCOLS), F32)
    for j in range(block_count):
        part = start[:, :, j * BCOLS : (j + 1) * BCOLS]
        lane_sums += jnp.sum(part * part, axis=(0, 1)).reshape(1, BCOLS)
    share[...] = jnp.broadcast_to(lane_sums, (count, BCOLS))


def total(count, own, core_in, z_in):
    vmem = pl.BlockSpec(memory_space=pltpu.VMEM)
    return pl.pallas_call(
        functools.partial(total_kernel, count),
        out_shape=(jax.ShapeDtypeStruct(own.shape, F32), jax.ShapeDtypeStruct((count, BCOLS), F32)),
        in_specs=[vmem] * (2 + CHUNKS),
        out_specs=(vmem, vmem),
        compiler_params=pltpu.CompilerParams(vmem_limit_bytes=VMEM_LIMIT),
        cost_estimate=pl.CostEstimate(flops=1_000_000, bytes_accessed=4_000_000, transcendentals=0),
        name="add_halos_and_square",
    )(own, core_in, *z_in)


def scale_kernel(cells, start, shares, out):
    energy = jnp.sum(shares[...]) / cells
    out[...] = start[...] / jnp.sqrt(jnp.full((1, 1, 1), energy + eps_energy, F32))


def scale(start, shares, cells):
    vmem = pl.BlockSpec(memory_space=pltpu.VMEM)
    return pl.pallas_call(
        functools.partial(scale_kernel, cells),
        out_shape=jax.ShapeDtypeStruct(start.shape, F32),
        in_specs=[vmem, vmem],
        out_specs=vmem,
        compiler_params=pltpu.CompilerParams(vmem_limit_bytes=VMEM_LIMIT),
        cost_estimate=pl.CostEstimate(flops=1_000_000, bytes_accessed=2_000_000, transcendentals=0),
        name="scale_start",
    )(start, shares)


def core_exchange(value):
    count = lax.axis_size("col")
    return lax.ppermute(value, "col", [(i, i ^ 1) for i in range(count)])


def z_exchange(value):
    count = lax.axis_size("col")
    pairs = [(i, (i + 1) % count if i % 2 else (i - 1) % count) for i in range(count)]
    return lax.ppermute(value, "col", pairs)


def shards(adj_final, inverses, dep_lists, dep_points, weights):
    count = lax.axis_size("col")
    all_blocks = count * inverses.shape[1]
    tables = (inverses, dep_lists, dep_points, weights)
    fields, halos, mid = adj_final, (), None
    for step in range(STEPS - 1, -1, -1):
        z_halos = []
        for chunk in range(CHUNKS):
            halo = halos[1 + chunk] if halos else None
            z_halos.append(z_exchange(edge(step, chunk, all_blocks, fields, *tables, halo=halo)))
        own, core_out, *written = rest(step, all_blocks, fields, *tables, halos=halos)
        if written:
            mid = written[0]
        fields, halos = own, (core_exchange(core_out), *z_halos)
    start, shares = total(count, fields, halos[0], halos[1:])
    shares = lax.all_to_all(shares, "col", 0, 0, tiled=True)
    return mid, scale(start, shares, adj_final.size * count)


def solution(mesh):
    in_specs = (
        P("mem", None, "col"),
        P("mem", "col", None, None),
        P("mem", "col", None),
        P("mem", None, "col"),
        P("mem", None, "col"),
    )
    out_specs = (P("mem", None, "col"), P("mem", None, "col"))
    return jax.shard_map(shards, mesh=mesh, in_specs=in_specs, out_specs=out_specs, check_vma=False)
```

time: 174 us -> 61.3 us (0.35)
  local copies, waits for them, and re-layouts: 58.9 us -> 5.72 us
  matrix products: 26.9 us -> 0 us
  loops' own time: 26.9 us -> 0 us
  other arithmetic: 16.6 us -> 0 us
  blocking collectives: 16.6 us -> 0 us
  Pallas kernels: 0 us -> 16.5 us
  waiting for transfers between devices: 17.5 us -> 25.6 us
  starting transfers between devices: 8.03 us -> 12.4 us
    dynamic_slice x56 -> x0, local copies, waits for them, and re-layouts: 36.4 us -> none  [the longest x40 24.3 us: one_slot(): position, inside = locate(route_row[slot_number])]
    another operation x10 -> x0, loops' own time: 26.9 us -> none  [the longest x8 26.4 us: add_block(): return lax.fori_loop(0, slot_limit, one_slot, accumulated)]
    dot_general x42 -> x0, matrix products: 26.9 us -> none  [the longest x40 24.1 us: one_slot(): jnp.dot(block_rows, matrix, precision=lax.Precision.HIGHEST, preferred_el...]
    psum x1 -> x0, blocking collectives: 16.6 us -> none  [shards(): energy = lax.psum(local_sum, 'col')]
    pallas_call x0 -> x8, Pallas kernels: none -> 16.5 us  [the longest x2 9.1 us: rest(): pl.pallas_call(functools.partial(rest_kernel, step, all_blocks, has_halo)...]
    reduce_sum x41 -> x0, other arithmetic: 9.18 us -> none  [the longest x40 8 us: slot_matrix(): return jnp.sum(one_hot * chosen[:, :, None], axis=0)]
    scatter-add x4 -> x0, other arithmetic: 6.34 us -> none  [the longest x2 4 us: spread(): owned = owned.at[:, :REACH].add(from_below)]
    slice x5 -> x0, local copies, waits for them, and re-layouts: 4.79 us -> none  [the longest x2 2.48 us: spread(): from_above = passed_along(extended[:, :REACH], 'col', -1)]
  transfers between devices with their start and end apart: 4 -> 7, of which waited for: 2 -> 5; matrix products, arithmetic and copies ran while one was open for 5% -> 3% of each run, Pallas kernels for 0% -> 10%
where the time goes in v1:
time: 61.3 us; the launch traced here: 61 us
  waiting for transfers between devices  25.6 us (42%)
  Pallas kernels  16.5 us (27%)
  starting transfers between devices  12.4 us (20%)
  local copies, waits for them, and re-layouts  5.72 us (9%)
  between operations  0.75 us (1%)
    ppermute x4, waiting for transfers between devices, z_exchange(): return lax.ppermute(value, 'col', pairs)  21.9 us
    pallas_call x2, Pallas kernels, rest(): pl.pallas_call(functools.partial(rest_kernel, step, all_blocks, has_halo)...  9.1 us
    ppermute x4, starting transfers between devices, z_exchange(): return lax.ppermute(value, 'col', pairs)  8.54 us
    pallas_call x4, Pallas kernels, edge(): pl.pallas_call(functools.partial(edge_kernel, step, chunk, all_blocks, ha...  6.08 us
    unnamed x12, local copies, waits for them, and re-layouts  5.72 us
    all_to_all x1, waiting for transfers between devices, shards(): shares = lax.all_to_all(shares, 'col', 0, 0, tiled=True)  3.7 us
    all_to_all x1, starting transfers between devices, shards(): shares = lax.all_to_all(shares, 'col', 0, 0, tiled=True)  3.31 us
  transfers between devices with their start and end apart: 7, of which 5 were waited for; matrix products, arithmetic and copies ran while one was open for 3% of the time, Pallas kernels for 10%

profile of v1, /device:TPU:0, one launch (start us, length us, event | category | flops | bytes accessed | tf_op | source)
XLA Modules:
  0.0 61.0 jit_solution(11489335373046624315)
XLA Ops:
  0.6 1.6 %copy.19.refs_1_ = f32[2,4,137,137]{3,2,1,0:T(8,128)S(1)} copy(f32[2,4,137,137]{3,1,2,0:T(4,128)} %param.6) | data formatting | bytes 1201216 | tf_op args[1]
  2.2 0.0 copy-done.3
  2.2 0.0 copy-start
  2.2 0.0 copy-start.1
  2.2 0.0 copy-start.2
  2.3 0.4 copy.18.refs_0_
  2.6 0.3 copy-done
  2.9 0.0 copy-done.1
  3.0 4.3 %rest_step1.1 = (f32[4,137,512]{2,1,0:T(8,128)S(1)}, f32[1096,128]{1,0:T(8,128)S(1)}) custom-call(f32[4,137,512]{2,1,0:T(8,128)S(1)} %copy.18.refs_0_, f32[2,4,137,137]{3,2,1,0:T(8,128)S(1)} %copy.19.refs_1_, s32[2,4,5]{2,1,0:T(4,128)S(1)} %copy-done.2, s32[2,4,512]{2,1,0:T(4,128)S(1)} %copy-done, f32[2,4,512]{2,1,0:T(4,128)S(1)} %copy-done.1), custom_call_target="tpu_custom_call" | custom-call | flops 2000000000 | bytes 5000000 | tf_op jit(solution)/shard_map/rest_step1/pallas_call | solution.py:252
  7.2 0.5 collective-permute-start
  7.7 1.5 %edge_step1_chunk0.1 = f32[548,128]{1,0:T(8,128)S(1)} custom-call(f32[4,137,512]{2,1,0:T(8,128)S(1)} %copy.18.refs_0_, f32[2,4,137,137]{3,2,1,0:T(8,128)S(1)} %copy.19.refs_1_, s32[2,4,5]{2,1,0:T(4,128)S(1)} %copy-done.2, s32[2,4,512]{2,1,0:T(4,128)S(1)} %copy-done, f32[2,4,512]{2,1,0:T(4,128)S(1)} %copy-done.1), custom_call_target="tpu_custom_call" | custom-call | flops 400000000 | bytes 2000000 | tf_op jit(solution)/shard_map/edge_step1_chunk0/pallas_call | solution.py:157
  9.3 4.8 %collective-permute-start.1 = (f32[548,128]{1,0:T(8,128)S(1)}, f32[548,128]{1,0:T(8,128)S(1)}, u32[]{:S(2)}, u32[]{:S(2)}) collective-permute-start(f32[548,128]{1,0:T(8,128)S(1)} %edge_step1_chunk0.1), channel_id=1, source_target_pairs={{0,7},{1,2},{2,1},{3,4},{4,3},{5,6},{6,5},{7,0},{8,15},{9,10},{10,... | collective-permute-start | bytes 841736 | tf_op jit(solution)/shard_map/ppermute | solution.py:331
  14.1 1.5 %edge_step1_chunk1.1 = f32[548,128]{1,0:T(8,128)S(1)} custom-call(f32[4,137,512]{2,1,0:T(8,128)S(1)} %copy.18.refs_0_, f32[2,4,137,137]{3,2,1,0:T(8,128)S(1)} %copy.19.refs_1_, s32[2,4,5]{2,1,0:T(4,128)S(1)} %copy-done.2, s32[2,4,512]{2,1,0:T(4,128)S(1)} %copy-done, f32[2,4,512]{2,1,0:T(4,128)S(1)} %copy-done.1), custom_call_target="tpu_custom_call" | custom-call | flops 400000000 | bytes 2000000 | tf_op jit(solution)/shard_map/edge_step1_chunk1/pallas_call | solution.py:157
  15.6 0.1 collective-permute-start.2
  15.7 5.6 %collective-permute-done.1.refs_6_.refs_5_ = f32[548,128]{1,0:T(8,128)S(1)} collective-permute-done((f32[548,128]{1,0:T(8,128)S(1)}, f32[548,128]{1,0:T(8,128)S(1)}, u32[]{:S(2)}, u32[]{:S(2)}) %collective-permute-start.1) | collective-permute-done | bytes 280608 | tf_op jit(solution)/shard_map/ppermute | solution.py:331
  21.3 5.5 %collective-permute-done.2.refs_7_.refs_5_ = f32[548,128]{1,0:T(8,128)S(1)} collective-permute-done((f32[548,128]{1,0:T(8,128)S(1)}, f32[548,128]{1,0:T(8,128)S(1)}, u32[]{:S(2)}, u32[]{:S(2)}) %collective-permute-start.2) | collective-permute-done | bytes 280608 | tf_op jit(solution)/shard_map/ppermute | solution.py:331
  26.7 0.0 collective-permute-done.refs_5_
  26.7 4.8 %rest_step0.1 = (f32[4,137,512]{2,1,0:T(8,128)S(1)}, f32[1096,128]{1,0:T(8,128)S(1)}, f32[4,137,512]{2,1,0:T(8,128)S(1)}) custom-call(f32[4,137,512]{2,1,0:T(8,128)S(1)} %get-tuple-element.9.refs_0_, f32[2,4,137,137]{3,2,1,0:T(8,128)S(1)} %copy.19.refs_1_, s32[2,4,5]{2,1,0:T(4,128)S(1)} %copy-done.2, s32[2,4,512]{2,1,0:T(4,128)S(1)} %copy-done, ...), custom_call_target="tpu_custom_call" | custom-call | flops 2000000000 | bytes 5000000 | tf_op jit(solution)/shard_map/rest_step0/pallas_call | solution.py:252
  31.6 0.1 collective-permute-start.3
  31.6 1.5 %edge_step0_chunk0.1 = f32[548,128]{1,0:T(8,128)S(1)} custom-call(f32[4,137,512]{2,1,0:T(8,128)S(1)} %get-tuple-element.9.refs_0_, f32[2,4,137,137]{3,2,1,0:T(8,128)S(1)} %copy.19.refs_1_, s32[2,4,5]{2,1,0:T(4,128)S(1)} %copy-done.2, s32[2,4,512]{2,1,0:T(4,128)S(1)} %copy-done, f32[2,4,512]{2,1,0:T(4,128)S(1)} %copy-done.1, ...), custom_call_target="tpu_custom_call" | custom-call | flops 400000000 | bytes 2000000 | tf_op jit(solution)/shard_map/edge_step0_chunk0/pallas_call | solution.py:157
  33.2 2.5 %collective-permute-start.4 = (f32[548,128]{1,0:T(8,128)S(1)}, f32[548,128]{1,0:T(8,128)S(1)}, u32[]{:S(2)}, u32[]{:S(2)}) collective-permute-start(f32[548,128]{1,0:T(8,128)S(1)} %edge_step0_chunk0.1), channel_id=1, source_target_pairs={{0,7},{1,2},{2,1},{3,4},{4,3},{5,6},{6,5},{7,0},{8,15},{9,10},{10,... | collective-permute-start | bytes 841736 | tf_op jit(solution)/shard_map/ppermute | solution.py:331
  35.7 1.5 %edge_step0_chunk1.1 = f32[548,128]{1,0:T(8,128)S(1)} custom-call(f32[4,137,512]{2,1,0:T(8,128)S(1)} %get-tuple-element.9.refs_0_, f32[2,4,137,137]{3,2,1,0:T(8,128)S(1)} %copy.19.refs_1_, s32[2,4,5]{2,1,0:T(4,128)S(1)} %copy-done.2, s32[2,4,512]{2,1,0:T(4,128)S(1)} %copy-done, f32[2,4,512]{2,1,0:T(4,128)S(1)} %copy-done.1, ...), custom_call_target="tpu_custom_call" | custom-call | flops 400000000 | bytes 2000000 | tf_op jit(solution)/shard_map/edge_step0_chunk1/pallas_call | solution.py:157
  37.2 1.2 %collective-permute-start.5 = (f32[548,128]{1,0:T(8,128)S(1)}, f32[548,128]{1,0:T(8,128)S(1)}, u32[]{:S(2)}, u32[]{:S(2)}) collective-permute-start(f32[548,128]{1,0:T(8,128)S(1)} %edge_step0_chunk1.1), channel_id=1, source_target_pairs={{0,7},{1,2},{2,1},{3,4},{4,3},{5,6},{6,5},{7,0},{8,15},{9,10},{10,... | collective-permute-start | bytes 841736 | tf_op jit(solution)/shard_map/ppermute | solution.py:331
  38.4 5.7 %collective-permute-done.4.refs_0_ = f32[548,128]{1,0:T(8,128)S(1)} collective-permute-done((f32[548,128]{1,0:T(8,128)S(1)}, f32[548,128]{1,0:T(8,128)S(1)}, u32[]{:S(2)}, u32[]{:S(2)}) %collective-permute-start.4) | collective-permute-done | bytes 280608 | tf_op jit(solution)/shard_map/ppermute | solution.py:331
  44.1 5.2 %collective-permute-done.5.refs_1_ = f32[548,128]{1,0:T(8,128)S(1)} collective-permute-done((f32[548,128]{1,0:T(8,128)S(1)}, f32[548,128]{1,0:T(8,128)S(1)}, u32[]{:S(2)}, u32[]{:S(2)}) %collective-permute-start.5) | collective-permute-done | bytes 280608 | tf_op jit(solution)/shard_map/ppermute | solution.py:331
  49.2 0.0 collective-permute-done.3.core_in
  49.2 1.1 %add_halos_and_square.1 = (f32[4,137,512]{2,1,0:T(8,128)S(1)}, f32[8,128]{1,0:T(8,128)}) custom-call(f32[4,137,512]{2,1,0:T(8,128)S(1)} %get-tuple-element.12.own, f32[1096,128]{1,0:T(8,128)S(1)} %collective-permute-done.3.core_in, f32[548,128]{1,0:T(8,128)S(1)} %collective-permute-done.4.refs_0_, f32[548,128]{1,0:T(8,128)S(1)} %collective-permute-done.5.refs_1_), custom_call_target="tpu_custom_call" | custom-call | flops 1000000 | bytes 4000000 | tf_op jit(solution)/shard_map/add_halos_and_square/pallas_call | solution.py:294
  50.4 3.3 %all-to-all-start = ((f32[8,1,128]{2,1,0:T(1,128)}), f32[8,1,128]{2,1,0:T(1,128)S(1)}, u32[]{:S(2)}, u32[]{:S(2)}) async-start(f32[8,1,128]{2,1,0:T(1,128)} %bitcast.1), calls=%async_computation | async-start | bytes 8192 | tf_op jit(solution)/shard_map/all_to_all | solution.py:349
  53.7 1.7 %copy.28 = f32[4,137,512]{2,0,1:T(4,128)} copy(f32[4,137,512]{2,1,0:T(8,128)S(1)} %get-tuple-element.18) | data formatting | bytes 2244608
  55.4 3.7 %all-to-all-done = f32[8,1,128]{2,1,0:T(1,128)S(1)} async-done(((f32[8,1,128]{2,1,0:T(1,128)}), f32[8,1,128]{2,1,0:T(1,128)S(1)}, u32[]{:S(2)}, u32[]{:S(2)}) %all-to-all-start) | async-done | bytes 4128 | tf_op jit(solution)/shard_map/all_to_all | solution.py:349
  59.1 0.2 scale_start.1
  59.3 1.7 %copy.29 = f32[4,137,512]{2,0,1:T(4,128)} copy(f32[4,137,512]{2,1,0:T(8,128)S(1)} %scale_start.1) | data formatting | bytes 2244608
  (2 shorter events, 0.0 us)
Async XLA Ops:
  0.6 1.6 %copy-start.3 = (f32[4,137,512]{2,0,1:T(4,128)S(1)}, f32[4,137,512]{2,0,1:T(4,128)}, u32[]{:S(2)}) copy-start(f32[4,137,512]{2,0,1:T(4,128)} %param.5) | copy-start | bytes 3366916
  2.2 0.7 %copy-start = (s32[2,4,512]{2,1,0:T(4,128)S(1)}, s32[2,4,512]{2,1,0:T(4,128)}, u32[]{:S(2)}) copy-start(s32[2,4,512]{2,1,0:T(4,128)} %refs_3_.11) | copy-start | bytes 49156
  2.2 0.7 %copy-start.1 = (f32[2,4,512]{2,1,0:T(4,128)S(1)}, f32[2,4,512]{2,1,0:T(4,128)}, u32[]{:S(2)}) copy-start(f32[2,4,512]{2,1,0:T(4,128)} %refs_4_.11) | copy-start | bytes 49156
  2.2 0.7 %copy-start.2 = (s32[2,4,5]{2,1,0:T(4,128)S(1)}, s32[2,4,5]{2,1,0:T(4,128)}, u32[]{:S(2)}) copy-start(s32[2,4,5]{2,1,0:T(4,128)} %refs_2_.11) | copy-start | bytes 484
  7.2 19.5 %collective-permute-start = (f32[1096,128]{1,0:T(8,128)S(1)}, f32[1096,128]{1,0:T(8,128)S(1)}, u32[]{:S(2)}, u32[]{:S(2)}) collective-permute-start(f32[1096,128]{1,0:T(8,128)S(1)} %get-tuple-element.10), channel_id=1, source_target_pairs={{0,1},{1,0},{2,3},{3,2},{4,5},{5,4},{6,7},{7,6},{8,9},{9,8},{10,11... | collective-permute-start | bytes 1683464 | tf_op jit(solution)/shard_map/ppermute | solution.py:325
  9.3 12.0 %collective-permute-start.1 = (f32[548,128]{1,0:T(8,128)S(1)}, f32[548,128]{1,0:T(8,128)S(1)}, u32[]{:S(2)}, u32[]{:S(2)}) collective-permute-start(f32[548,128]{1,0:T(8,128)S(1)} %edge_step1_chunk0.1), channel_id=1, source_target_pairs={{0,7},{1,2},{2,1},{3,4},{4,3},{5,6},{6,5},{7,0},{8,15},{9,10},{10,... | collective-permute-start | bytes 841736 | tf_op jit(solution)/shard_map/ppermute | solution.py:331
  15.6 11.1 %collective-permute-start.2 = (f32[548,128]{1,0:T(8,128)S(1)}, f32[548,128]{1,0:T(8,128)S(1)}, u32[]{:S(2)}, u32[]{:S(2)}) collective-permute-start(f32[548,128]{1,0:T(8,128)S(1)} %edge_step1_chunk1.1), channel_id=1, source_target_pairs={{0,7},{1,2},{2,1},{3,4},{4,3},{5,6},{6,5},{7,0},{8,15},{9,10},{10,... | collective-permute-start | bytes 841736 | tf_op jit(solution)/shard_map/ppermute | solution.py:331
  31.6 17.7 %collective-permute-start.3 = (f32[1096,128]{1,0:T(8,128)S(1)}, f32[1096,128]{1,0:T(8,128)S(1)}, u32[]{:S(2)}, u32[]{:S(2)}) collective-permute-start(f32[1096,128]{1,0:T(8,128)S(1)} %get-tuple-element.13), channel_id=1, source_target_pairs={{0,1},{1,0},{2,3},{3,2},{4,5},{5,4},{6,7},{7,6},{8,9},{9,8},{10,11... | collective-permute-start | bytes 1683464 | tf_op jit(solution)/shard_map/ppermute | solution.py:325
  33.2 10.9 %collective-permute-start.4 = (f32[548,128]{1,0:T(8,128)S(1)}, f32[548,128]{1,0:T(8,128)S(1)}, u32[]{:S(2)}, u32[]{:S(2)}) collective-permute-start(f32[548,128]{1,0:T(8,128)S(1)} %edge_step0_chunk0.1), channel_id=1, source_target_pairs={{0,7},{1,2},{2,1},{3,4},{4,3},{5,6},{6,5},{7,0},{8,15},{9,10},{10,... | collective-permute-start | bytes 841736 | tf_op jit(solution)/shard_map/ppermute | solution.py:331
  37.2 12.0 %collective-permute-start.5 = (f32[548,128]{1,0:T(8,128)S(1)}, f32[548,128]{1,0:T(8,128)S(1)}, u32[]{:S(2)}, u32[]{:S(2)}) collective-permute-start(f32[548,128]{1,0:T(8,128)S(1)} %edge_step0_chunk1.1), channel_id=1, source_target_pairs={{0,7},{1,2},{2,1},{3,4},{4,3},{5,6},{6,5},{7,0},{8,15},{9,10},{10,... | collective-permute-start | bytes 841736 | tf_op jit(solution)/shard_map/ppermute | solution.py:331
  50.4 8.7 %all-to-all-start = ((f32[8,1,128]{2,1,0:T(1,128)}), f32[8,1,128]{2,1,0:T(1,128)S(1)}, u32[]{:S(2)}, u32[]{:S(2)}) async-start(f32[8,1,128]{2,1,0:T(1,128)} %bitcast.1), calls=%async_computation | async-start | bytes 8192 | tf_op jit(solution)/shard_map/all_to_all | solution.py:349

commit v2 on v0

v2 whole, which is shorter than its diff:
```python
import functools

import jax
import jax.numpy as jnp
from jax import lax
from jax.experimental import pallas as pl
from jax.experimental.pallas import tpu as pltpu
from jax.sharding import PartitionSpec as P

BCOLS = 128
REACH = 2
SLOTS = 5
POINTS = 4
STEPS = 2
VMEM_LIMIT = 32 * 1024 * 1024

eps_energy = 1e-06

F32 = jnp.float32
BF16 = jnp.bfloat16
ANY = pl.BlockSpec(memory_space=pl.ANY)
HBM = pl.BlockSpec(memory_space=pltpu.HBM)
VMEM = pl.BlockSpec(memory_space=pltpu.VMEM)


def z_blocks(block_count):
    follows = lax.rem(lax.axis_index("col"), 2)
    near = follows * (block_count - 1)
    away = 2 * follows - 1
    return near, near - away, near + away, near + 2 * away


def core_side(block_count):
    follows = 1 - lax.rem(lax.axis_index("col"), 2)
    return follows * (block_count - REACH), follows * (block_count + REACH) - REACH


def lanes(block, count=1):
    return pl.ds(pl.multiple_of(block * BCOLS, BCOLS), count * BCOLS)


def split(value):
    high = value.astype(BF16)
    return high, (value - high.astype(F32)).astype(BF16)


def dot3(left, right, dims):
    def one(a, b):
        return lax.dot_general(a, b, (dims, ((), ())), preferred_element_type=F32)

    return one(left[0], right[0]) + (one(left[0], right[1]) + one(left[1], right[0]))


def target_columns(points, routes, step, block, block_count, all_blocks):
    slots = points // BCOLS
    here = lax.axis_index("col") * block_count + block
    found = jnp.zeros_like(points)
    for slot in range(SLOTS):
        offset = lax.rem(routes[step, block, slot] - here + REACH + all_blocks, all_blocks) - REACH
        found = jnp.where(slots == slot, (block + offset) * BCOLS, found)
    return found + points % BCOLS


def spread_matrix(targets, weights, first_column, rows=BCOLS):
    row = lax.broadcasted_iota(jnp.int32, (rows, targets.shape[1]), 0) + first_column
    total = jnp.zeros(row.shape, F32)
    for point in range(POINTS):
        total += jnp.where(row == targets[point : point + 1], weights[point : point + 1], 0.0)
    return split(total)


def diffuse(inverse, field, out, cols):
    variables = field.shape[1]
    wide = jnp.concatenate([field[:, v, :] for v in range(variables)], axis=1)
    result = dot3(split(inverse.T), split(wide), ((1,), (0,)))
    for v in range(variables):
        out[:, v, cols] = result[:, v * BCOLS : (v + 1) * BCOLS]


def rows_of(value):
    return value.reshape(value.shape[0] * value.shape[1], value.shape[2])


def spread(diffused, matrix):
    levels, variables, _ = diffused.shape
    sums = dot3(split(rows_of(diffused)), matrix, ((1,), (1,)))
    return sums.reshape(levels, variables, sums.shape[1])


def fetch(sems, pairs):
    copies = [pltpu.make_async_copy(source, target, sems.at[i]) for i, (source, target) in enumerate(pairs)]
    for copy in copies:
        copy.start()
    return copies


def call(kernel, operands, in_specs, outs, out_specs, scratch, flops, name):
    return pl.pallas_call(
        kernel,
        out_shape=outs,
        in_specs=in_specs,
        out_specs=out_specs,
        scratch_shapes=scratch,
        compiler_params=pltpu.CompilerParams(vmem_limit_bytes=VMEM_LIMIT),
        cost_estimate=pl.CostEstimate(flops=flops, bytes_accessed=1_000_000, transcendentals=0),
        name=name,
    )(*operands)


def first_edge_kernel(step, all_blocks, *refs):
    fields, inverses, routes, points, weights, to_near, to_far = refs[:7]
    field, inverse, route, point, weight, tall, sems = refs[7:]
    block_count = inverses.shape[2]
    near, far, target_near, target_far = z_blocks(block_count)
    copies = fetch(
        sems,
        [
            (routes, route),
            (points.at[step], point),
            (weights.at[step], weight),
            (inverses.at[step], inverse),
            (fields.at[:, :, lanes(near)], field.at[0]),
            (fields.at[:, :, lanes(far)], field.at[1]),
        ],
    )
    for copy in copies[:3]:
        copy.wait()
    matrices = []
    for block in (near, far):
        targets = target_columns(point[:, lanes(block)], route, step, block, block_count, all_blocks)
        halves = [
            spread_matrix(targets, weight[:, lanes(block)], target * BCOLS) for target in (target_near, target_far)
        ]
        matrices.append([jnp.concatenate(parts, axis=0) for parts in zip(*halves)])
    matrix = [jnp.concatenate(parts, axis=1) for parts in zip(*matrices)]
    for copy in copies[3:]:
        copy.wait()
    for j, block in enumerate((near, far)):
        diffuse(inverse[:, block, :], field.at[j], tall, slice(j * BCOLS, (j + 1) * BCOLS))
    sums = spread(tall[...], matrix)
    to_near[...] = sums[:, :, :BCOLS]
    to_far[...] = sums[:, :, BCOLS:]


def tables_scratch(inverses, routes):
    levels, block_count = inverses.shape[1:3]
    return [
        pltpu.VMEM((levels, block_count, levels), F32),
        pltpu.SMEM(routes.shape, jnp.int32),
        pltpu.VMEM((POINTS, block_count * BCOLS), jnp.int32),
        pltpu.VMEM((POINTS, block_count * BCOLS), F32),
    ]


def first_edge(step, all_blocks, fields, tables):
    levels, variables, _ = fields.shape
    one = jax.ShapeDtypeStruct((levels, variables, BCOLS), F32)
    return call(
        functools.partial(first_edge_kernel, step, all_blocks),
        (fields, *tables),
        [HBM] * 5,
        (one, one),
        (VMEM, VMEM),
        [
            pltpu.VMEM((2, levels, variables, BCOLS), F32),
            *tables_scratch(*tables[:2]),
            pltpu.VMEM((levels, variables, 2 * BCOLS), F32),
            pltpu.SemaphoreType.DMA((6,)),
        ],
        400_000_000,
        f"first_edge_step{step}",
    )


def near_edge_kernel(step, all_blocks, *refs):
    own, halo, inverses, routes, points, weights, to_far, to_near = refs[:8]
    inverse, route, point, weight, field, tall, sems = refs[8:]
    block_count = inverses.shape[2]
    near, _, target_near, target_far = z_blocks(block_count)
    copies = fetch(
        sems, [(routes, route), (points.at[step], point), (weights.at[step], weight), (inverses.at[step], inverse)]
    )
    field[...] = own[:, :, lanes(near)] + halo[...]
    for copy in copies:
        copy.wait()
    targets = target_columns(point[:, lanes(near)], route, step, near, block_count, all_blocks)
    halves = [spread_matrix(targets, weight[:, lanes(near)], target * BCOLS) for target in (target_far, target_near)]
    matrix = [jnp.concatenate(parts, axis=0) for parts in zip(*halves)]
    diffuse(inverse[:, near, :], field, tall, slice(0, BCOLS))
    sums = spread(tall[...], matrix)
    to_far[...] = sums[:, :, :BCOLS]
    to_near[...] = sums[:, :, BCOLS:]


def near_edge(step, all_blocks, own, halo, tables):
    one = jax.ShapeDtypeStruct(halo.shape, F32)
    return call(
        functools.partial(near_edge_kernel, step, all_blocks),
        (own, halo, *tables),
        [VMEM, VMEM] + [HBM] * 4,
        (one, one),
        (VMEM, VMEM),
        [
            *tables_scratch(*tables[:2]),
            pltpu.VMEM(halo.shape, F32),
            pltpu.VMEM(halo.shape, F32),
            pltpu.SemaphoreType.DMA((4,)),
        ],
        300_000_000,
        f"near_edge_step{step}",
    )


def far_edge_kernel(step, all_blocks, *refs):
    own, halo, partial, inverses, routes, points, weights, to_near = refs[:8]
    inverse, route, point, weight, field, tall, sems = refs[8:]
    block_count = inverses.shape[2]
    _, far, target_near, _ = z_blocks(block_count)
    copies = fetch(
        sems, [(routes, route), (points.at[step], point), (weights.at[step], weight), (inverses.at[step], inverse)]
    )
    field[...] = own[:, :, lanes(far)] + halo[...]
    for copy in copies:
        copy.wait()
    targets = target_columns(point[:, lanes(far)], route, step, far, block_count, all_blocks)
    matrix = spread_matrix(targets, weight[:, lanes(far)], target_near * BCOLS)
    diffuse(inverse[:, far, :], field, tall, slice(0, BCOLS))
    to_near[...] = partial[...] + spread(tall[...], matrix)


def far_edge(step, all_blocks, own, halo, partial, tables):
    return call(
        functools.partial(far_edge_kernel, step, all_blocks),
        (own, halo, partial, *tables),
        [VMEM] * 3 + [HBM] * 4,
        jax.ShapeDtypeStruct(halo.shape, F32),
        VMEM,
        [
            *tables_scratch(*tables[:2]),
            pltpu.VMEM(halo.shape, F32),
            pltpu.VMEM(halo.shape, F32),
            pltpu.SemaphoreType.DMA((4,)),
        ],
        300_000_000,
        f"far_edge_step{step}",
    )


def rest_kernel(step, all_blocks, has_halo, *refs):
    fields, inverses, routes, points, weights, _ = refs[:6]
    halos = refs[6 : 6 + 3 * has_halo]
    refs = refs[6 + 3 * has_halo :]
    own, core_out = refs[:2]
    mid = refs[2] if has_halo else None
    inverse, route, point, weight, field, tall, sems = refs[2 + has_halo :]
    block_count = inverses.shape[2]
    near, far, _, _ = z_blocks(block_count)
    core_first, core_target = core_side(block_count)
    pairs = [(routes, route), (points.at[step], point), (weights.at[step], weight), (inverses.at[step], inverse)]
    if not has_halo:
        pairs.append((fields, field))
    copies = fetch(sems, pairs)
    if has_halo:
        core_in, near_in, far_in = halos
        field[:, :, lanes(core_first, REACH)] = fields[:, :, lanes(core_first, REACH)] + core_in[...]
        field[:, :, lanes(near)] = fields[:, :, lanes(near)] + near_in[...]
        field[:, :, lanes(far)] = fields[:, :, lanes(far)] + far_in[...]
        mid_copy = pltpu.make_async_copy(field, mid, sems.at[5])
        mid_copy.start()
    for copy in copies[:3]:
        copy.wait()
    for j in range(block_count):
        cols = slice(j * BCOLS, (j + 1) * BCOLS)
        point[:, cols] = target_columns(point[:, cols], route, step, j, block_count, all_blocks)
    side = lanes(core_first, REACH)
    outer = spread_matrix(point[:, side], weight[:, side], core_target * BCOLS, REACH * BCOLS)
    inner = spread_matrix(point[...], weight[...], 0, block_count * BCOLS)
    for copy in copies[3:]:
        copy.wait()
    for j in range(block_count):
        cols = slice(j * BCOLS, (j + 1) * BCOLS)
        diffuse(inverse[:, j, :], field.at[:, :, cols], tall, cols)
    core_out[...] = spread(tall[:, :, side], outer)
    own[...] = spread(tall[...], inner)
    if has_halo:
        mid_copy.wait()


def rest(step, all_blocks, fields, tables, behind, halos=()):
    levels, variables, _ = fields.shape
    has_halo = bool(halos)
    whole = jax.ShapeDtypeStruct(fields.shape, F32)
    side = jax.ShapeDtypeStruct((levels, variables, REACH * BCOLS), F32)
    return call(
        functools.partial(rest_kernel, step, all_blocks, has_halo),
        (fields, *tables, behind, *halos),
        [VMEM if has_halo else HBM] + [HBM] * 4 + [ANY] + [VMEM] * len(halos),
        (whole, side) + ((whole,) if has_halo else ()),
        (VMEM, VMEM) + ((HBM,) if has_halo else ()),
        [
            *tables_scratch(*tables[:2]),
            pltpu.VMEM(fields.shape, F32),
            pltpu.VMEM(fields.shape, F32),
            pltpu.SemaphoreType.DMA((6,)),
        ],
        2_000_000_000,
        f"rest_step{step}",
    )


def squares(value):
    return jnp.sum(rows_of(value * value), axis=0, keepdims=True)


def most_kernel(own, core_in, far_in, start, lane_sums):
    block_count = own.shape[2] // BCOLS
    near, far, _, _ = z_blocks(block_count)
    side = lanes(core_side(block_count)[0], REACH)
    core = own[:, :, side] + core_in[...]
    behind = own[:, :, lanes(far)] + far_in[...]
    start[:, :, side] = core
    start[:, :, lanes(far)] = behind
    start[:, :, lanes(near)] = own[:, :, lanes(near)]
    core = squares(core)
    lane_sums[...] = core[:, :BCOLS] + core[:, BCOLS:] + squares(behind)


def most(own, core_in, far_in):
    return call(
        most_kernel,
        (own, core_in, far_in),
        [VMEM] * 3,
        (jax.ShapeDtypeStruct(own.shape, F32), jax.ShapeDtypeStruct((1, BCOLS), F32)),
        (VMEM, VMEM),
        [],
        1_000_000,
        "squares_of_most_blocks",
    )


def last_kernel(start, near_in, lane_sums, shares):
    near = z_blocks(start.shape[2] // BCOLS)[0]
    sums = lane_sums[...] + squares(start[:, :, lanes(near)] + near_in[...])
    shares[...] = jnp.broadcast_to(sums, shares.shape)


def last(count, start, near_in, lane_sums):
    return call(
        last_kernel,
        (start, near_in, lane_sums),
        [VMEM] * 3,
        jax.ShapeDtypeStruct((count, BCOLS), F32),
        VMEM,
        [],
        1_000_000,
        "squares_of_last_block",
    )


def scale_kernel(cells, start, near_in, shares, out, held, sems):
    block_count = start.shape[2] // BCOLS
    near = z_blocks(block_count)[0]
    energy = jnp.sum(shares[...]) / cells
    root = jnp.sqrt(jnp.full((1, 1, 1), energy + eps_energy, F32))
    copies = []
    for j in range(block_count):
        cols = slice(j * BCOLS, (j + 1) * BCOLS)
        held[:, :, cols] = (start[:, :, cols] + jnp.where(near == j, near_in[...], 0.0)) / root
        copies.append(pltpu.make_async_copy(held.at[:, :, cols], out.at[:, :, cols], sems.at[j]))
        copies[-1].start()
    for copy in copies:
        copy.wait()


def scale(start, near_in, shares, cells):
    return call(
        functools.partial(scale_kernel, cells),
        (start, near_in, shares),
        [VMEM] * 3,
        jax.ShapeDtypeStruct(start.shape, F32),
        HBM,
        [pltpu.VMEM(start.shape, F32), pltpu.SemaphoreType.DMA((start.shape[2] // BCOLS,))],
        1_000_000,
        "scale_start",
    )


def core_exchange(value):
    count = lax.axis_size("col")
    return lax.ppermute(value, "col", [(i, i ^ 1) for i in range(count)])


def z_exchange(value):
    count = lax.axis_size("col")
    pairs = [(i, (i + 1) % count if i % 2 else (i - 1) % count) for i in range(count)]
    return lax.ppermute(value, "col", pairs)


def shards(adj_final, inverses, dep_lists, dep_points, weights):
    count = lax.axis_size("col")
    all_blocks = count * inverses.shape[1]
    fields = jnp.transpose(adj_final, (1, 0, 2))
    tables = (jnp.transpose(inverses, (0, 2, 1, 3)), dep_lists, dep_points, weights)

    to_near, to_far = first_edge(1, all_blocks, fields, tables)
    near_in = z_exchange(to_near)
    far_in = z_exchange(to_far)
    own, core_out = rest(1, all_blocks, fields, tables, to_near)
    core_in = core_exchange(core_out)

    to_far, partial = near_edge(0, all_blocks, own, near_in, tables)
    next_far_in = z_exchange(to_far)
    to_near = far_edge(0, all_blocks, own, far_in, partial, tables)
    next_near_in = z_exchange(to_near)
    own, core_out, mid = rest(0, all_blocks, own, tables, to_near, (core_in, near_in, far_in))
    core_in = core_exchange(core_out)

    start, lane_sums = most(own, core_in, next_far_in)
    shares = last(count, start, next_near_in, lane_sums)
    shares = lax.all_to_all(shares, "col", 0, 0, tiled=True)
    lanczos = scale(start, next_near_in, shares, adj_final.size * count)
    return jnp.transpose(mid, (1, 0, 2)), jnp.transpose(lanczos, (1, 0, 2))


def solution(mesh):
    in_specs = (
        P("mem", None, "col"),
        P("mem", "col", None, None),
        P("mem", "col", None),
        P("mem", None, "col"),
        P("mem", None, "col"),
    )
    out_specs = (P("mem", None, "col"), P("mem", None, "col"))
    return jax.shard_map(shards, mesh=mesh, in_specs=in_specs, out_specs=out_specs, check_vma=False)
```

time: 174 us -> 63.8 us (0.37)
  local copies, waits for them, and re-layouts: 58.9 us -> 4.64 us
  matrix products: 26.9 us -> 0 us
  loops' own time: 26.9 us -> 0 us
  Pallas kernels: 0 us -> 17.4 us
  other arithmetic: 16.6 us -> 0 us
  blocking collectives: 16.6 us -> 7.92 us
  waiting for transfers between devices: 17.5 us -> 23.5 us
    dynamic_slice x56 -> x0, local copies, waits for them, and re-layouts: 36.4 us -> none  [the longest x40 24.3 us: one_slot(): position, inside = locate(route_row[slot_number])]
    another operation x10 -> x0, loops' own time: 26.9 us -> none  [the longest x8 26.4 us: add_block(): return lax.fori_loop(0, slot_limit, one_slot, accumulated)]
    dot_general x42 -> x0, matrix products: 26.9 us -> none  [the longest x40 24.1 us: one_slot(): jnp.dot(block_rows, matrix, precision=lax.Precision.HIGHEST, preferred_el...]
    pallas_call x0 -> x8, Pallas kernels: none -> 17.4 us  [call(): pl.pallas_call(kernel, out_shape=outs, in_specs=in_specs, out_specs=out_s...]
    psum x1 -> x0, blocking collectives: 16.6 us -> none  [shards(): energy = lax.psum(local_sum, 'col')]
    reduce_sum x41 -> x0, other arithmetic: 9.18 us -> none  [the longest x40 8 us: slot_matrix(): return jnp.sum(one_hot * chosen[:, :, None], axis=0)]
    all_to_all x0 -> x1, blocking collectives: none -> 7.92 us  [shards(): shares = lax.all_to_all(shares, 'col', 0, 0, tiled=True)]
    scatter-add x4 -> x0, other arithmetic: 6.34 us -> none  [the longest x2 4 us: spread(): owned = owned.at[:, :REACH].add(from_below)]
  transfers between devices with their start and end apart: 4 -> 6, of which waited for: 2 -> 4; matrix products, arithmetic and copies ran while one was open for 5% -> 0% of each run, Pallas kernels for 0% -> 5%
where the time goes in v2:
time: 63.8 us; the launch traced here: 63.4 us
  waiting for transfers between devices  23.5 us (37%)
  Pallas kernels  17.4 us (27%)
  starting transfers between devices  8.94 us (14%)
  blocking collectives  7.92 us (12%)
  local copies, waits for them, and re-layouts  4.64 us (7%)
  between operations  0.9 us (1%)
    ppermute x4, waiting for transfers between devices, z_exchange(): return lax.ppermute(value, 'col', pairs)  23.5 us
    pallas_call x8, Pallas kernels, call(): pl.pallas_call(kernel, out_shape=outs, in_specs=in_specs, out_specs=out_s...  17.4 us
    ppermute x4, starting transfers between devices, z_exchange(): return lax.ppermute(value, 'col', pairs)  8.35 us
    all_to_all x1, blocking collectives, shards(): shares = lax.all_to_all(shares, 'col', 0, 0, tiled=True)  7.92 us
    unnamed x18, local copies, waits for them, and re-layouts  4.64 us
  transfers between devices with their start and end apart: 6, of which 4 were waited for; matrix products, arithmetic and copies ran while one was open for 0% of the time, Pallas kernels for 5%

profile of v2, /device:TPU:0, one launch (start us, length us, event | category | flops | bytes accessed | tf_op | source)
XLA Modules:
  0.0 63.4 jit_solution(37173484318708050)
XLA Ops:
  0.6 0.0 copy-start
  0.6 1.2 %copy-done = f32[2,4,137,137]{3,1,2,0:T(4,128)S(1)} copy-done((f32[2,4,137,137]{3,1,2,0:T(4,128)S(1)}, f32[2,4,137,137]{3,1,2,0:T(4,128)}, u32[]{:S(2)}) %copy-start) | copy-done | bytes 600632
  1.9 1.2 %copy-done.2 = f32[4,137,512]{2,0,1:T(4,128)S(1)} copy-done((f32[4,137,512]{2,0,1:T(4,128)S(1)}, f32[4,137,512]{2,0,1:T(4,128)}, u32[]{:S(2)}) %copy-start.2) | copy-done | bytes 1122328
  3.1 0.7 %copy-done.3 = s32[2,4,512]{2,1,0:T(4,128)S(1)} copy-done((s32[2,4,512]{2,1,0:T(4,128)S(1)}, s32[2,4,512]{2,1,0:T(4,128)}, u32[]{:S(2)}) %copy-start.3) | copy-done | bytes 16408
  3.9 0.7 %copy-done.5 = f32[2,4,512]{2,1,0:T(4,128)S(1)} copy-done((f32[2,4,512]{2,1,0:T(4,128)S(1)}, f32[2,4,512]{2,1,0:T(4,128)}, u32[]{:S(2)}) %copy-start.5) | copy-done | bytes 16408
  4.6 0.7 %copy-done.7 = s32[2,4,5]{2,1,0:T(4,128)S(1)} copy-done((s32[2,4,5]{2,1,0:T(4,128)S(1)}, s32[2,4,5]{2,1,0:T(4,128)}, u32[]{:S(2)}) %copy-start.7) | copy-done | bytes 184
  5.3 2.0 %first_edge_step1.1 = (f32[137,4,128]{2,1,0:T(4,128)S(1)}, f32[137,4,128]{2,1,0:T(4,128)S(1)}) custom-call(f32[137,4,512]{2,1,0:T(4,128)S(1)} %bitcast.13, f32[2,137,4,137]{3,2,1,0:T(4,128)S(1)} %bitcast.8, s32[2,4,5]{2,1,0:T(4,128)S(1)} %copy-done.7, s32[2,4,512]{2,1,0:T(4,128)S(1)} %copy-done.3, f32[2,4,512]{2,1,0:T(4,128)S(1)} %copy-done.5), custom_call_target="tpu_custom_call" | custom-call | flops 400000000 | bytes 1000000 | tf_op jit(solution)/shard_map/first_edge_step1/pallas_call | solution.py:98
  7.3 0.0 copy-start.1
  7.3 0.0 copy-start.4
  7.3 0.0 copy-start.6
  7.3 0.0 copy-start.8
  7.3 5.3 %rest_step1.1 = (f32[137,4,512]{2,1,0:T(4,128)S(1)}, f32[137,4,256]{2,1,0:T(4,128)S(1)}) custom-call(f32[137,4,512]{2,1,0:T(4,128)S(1)} %bitcast.14, f32[2,137,4,137]{3,2,1,0:T(4,128)S(1)} %bitcast.9, s32[2,4,5]{2,1,0:T(4,128)S(1)} %copy-done.7, s32[2,4,512]{2,1,0:T(4,128)S(1)} %copy-done.3, f32[2,4,512]{2,1,0:T(4,128)S(1)} %copy-done.5, ...), custom_call_target="tpu_custom_call" | custom-call | flops 2000000000 | bytes 1000000 | tf_op jit(solution)/shard_map/rest_step1/pallas_call | solution.py:98
  12.6 0.5 collective-permute-start.2
  13.1 4.7 %collective-permute-start.1 = (f32[137,4,128]{2,1,0:T(4,128)S(1)}, f32[137,4,128]{2,1,0:T(4,128)S(1)}, u32[]{:S(2)}, u32[]{:S(2)}) collective-permute-start(f32[137,4,128]{2,1,0:T(4,128)S(1)} %get-tuple-element.13.refs_5_), channel_id=1, source_target_pairs={{0,7},{1,2},{2,1},{3,4},{4,3},{5,6},{6,5},{7,0},{8,15},{9,10},{10,... | collective-permute-start | bytes 841736 | tf_op jit(solution)/shard_map/ppermute | solution.py:396
  17.8 0.0 collective-permute-start
  17.9 7.1 %collective-permute-done.1.refs_1_.refs_7_ = f32[137,4,128]{2,1,0:T(4,128)S(1)} collective-permute-done((f32[137,4,128]{2,1,0:T(4,128)S(1)}, f32[137,4,128]{2,1,0:T(4,128)S(1)}, u32[]{:S(2)}, u32[]{:S(2)}) %collective-permute-start.1) | collective-permute-done | bytes 280608 | tf_op jit(solution)/shard_map/ppermute | solution.py:396
  25.0 0.0 copy-done.4
  25.0 1.5 %near_edge_step0.1 = (f32[137,4,128]{2,1,0:T(4,128)S(1)}, f32[137,4,128]{2,1,0:T(4,128)S(1)}) custom-call(f32[137,4,512]{2,1,0:T(4,128)S(1)} %get-tuple-element.14.refs_0_, f32[137,4,128]{2,1,0:T(4,128)S(1)} %collective-permute-done.1.refs_1_.refs_7_, f32[2,137,4,137]{3,2,1,0:T(4,128)S(1)} %bitcast.10, s32[2,4,5]{2,1,0:T(4,128)S(1)} %copy-done.8, ...), custom_call_target="tpu_custom_call" | custom-call | flops 300000000 | bytes 1000000 | tf_op jit(solution)/shard_map/near_edge_step0/pallas_call | solution.py:98
  26.5 3.8 %collective-permute-done.refs_1_.refs_8_ = f32[137,4,128]{2,1,0:T(4,128)S(1)} collective-permute-done((f32[137,4,128]{2,1,0:T(4,128)S(1)}, f32[137,4,128]{2,1,0:T(4,128)S(1)}, u32[]{:S(2)}, u32[]{:S(2)}) %collective-permute-start) | collective-permute-done | bytes 280608 | tf_op jit(solution)/shard_map/ppermute | solution.py:396
  30.4 1.5 %far_edge_step0.1.refs_5_ = f32[137,4,128]{2,1,0:T(4,128)S(1)} custom-call(f32[137,4,512]{2,1,0:T(4,128)S(1)} %get-tuple-element.14.refs_0_, f32[137,4,128]{2,1,0:T(4,128)S(1)} %collective-permute-done.refs_1_.refs_8_, f32[137,4,128]{2,1,0:T(4,128)S(1)} %get-tuple-element.16.refs_2_, f32[2,137,4,137]{3,2,1,0:T(4,128)S(1)} %bitcast.11, ...), custom_call_target="tpu_custom_call" | custom-call | flops 300000000 | bytes 1000000 | tf_op jit(solution)/shard_map/far_edge_step0/pallas_call | solution.py:98
  31.9 0.0 collective-permute-done.2.refs_6_
  32.0 5.3 %rest_step0.1 = (f32[137,4,512]{2,1,0:T(4,128)S(1)}, f32[137,4,256]{2,1,0:T(4,128)S(1)}, f32[137,4,512]{2,1,0:T(4,128)}) custom-call(f32[137,4,512]{2,1,0:T(4,128)S(1)} %get-tuple-element.14.refs_0_, f32[2,137,4,137]{3,2,1,0:T(4,128)S(1)} %bitcast.12, s32[2,4,5]{2,1,0:T(4,128)S(1)} %copy-done.8, s32[2,4,512]{2,1,0:T(4,128)S(1)} %copy-done.4, ...), custom_call_target="tpu_custom_call" | custom-call | flops 2000000000 | bytes 1000000 | tf_op jit(solution)/shard_map/rest_step0/pallas_call | solution.py:98
  37.2 0.1 collective-permute-start.3
  37.3 2.5 %collective-permute-start.4 = (f32[137,4,128]{2,1,0:T(4,128)S(1)}, f32[137,4,128]{2,1,0:T(4,128)S(1)}, u32[]{:S(2)}, u32[]{:S(2)}) collective-permute-start(f32[137,4,128]{2,1,0:T(4,128)S(1)} %get-tuple-element.21), channel_id=1, source_target_pairs={{0,7},{1,2},{2,1},{3,4},{4,3},{5,6},{6,5},{7,0},{8,15},{9,10},{10,... | collective-permute-start | bytes 841736 | tf_op jit(solution)/shard_map/ppermute | solution.py:396
  39.8 1.1 %collective-permute-start.5 = (f32[137,4,128]{2,1,0:T(4,128)S(1)}, f32[137,4,128]{2,1,0:T(4,128)S(1)}, u32[]{:S(2)}, u32[]{:S(2)}) collective-permute-start(f32[137,4,128]{2,1,0:T(4,128)S(1)} %far_edge_step0.1.refs_5_), channel_id=1, source_target_pairs={{0,7},{1,2},{2,1},{3,4},{4,3},{5,6},{6,5},{7,0},{8,15},{9,10},{10,... | collective-permute-start | bytes 841736 | tf_op jit(solution)/shard_map/ppermute | solution.py:396
  40.9 7.2 %collective-permute-done.4.far_in = f32[137,4,128]{2,1,0:T(4,128)S(1)} collective-permute-done((f32[137,4,128]{2,1,0:T(4,128)S(1)}, f32[137,4,128]{2,1,0:T(4,128)S(1)}, u32[]{:S(2)}, u32[]{:S(2)}) %collective-permute-start.4) | collective-permute-done | bytes 280608 | tf_op jit(solution)/shard_map/ppermute | solution.py:396
  48.1 0.0 collective-permute-done.3.core_in
  48.1 0.3 squares_of_most_blocks.1
  48.4 5.4 %collective-permute-done.5.near_in = f32[137,4,128]{2,1,0:T(4,128)S(1)} collective-permute-done((f32[137,4,128]{2,1,0:T(4,128)S(1)}, f32[137,4,128]{2,1,0:T(4,128)S(1)}, u32[]{:S(2)}, u32[]{:S(2)}) %collective-permute-start.5) | collective-permute-done | bytes 280608 | tf_op jit(solution)/shard_map/ppermute | solution.py:396
  53.8 0.1 squares_of_last_block.1
  53.9 7.9 %all_to_all.11 = f32[8,1,128]{2,1,0:T(1,128)S(1)} all-to-all(f32[8,1,128]{2,1,0:T(1,128)S(1)} %bitcast.16), channel_id=1, replica_groups=mesh['mem'=4,'col'=8] {'col'}, dimensions={0} | all-to-all | bytes 8192 | tf_op jit(solution)/shard_map/all_to_all | solution.py:420
  61.8 1.4 %scale_start.1 = f32[137,4,512]{2,1,0:T(4,128)} custom-call(f32[137,4,512]{2,1,0:T(4,128)S(1)} %get-tuple-element.22.start, f32[137,4,128]{2,1,0:T(4,128)S(1)} %collective-permute-done.5.near_in, f32[8,128]{1,0:T(8,128)S(1)} %bitcast.15), custom_call_target="tpu_custom_call" | custom-call | flops 1000000 | bytes 1000000 | tf_op jit(solution)/shard_map/scale_start/pallas_call | solution.py:98
  (7 shorter events, 0.0 us)
Async XLA Ops:
  0.6 1.3 %copy-start = (f32[2,4,137,137]{3,1,2,0:T(4,128)S(1)}, f32[2,4,137,137]{3,1,2,0:T(4,128)}, u32[]{:S(2)}) copy-start(f32[2,4,137,137]{3,1,2,0:T(4,128)} %param.6) | copy-start | bytes 1801828
  1.9 1.3 %copy-start.2 = (f32[4,137,512]{2,0,1:T(4,128)S(1)}, f32[4,137,512]{2,0,1:T(4,128)}, u32[]{:S(2)}) copy-start(f32[4,137,512]{2,0,1:T(4,128)} %param.5) | copy-start | bytes 3366916
  3.1 0.7 %copy-start.3 = (s32[2,4,512]{2,1,0:T(4,128)S(1)}, s32[2,4,512]{2,1,0:T(4,128)}, u32[]{:S(2)}) copy-start(s32[2,4,512]{2,1,0:T(4,128)} %refs_3_.7) | copy-start | bytes 49156
  3.9 0.7 %copy-start.5 = (f32[2,4,512]{2,1,0:T(4,128)S(1)}, f32[2,4,512]{2,1,0:T(4,128)}, u32[]{:S(2)}) copy-start(f32[2,4,512]{2,1,0:T(4,128)} %refs_4_.9) | copy-start | bytes 49156
  4.6 0.7 %copy-start.7 = (s32[2,4,5]{2,1,0:T(4,128)S(1)}, s32[2,4,5]{2,1,0:T(4,128)}, u32[]{:S(2)}) copy-start(s32[2,4,5]{2,1,0:T(4,128)} %refs_2_.5) | copy-start | bytes 484
  7.3 17.7 %copy-start.1 = (f32[2,4,137,137]{3,1,2,0:T(4,128)S(1)}, f32[2,4,137,137]{3,1,2,0:T(4,128)}, u32[]{:S(2)}) copy-start(f32[2,4,137,137]{3,1,2,0:T(4,128)} %param.6) | copy-start | bytes 1801828
  7.3 17.7 %copy-start.4 = (s32[2,4,512]{2,1,0:T(4,128)S(1)}, s32[2,4,512]{2,1,0:T(4,128)}, u32[]{:S(2)}) copy-start(s32[2,4,512]{2,1,0:T(4,128)} %refs_3_.7) | copy-start | bytes 49156
  7.3 17.7 %copy-start.6 = (f32[2,4,512]{2,1,0:T(4,128)S(1)}, f32[2,4,512]{2,1,0:T(4,128)}, u32[]{:S(2)}) copy-start(f32[2,4,512]{2,1,0:T(4,128)} %refs_4_.9) | copy-start | bytes 49156
  7.3 17.7 %copy-start.8 = (s32[2,4,5]{2,1,0:T(4,128)S(1)}, s32[2,4,5]{2,1,0:T(4,128)}, u32[]{:S(2)}) copy-start(s32[2,4,5]{2,1,0:T(4,128)} %refs_2_.5) | copy-start | bytes 484
  12.6 19.4 %collective-permute-start.2 = (f32[137,4,256]{2,1,0:T(4,128)S(1)}, f32[137,4,256]{2,1,0:T(4,128)S(1)}, u32[]{:S(2)}, u32[]{:S(2)}) collective-permute-start(f32[137,4,256]{2,1,0:T(4,128)S(1)} %get-tuple-element.17), channel_id=1, source_target_pairs={{0,1},{1,0},{2,3},{3,2},{4,5},{5,4},{6,7},{7,6},{8,9},{9,8},{10,11... | collective-permute-start | bytes 1683464 | tf_op jit(solution)/shard_map/ppermute | solution.py:390
  13.1 11.9 %collective-permute-start.1 = (f32[137,4,128]{2,1,0:T(4,128)S(1)}, f32[137,4,128]{2,1,0:T(4,128)S(1)}, u32[]{:S(2)}, u32[]{:S(2)}) collective-permute-start(f32[137,4,128]{2,1,0:T(4,128)S(1)} %get-tuple-element.13.refs_5_), channel_id=1, source_target_pairs={{0,7},{1,2},{2,1},{3,4},{4,3},{5,6},{6,5},{7,0},{8,15},{9,10},{10,... | collective-permute-start | bytes 841736 | tf_op jit(solution)/shard_map/ppermute | solution.py:396
  17.8 12.6 %collective-permute-start = (f32[137,4,128]{2,1,0:T(4,128)S(1)}, f32[137,4,128]{2,1,0:T(4,128)S(1)}, u32[]{:S(2)}, u32[]{:S(2)}) collective-permute-start(f32[137,4,128]{2,1,0:T(4,128)S(1)} %get-tuple-element.15), channel_id=1, source_target_pairs={{0,7},{1,2},{2,1},{3,4},{4,3},{5,6},{6,5},{7,0},{8,15},{9,10},{10,... | collective-permute-start | bytes 841736 | tf_op jit(solution)/shard_map/ppermute | solution.py:396
  37.2 10.9 %collective-permute-start.3 = (f32[137,4,256]{2,1,0:T(4,128)S(1)}, f32[137,4,256]{2,1,0:T(4,128)S(1)}, u32[]{:S(2)}, u32[]{:S(2)}) collective-permute-start(f32[137,4,256]{2,1,0:T(4,128)S(1)} %get-tuple-element.20), channel_id=1, source_target_pairs={{0,1},{1,0},{2,3},{3,2},{4,5},{5,4},{6,7},{7,6},{8,9},{9,8},{10,11... | collective-permute-start | bytes 1683464 | tf_op jit(solution)/shard_map/ppermute | solution.py:390
  37.3 10.8 %collective-permute-start.4 = (f32[137,4,128]{2,1,0:T(4,128)S(1)}, f32[137,4,128]{2,1,0:T(4,128)S(1)}, u32[]{:S(2)}, u32[]{:S(2)}) collective-permute-start(f32[137,4,128]{2,1,0:T(4,128)S(1)} %get-tuple-element.21), channel_id=1, source_target_pairs={{0,7},{1,2},{2,1},{3,4},{4,3},{5,6},{6,5},{7,0},{8,15},{9,10},{10,... | collective-permute-start | bytes 841736 | tf_op jit(solution)/shard_map/ppermute | solution.py:396
  39.8 14.0 %collective-permute-start.5 = (f32[137,4,128]{2,1,0:T(4,128)S(1)}, f32[137,4,128]{2,1,0:T(4,128)S(1)}, u32[]{:S(2)}, u32[]{:S(2)}) collective-permute-start(f32[137,4,128]{2,1,0:T(4,128)S(1)} %far_edge_step0.1.refs_5_), channel_id=1, source_target_pairs={{0,7},{1,2},{2,1},{3,4},{4,3},{5,6},{6,5},{7,0},{8,15},{9,10},{10,... | collective-permute-start | bytes 841736 | tf_op jit(solution)/shard_map/ppermute | solution.py:396

commit v3 on v2

--- a/solution.py
+++ b/solution.py
@@ -13,6 +13,7 @@
 POINTS = 4
 STEPS = 2
 VMEM_LIMIT = 32 * 1024 * 1024
+FIRST_LIMIT = 62 * 1024 * 1024
 
 eps_energy = 1e-06
 
@@ -94,24 +95,25 @@
     return copies
 
 
-def call(kernel, operands, in_specs, outs, out_specs, scratch, flops, name):
+def call(kernel, operands, in_specs, outs, out_specs, scratch, flops, name, limit=VMEM_LIMIT):
     return pl.pallas_call(
         kernel,
         out_shape=outs,
         in_specs=in_specs,
         out_specs=out_specs,
         scratch_shapes=scratch,
-        compiler_params=pltpu.CompilerParams(vmem_limit_bytes=VMEM_LIMIT),
+        compiler_params=pltpu.CompilerParams(vmem_limit_bytes=limit),
         cost_estimate=pl.CostEstimate(flops=flops, bytes_accessed=1_000_000, transcendentals=0),
         name=name,
     )(*operands)
 
 
 def first_edge_kernel(step, all_blocks, *refs):
-    fields, inverses, routes, points, weights, to_near, to_far = refs[:7]
-    field, inverse, route, point, weight, tall, sems = refs[7:]
+    fields, inverses, routes, points, weights, to_near, to_far, to_core = refs[:8]
+    field, inverse, route, point, weight, tall, sems = refs[8:]
     block_count = inverses.shape[2]
     near, far, target_near, target_far = z_blocks(block_count)
+    first, first_target = core_side(block_count)
     copies = fetch(
         sems,
         [
@@ -121,25 +123,30 @@
             (inverses.at[step], inverse),
             (fields.at[:, :, lanes(near)], field.at[0]),
             (fields.at[:, :, lanes(far)], field.at[1]),
+            (fields.at[:, :, lanes(first)], field.at[2]),
+            (fields.at[:, :, lanes(first + 1)], field.at[3]),
         ],
     )
     for copy in copies[:3]:
         copy.wait()
-    matrices = []
-    for block in (near, far):
-        targets = target_columns(point[:, lanes(block)], route, step, block, block_count, all_blocks)
-        halves = [
-            spread_matrix(targets, weight[:, lanes(block)], target * BCOLS) for target in (target_near, target_far)
-        ]
-        matrices.append([jnp.concatenate(parts, axis=0) for parts in zip(*halves)])
-    matrix = [jnp.concatenate(parts, axis=1) for parts in zip(*matrices)]
+    def matrix_of(blocks, first_columns):
+        parts = []
+        for block in blocks:
+            targets = target_columns(point[:, lanes(block)], route, step, block, block_count, all_blocks)
+            halves = [spread_matrix(targets, weight[:, lanes(block)], column) for column in first_columns]
+            parts.append([jnp.concatenate(half, axis=0) for half in zip(*halves)])
+        return [jnp.concatenate(part, axis=1) for part in zip(*parts)]
+
+    z_matrix = matrix_of((near, far), (target_near * BCOLS, target_far * BCOLS))
+    core_matrix = matrix_of((first, first + 1), (first_target * BCOLS, (first_target + 1) * BCOLS))
     for copy in copies[3:]:
         copy.wait()
-    for j, block in enumerate((near, far)):
+    for j, block in enumerate((near, far, first, first + 1)):
         diffuse(inverse[:, block, :], field.at[j], tall, slice(j * BCOLS, (j + 1) * BCOLS))
-    sums = spread(tall[...], matrix)
+    sums = spread(tall[:, :, : 2 * BCOLS], z_matrix)
     to_near[...] = sums[:, :, :BCOLS]
     to_far[...] = sums[:, :, BCOLS:]
+    to_core[...] = spread(tall[:, :, 2 * BCOLS :], core_matrix)
 
 
 def tables_scratch(inverses, routes):
@@ -159,16 +166,17 @@
         functools.partial(first_edge_kernel, step, all_blocks),
         (fields, *tables),
         [HBM] * 5,
-        (one, one),
-        (VMEM, VMEM),
-        [
-            pltpu.VMEM((2, levels, variables, BCOLS), F32),
+        (one, one, jax.ShapeDtypeStruct((levels, variables, REACH * BCOLS), F32)),
+        (VMEM, VMEM, VMEM),
+        [
+            pltpu.VMEM((4, levels, variables, BCOLS), F32),
             *tables_scratch(*tables[:2]),
-            pltpu.VMEM((levels, variables, 2 * BCOLS), F32),
-            pltpu.SemaphoreType.DMA((6,)),
+            pltpu.VMEM((levels, variables, 4 * BCOLS), F32),
+            pltpu.SemaphoreType.DMA((8,)),
         ],
         400_000_000,
         f"first_edge_step{step}",
+        FIRST_LIMIT,
     )
 
 
@@ -246,65 +254,128 @@
     )
 
 
-def rest_kernel(step, all_blocks, has_halo, *refs):
-    fields, inverses, routes, points, weights, _ = refs[:6]
-    halos = refs[6 : 6 + 3 * has_halo]
-    refs = refs[6 + 3 * has_halo :]
-    own, core_out = refs[:2]
-    mid = refs[2] if has_halo else None
-    inverse, route, point, weight, field, tall, sems = refs[2 + has_halo :]
+def inner_kernel(step, all_blocks, fields, inverses, routes, points, weights, core_in, own, *scratch):
+    inverse, route, point, weight, field, tall, sems = scratch
     block_count = inverses.shape[2]
-    near, far, _, _ = z_blocks(block_count)
-    core_first, core_target = core_side(block_count)
-    pairs = [(routes, route), (points.at[step], point), (weights.at[step], weight), (inverses.at[step], inverse)]
-    if not has_halo:
-        pairs.append((fields, field))
-    copies = fetch(sems, pairs)
-    if has_halo:
-        core_in, near_in, far_in = halos
-        field[:, :, lanes(core_first, REACH)] = fields[:, :, lanes(core_first, REACH)] + core_in[...]
-        field[:, :, lanes(near)] = fields[:, :, lanes(near)] + near_in[...]
-        field[:, :, lanes(far)] = fields[:, :, lanes(far)] + far_in[...]
-        mid_copy = pltpu.make_async_copy(field, mid, sems.at[5])
-        mid_copy.start()
+    copies = fetch(
+        sems,
+        [
+            (routes, route),
+            (points.at[step], point),
+            (weights.at[step], weight),
+            (inverses.at[step], inverse),
+            (fields, field),
+        ],
+    )
     for copy in copies[:3]:
         copy.wait()
+    diffuse_and_spread(step, all_blocks, copies[3:], inverse, route, point, weight, field, tall, own)
+    side = lanes(core_side(block_count)[0], REACH)
+    own[:, :, side] += core_in[...]
+
+
+def diffuse_and_spread(step, all_blocks, copies, inverse, route, point, weight, field, tall, own):
+    block_count = inverse.shape[1]
     for j in range(block_count):
         cols = slice(j * BCOLS, (j + 1) * BCOLS)
         point[:, cols] = target_columns(point[:, cols], route, step, j, block_count, all_blocks)
-    side = lanes(core_first, REACH)
-    outer = spread_matrix(point[:, side], weight[:, side], core_target * BCOLS, REACH * BCOLS)
-    inner = spread_matrix(point[...], weight[...], 0, block_count * BCOLS)
-    for copy in copies[3:]:
+    matrix = spread_matrix(point[...], weight[...], 0, block_count * BCOLS)
+    for copy in copies:
         copy.wait()
     for j in range(block_count):
         cols = slice(j * BCOLS, (j + 1) * BCOLS)
         diffuse(inverse[:, j, :], field.at[:, :, cols], tall, cols)
-    core_out[...] = spread(tall[:, :, side], outer)
-    own[...] = spread(tall[...], inner)
-    if has_halo:
-        mid_copy.wait()
-
-
-def rest(step, all_blocks, fields, tables, behind, halos=()):
-    levels, variables, _ = fields.shape
-    has_halo = bool(halos)
-    whole = jax.ShapeDtypeStruct(fields.shape, F32)
-    side = jax.ShapeDtypeStruct((levels, variables, REACH * BCOLS), F32)
-    return call(
-        functools.partial(rest_kernel, step, all_blocks, has_halo),
-        (fields, *tables, behind, *halos),
-        [VMEM if has_halo else HBM] + [HBM] * 4 + [ANY] + [VMEM] * len(halos),
-        (whole, side) + ((whole,) if has_halo else ()),
-        (VMEM, VMEM) + ((HBM,) if has_halo else ()),
+    own[...] = spread(tall[...], matrix)
+
+
+def inner(step, all_blocks, fields, tables, core_in):
+    return call(
+        functools.partial(inner_kernel, step, all_blocks),
+        (fields, *tables, core_in),
+        [HBM] * 5 + [VMEM],
+        jax.ShapeDtypeStruct(fields.shape, F32),
+        VMEM,
         [
             *tables_scratch(*tables[:2]),
             pltpu.VMEM(fields.shape, F32),
             pltpu.VMEM(fields.shape, F32),
-            pltpu.SemaphoreType.DMA((6,)),
+            pltpu.SemaphoreType.DMA((5,)),
         ],
         2_000_000_000,
-        f"rest_step{step}",
+        f"inner_step{step}",
+    )
+
+
+def core_edge_kernel(step, all_blocks, fields, inverses, routes, points, weights, to_core, *scratch):
+    inverse, route, point, weight, tall, sems = scratch
+    block_count = inverses.shape[2]
+    first, first_target = core_side(block_count)
+    copies = fetch(
+        sems, [(routes, route), (points.at[step], point), (weights.at[step], weight), (inverses.at[step], inverse)]
+    )
+    for copy in copies:
+        copy.wait()
+    parts = []
+    for j in range(REACH):
+        block = first + j
+        targets = target_columns(point[:, lanes(block)], route, step, block, block_count, all_blocks)
+        parts.append(spread_matrix(targets, weight[:, lanes(block)], first_target * BCOLS, REACH * BCOLS))
+        cols = slice(j * BCOLS, (j + 1) * BCOLS)
+        diffuse(inverse[:, block, :], fields.at[:, :, lanes(block)], tall, cols)
+    matrix = [jnp.concatenate(part, axis=1) for part in zip(*parts)]
+    to_core[...] = spread(tall[...], matrix)
+
+
+def core_edge(step, all_blocks, fields, tables):
+    levels, variables, _ = fields.shape
+    side = (levels, variables, REACH * BCOLS)
+    return call(
+        functools.partial(core_edge_kernel, step, all_blocks),
+        (fields, *tables),
+        [VMEM] + [HBM] * 4,
+        jax.ShapeDtypeStruct(side, F32),
+        VMEM,
+        [*tables_scratch(*tables[:2]), pltpu.VMEM(side, F32), pltpu.SemaphoreType.DMA((4,))],
+        400_000_000,
+        f"core_edge_step{step}",
+    )
+
+
+def outer_kernel(step, all_blocks, fields, near_in, far_in, inverses, routes, points, weights, _, own, mid, *scratch):
+    inverse, route, point, weight, field, tall, sems = scratch
+    block_count = inverses.shape[2]
+    near, far, _, _ = z_blocks(block_count)
+    first = core_side(block_count)[0]
+    copies = fetch(
+        sems, [(routes, route), (points.at[step], point), (weights.at[step], weight), (inverses.at[step], inverse)]
+    )
+    field[:, :, lanes(first, REACH)] = fields[:, :, lanes(first, REACH)]
+    field[:, :, lanes(near)] = fields[:, :, lanes(near)] + near_in[...]
+    field[:, :, lanes(far)] = fields[:, :, lanes(far)] + far_in[...]
+    mid_copy = pltpu.make_async_copy(field, mid, sems.at[4])
+    mid_copy.start()
+    for copy in copies[:3]:
+        copy.wait()
+    diffuse_and_spread(step, all_blocks, copies[3:], inverse, route, point, weight, field, tall, own)
+    mid_copy.wait()
+
+
+def outer(step, all_blocks, fields, near_in, far_in, tables, behind):
+    whole = jax.ShapeDtypeStruct(fields.shape, F32)
+    return call(
+        functools.partial(outer_kernel, step, all_blocks),
+        (fields, near_in, far_in, *tables, behind),
+        [VMEM] * 3 + [HBM] * 4 + [ANY],
+        (whole, whole),
+        (VMEM, HBM),
+        [
+            *tables_scratch(*tables[:2]),
+            pltpu.VMEM(fields.shape, F32),
+            pltpu.VMEM(fields.shape, F32),
+            pltpu.SemaphoreType.DMA((5,)),
+        ],
+        2_000_000_000,
+        f"outer_step{step}",
     )
 
 
@@ -402,20 +473,19 @@
     fields = jnp.transpose(adj_final, (1, 0, 2))
     tables = (jnp.transpose(inverses, (0, 2, 1, 3)), dep_lists, dep_points, weights)
 
-    to_near, to_far = first_edge(1, all_blocks, fields, tables)
+    to_near, to_far, to_core = first_edge(1, all_blocks, fields, tables)
     near_in = z_exchange(to_near)
     far_in = z_exchange(to_far)
-    own, core_out = rest(1, all_blocks, fields, tables, to_near)
-    core_in = core_exchange(core_out)
-
+    own = inner(1, all_blocks, fields, tables, core_exchange(to_core))
+
+    next_core_in = core_exchange(core_edge(0, all_blocks, own, tables))
     to_far, partial = near_edge(0, all_blocks, own, near_in, tables)
     next_far_in = z_exchange(to_far)
     to_near = far_edge(0, all_blocks, own, far_in, partial, tables)
     next_near_in = z_exchange(to_near)
-    own, core_out, mid = rest(0, all_blocks, own, tables, to_near, (core_in, near_in, far_in))
-    core_in = core_exchange(core_out)
-
-    start, lane_sums = most(own, core_in, next_far_in)
+    own, mid = outer(0, all_blocks, own, near_in, far_in, tables, to_near)
+
+    start, lane_sums = most(own, next_core_in, next_far_in)
     shares = last(count, start, next_near_in, lane_sums)
     shares = lax.all_to_all(shares, "col", 0, 0, tiled=True)
     lanczos = scale(start, next_near_in, shares, adj_final.size * count)

time: 63.8 us -> 48.1 us (0.75)
  waiting for transfers between devices: 23.5 us -> 4.93 us
  Pallas kernels: 17.4 us -> 21.4 us
  local copies, waits for them, and re-layouts: 4.64 us -> 1.26 us
  blocking collectives: 7.92 us -> 9.25 us
  starting transfers between devices: 8.94 us -> 10.1 us
    ppermute x4, waiting for transfers between devices: 23.5 us -> 4.93 us  [z_exchange(): return lax.ppermute(value, 'col', pairs)]
    pallas_call x8 -> x9, Pallas kernels: 17.4 us -> 21.4 us  [call(): pl.pallas_call(kernel, out_shape=outs, in_specs=in_specs, out_specs=out_s...]
    unnamed x18 -> x10, local copies, waits for them, and re-layouts: 4.64 us -> 1.26 us
    all_to_all x1, blocking collectives: 7.92 us -> 9.25 us  [shards(): shares = lax.all_to_all(shares, 'col', 0, 0, tiled=True)]
    ppermute x4, starting transfers between devices: 8.35 us -> 9.5 us  [z_exchange(): return lax.ppermute(value, 'col', pairs)]
  transfers between devices with their start and end apart: 6 -> 6, of which waited for: 4 -> 1; matrix products, arithmetic and copies ran while one was open for 0% -> 0% of each run, Pallas kernels for 5% -> 31%
where the time goes in v3:
time: 48.1 us; the launch traced here: 47.8 us
  Pallas kernels  21.4 us (44%)
  starting transfers between devices  10.1 us (21%)
  blocking collectives  9.25 us (19%)
  waiting for transfers between devices  4.93 us (10%)
  local copies, waits for them, and re-layouts  1.26 us (3%)
  between operations  0.94 us (2%)
    pallas_call x9, Pallas kernels, call(): pl.pallas_call(kernel, out_shape=outs, in_specs=in_specs, out_specs=out_s...  21.4 us
    ppermute x4, starting transfers between devices, z_exchange(): return lax.ppermute(value, 'col', pairs)  9.5 us
    all_to_all x1, blocking collectives, shards(): shares = lax.all_to_all(shares, 'col', 0, 0, tiled=True)  9.25 us
    ppermute x4, waiting for transfers between devices, z_exchange(): return lax.ppermute(value, 'col', pairs)  4.93 us
    unnamed x10, local copies, waits for them, and re-layouts  1.26 us
  transfers between devices with their start and end apart: 6, of which 1 were waited for; matrix products, arithmetic and copies ran while one was open for 0% of the time, Pallas kernels for 31%

profile of v3, /device:TPU:0, one launch (start us, length us, event | category | flops | bytes accessed | tf_op | source)
XLA Modules:
  0.0 47.8 jit_solution(10374930793636651989)
XLA Ops:
  0.6 0.0 copy-start
  0.6 0.0 copy-start.2
  0.7 0.0 copy-start.3
  0.7 0.0 copy-start.4
  0.7 4.9 %first_edge_step1.1 = (f32[137,4,128]{2,1,0:T(4,128)}, f32[137,4,128]{2,1,0:T(4,128)}, f32[137,4,256]{2,1,0:T(4,128)}) custom-call(f32[137,4,512]{2,1,0:T(4,128)} %bitcast.14, f32[2,137,4,137]{3,2,1,0:T(4,128)} %bitcast.8, s32[2,4,5]{2,1,0:T(4,128)} %routes.5, s32[2,4,512]{2,1,0:T(4,128)} %points.5, f32[2,4,512]{2,1,0:T(4,128)} %weights.5), custom_call_target="tpu_custom_call" | custom-call | flops 400000000 | bytes 1000000 | tf_op jit(solution)/shard_map/first_edge_step1/pallas_call | solution.py:99
  5.6 0.5 %collective-permute-start = (f32[137,4,256]{2,1,0:T(4,128)}, f32[137,4,256]{2,1,0:T(4,128)S(1)}, u32[]{:S(2)}, u32[]{:S(2)}) collective-permute-start(f32[137,4,256]{2,1,0:T(4,128)} %get-tuple-element.11), channel_id=1, source_target_pairs={{0,1},{1,0},{2,3},{3,2},{4,5},{5,4},{6,7},{7,6},{8,9},{9,8},{10,11... | collective-permute-start | bytes 1683464 | tf_op jit(solution)/shard_map/ppermute | solution.py:461
  6.1 4.7 %collective-permute-start.1 = (f32[137,4,128]{2,1,0:T(4,128)}, f32[137,4,128]{2,1,0:T(4,128)S(1)}, u32[]{:S(2)}, u32[]{:S(2)}) collective-permute-start(f32[137,4,128]{2,1,0:T(4,128)} %get-tuple-element.12), channel_id=1, source_target_pairs={{0,7},{1,2},{2,1},{3,4},{4,3},{5,6},{6,5},{7,0},{8,15},{9,10},{10,... | collective-permute-start | bytes 841736 | tf_op jit(solution)/shard_map/ppermute | solution.py:467
  10.8 0.0 collective-permute-start.2
  10.8 0.0 collective-permute-done.core_in
  10.8 0.0 copy-done
  10.8 0.0 copy-done.2
  10.9 0.0 copy-done.3
  10.9 0.0 copy-done.4
  10.9 0.0 copy-start.1
  10.9 1.2 %copy-done.1 = f32[4,137,512]{2,0,1:T(4,128)S(1)} copy-done((f32[4,137,512]{2,0,1:T(4,128)S(1)}, f32[4,137,512]{2,0,1:T(4,128)}, u32[]{:S(2)}) %copy-start.1) | copy-done | bytes 1122328
  12.1 4.8 %inner_step1.1.refs_0_.fields = f32[137,4,512]{2,1,0:T(4,128)S(1)} custom-call(f32[137,4,512]{2,1,0:T(4,128)S(1)} %bitcast.15, f32[2,137,4,137]{3,2,1,0:T(4,128)S(1)} %bitcast.9, s32[2,4,5]{2,1,0:T(4,128)S(1)} %copy-done.4, s32[2,4,512]{2,1,0:T(4,128)S(1)} %copy-done.2, f32[2,4,512]{2,1,0:T(4,128)S(1)} %copy-done.3, ...), custom_call_target="tpu_custom_call" | custom-call | flops 2000000000 | bytes 1000000 | tf_op jit(solution)/shard_map/inner_step1/pallas_call | solution.py:99
  17.0 2.0 %core_edge_step0.1 = f32[137,4,256]{2,1,0:T(4,128)S(1)} custom-call(f32[137,4,512]{2,1,0:T(4,128)S(1)} %inner_step1.1.refs_0_.fields, f32[2,137,4,137]{3,2,1,0:T(4,128)S(1)} %bitcast.10, s32[2,4,5]{2,1,0:T(4,128)S(1)} %copy-done.4, s32[2,4,512]{2,1,0:T(4,128)S(1)} %copy-done.2, f32[2,4,512]{2,1,0:T(4,128)S(1)} %copy-done.3), custom_call_target="tpu_custom_call" | custom-call | flops 400000000 | bytes 1000000 | tf_op jit(solution)/shard_map/core_edge_step0/pallas_call | solution.py:99
  19.0 0.1 collective-permute-start.3
  19.1 0.0 collective-permute-done.1.refs_1_.near_in
  19.1 1.5 %near_edge_step0.1 = (f32[137,4,128]{2,1,0:T(4,128)S(1)}, f32[137,4,128]{2,1,0:T(4,128)S(1)}) custom-call(f32[137,4,512]{2,1,0:T(4,128)S(1)} %inner_step1.1.refs_0_.fields, f32[137,4,128]{2,1,0:T(4,128)S(1)} %collective-permute-done.1.refs_1_.near_in, f32[2,137,4,137]{3,2,1,0:T(4,128)S(1)} %bitcast.11, s32[2,4,5]{2,1,0:T(4,128)S(1)} %copy-done.4, ...), custom_call_target="tpu_custom_call" | custom-call | flops 300000000 | bytes 1000000 | tf_op jit(solution)/shard_map/near_edge_step0/pallas_call | solution.py:99
  20.7 3.5 %collective-permute-start.4 = (f32[137,4,128]{2,1,0:T(4,128)S(1)}, f32[137,4,128]{2,1,0:T(4,128)S(1)}, u32[]{:S(2)}, u32[]{:S(2)}) collective-permute-start(f32[137,4,128]{2,1,0:T(4,128)S(1)} %get-tuple-element.17), channel_id=1, source_target_pairs={{0,7},{1,2},{2,1},{3,4},{4,3},{5,6},{6,5},{7,0},{8,15},{9,10},{10,... | collective-permute-start | bytes 841736 | tf_op jit(solution)/shard_map/ppermute | solution.py:467
  24.2 0.0 collective-permute-done.2.refs_1_.far_in
  24.2 1.5 %far_edge_step0.1._ = f32[137,4,128]{2,1,0:T(4,128)S(1)} custom-call(f32[137,4,512]{2,1,0:T(4,128)S(1)} %inner_step1.1.refs_0_.fields, f32[137,4,128]{2,1,0:T(4,128)S(1)} %collective-permute-done.2.refs_1_.far_in, f32[137,4,128]{2,1,0:T(4,128)S(1)} %get-tuple-element.14.refs_2_, f32[2,137,4,137]{3,2,1,0:T(4,128)S(1)} %bitcast.12, s32[2,4,5]{2,1,0:T(4,128)S(1)} %copy-done.4, ...), custom_call_target="tpu_custom_call" | custom-call | flops 300000000 | bytes 1000000 | tf_op jit(solution)/shard_map/far_edge_step0/pallas_call | solution.py:99
  25.8 1.2 %collective-permute-start.5 = (f32[137,4,128]{2,1,0:T(4,128)S(1)}, f32[137,4,128]{2,1,0:T(4,128)S(1)}, u32[]{:S(2)}, u32[]{:S(2)}) collective-permute-start(f32[137,4,128]{2,1,0:T(4,128)S(1)} %far_edge_step0.1._), channel_id=1, source_target_pairs={{0,7},{1,2},{2,1},{3,4},{4,3},{5,6},{6,5},{7,0},{8,15},{9,10},{10,... | collective-permute-start | bytes 841736 | tf_op jit(solution)/shard_map/ppermute | solution.py:467
  27.0 4.7 %outer_step0.1 = (f32[137,4,512]{2,1,0:T(4,128)S(1)}, f32[137,4,512]{2,1,0:T(4,128)}) custom-call(f32[137,4,512]{2,1,0:T(4,128)S(1)} %inner_step1.1.refs_0_.fields, f32[137,4,128]{2,1,0:T(4,128)S(1)} %collective-permute-done.1.refs_1_.near_in, f32[137,4,128]{2,1,0:T(4,128)S(1)} %collective-permute-done.2.refs_1_.far_in, f32[2,137,4,137]{3,2,1,0:T(4,128)S(1)} %bitcast.13, ...), custom_call_target="tpu_custom_call" | custom-call | flops 2000000000 | bytes 1000000 | tf_op jit(solution)/shard_map/outer_step0/pallas_call | solution.py:99
  31.7 0.0 collective-permute-done.4.far_in
  31.7 0.0 collective-permute-done.3.core_in
  31.7 0.3 squares_of_most_blocks.1
  32.1 4.9 %collective-permute-done.5.near_in = f32[137,4,128]{2,1,0:T(4,128)S(1)} collective-permute-done((f32[137,4,128]{2,1,0:T(4,128)S(1)}, f32[137,4,128]{2,1,0:T(4,128)S(1)}, u32[]{:S(2)}, u32[]{:S(2)}) %collective-permute-start.5) | collective-permute-done | bytes 280608 | tf_op jit(solution)/shard_map/ppermute | solution.py:467
  37.0 0.1 squares_of_last_block.1
  37.1 9.3 %all_to_all.11 = f32[8,1,128]{2,1,0:T(1,128)S(1)} all-to-all(f32[8,1,128]{2,1,0:T(1,128)S(1)} %bitcast.17), channel_id=1, replica_groups=mesh['mem'=4,'col'=8] {'col'}, dimensions={0} | all-to-all | bytes 8192 | tf_op jit(solution)/shard_map/all_to_all | solution.py:490
  46.3 1.4 %scale_start.1 = f32[137,4,512]{2,1,0:T(4,128)} custom-call(f32[137,4,512]{2,1,0:T(4,128)S(1)} %get-tuple-element.18.start, f32[137,4,128]{2,1,0:T(4,128)S(1)} %collective-permute-done.5.near_in, f32[8,128]{1,0:T(8,128)S(1)} %bitcast.16), custom_call_target="tpu_custom_call" | custom-call | flops 1000000 | bytes 1000000 | tf_op jit(solution)/shard_map/scale_start/pallas_call | solution.py:99
Async XLA Ops:
  0.6 10.2 %copy-start = (f32[2,4,137,137]{3,1,2,0:T(4,128)S(1)}, f32[2,4,137,137]{3,1,2,0:T(4,128)}, u32[]{:S(2)}) copy-start(f32[2,4,137,137]{3,1,2,0:T(4,128)} %param.6) | copy-start | bytes 1801828
  0.6 10.2 %copy-start.2 = (s32[2,4,512]{2,1,0:T(4,128)S(1)}, s32[2,4,512]{2,1,0:T(4,128)}, u32[]{:S(2)}) copy-start(s32[2,4,512]{2,1,0:T(4,128)} %points.5) | copy-start | bytes 49156
  0.7 10.2 %copy-start.3 = (f32[2,4,512]{2,1,0:T(4,128)S(1)}, f32[2,4,512]{2,1,0:T(4,128)}, u32[]{:S(2)}) copy-start(f32[2,4,512]{2,1,0:T(4,128)} %weights.5) | copy-start | bytes 49156
  0.7 10.2 %copy-start.4 = (s32[2,4,5]{2,1,0:T(4,128)S(1)}, s32[2,4,5]{2,1,0:T(4,128)}, u32[]{:S(2)}) copy-start(s32[2,4,5]{2,1,0:T(4,128)} %routes.5) | copy-start | bytes 484
  5.6 5.3 %collective-permute-start = (f32[137,4,256]{2,1,0:T(4,128)}, f32[137,4,256]{2,1,0:T(4,128)S(1)}, u32[]{:S(2)}, u32[]{:S(2)}) collective-permute-start(f32[137,4,256]{2,1,0:T(4,128)} %get-tuple-element.11), channel_id=1, source_target_pairs={{0,1},{1,0},{2,3},{3,2},{4,5},{5,4},{6,7},{7,6},{8,9},{9,8},{10,11... | collective-permute-start | bytes 1683464 | tf_op jit(solution)/shard_map/ppermute | solution.py:461
  6.1 13.0 %collective-permute-start.1 = (f32[137,4,128]{2,1,0:T(4,128)}, f32[137,4,128]{2,1,0:T(4,128)S(1)}, u32[]{:S(2)}, u32[]{:S(2)}) collective-permute-start(f32[137,4,128]{2,1,0:T(4,128)} %get-tuple-element.12), channel_id=1, source_target_pairs={{0,7},{1,2},{2,1},{3,4},{4,3},{5,6},{6,5},{7,0},{8,15},{9,10},{10,... | collective-permute-start | bytes 841736 | tf_op jit(solution)/shard_map/ppermute | solution.py:467
  10.8 13.4 %collective-permute-start.2 = (f32[137,4,128]{2,1,0:T(4,128)}, f32[137,4,128]{2,1,0:T(4,128)S(1)}, u32[]{:S(2)}, u32[]{:S(2)}) collective-permute-start(f32[137,4,128]{2,1,0:T(4,128)} %get-tuple-element.13), channel_id=1, source_target_pairs={{0,7},{1,2},{2,1},{3,4},{4,3},{5,6},{6,5},{7,0},{8,15},{9,10},{10,... | collective-permute-start | bytes 841736 | tf_op jit(solution)/shard_map/ppermute | solution.py:467
  10.9 1.3 %copy-start.1 = (f32[4,137,512]{2,0,1:T(4,128)S(1)}, f32[4,137,512]{2,0,1:T(4,128)}, u32[]{:S(2)}) copy-start(f32[4,137,512]{2,0,1:T(4,128)} %param.5) | copy-start | bytes 3366916
  19.0 12.7 %collective-permute-start.3 = (f32[137,4,256]{2,1,0:T(4,128)S(1)}, f32[137,4,256]{2,1,0:T(4,128)S(1)}, u32[]{:S(2)}, u32[]{:S(2)}) collective-permute-start(f32[137,4,256]{2,1,0:T(4,128)S(1)} %core_edge_step0.1), channel_id=1, source_target_pairs={{0,1},{1,0},{2,3},{3,2},{4,5},{5,4},{6,7},{7,6},{8,9},{9,8},{10,11... | collective-permute-start | bytes 1683464 | tf_op jit(solution)/shard_map/ppermute | solution.py:461
  20.7 11.0 %collective-permute-start.4 = (f32[137,4,128]{2,1,0:T(4,128)S(1)}, f32[137,4,128]{2,1,0:T(4,128)S(1)}, u32[]{:S(2)}, u32[]{:S(2)}) collective-permute-start(f32[137,4,128]{2,1,0:T(4,128)S(1)} %get-tuple-element.17), channel_id=1, source_target_pairs={{0,7},{1,2},{2,1},{3,4},{4,3},{5,6},{6,5},{7,0},{8,15},{9,10},{10,... | collective-permute-start | bytes 841736 | tf_op jit(solution)/shard_map/ppermute | solution.py:467
  25.8 11.2 %collective-permute-start.5 = (f32[137,4,128]{2,1,0:T(4,128)S(1)}, f32[137,4,128]{2,1,0:T(4,128)S(1)}, u32[]{:S(2)}, u32[]{:S(2)}) collective-permute-start(f32[137,4,128]{2,1,0:T(4,128)S(1)} %far_edge_step0.1._), channel_id=1, source_target_pairs={{0,7},{1,2},{2,1},{3,4},{4,3},{5,6},{6,5},{7,0},{8,15},{9,10},{10,... | collective-permute-start | bytes 841736 | tf_op jit(solution)/shard_map/ppermute | solution.py:467

commit v4 on v2

v4 whole, which is shorter than its diff:
```python
import functools

import jax
import jax.numpy as jnp
from jax import lax
from jax.experimental import pallas as pl
from jax.experimental.pallas import tpu as pltpu
from jax.sharding import PartitionSpec as P

BCOLS = 128
REACH = 2
SLOTS = 5
POINTS = 4
STEPS = 2
VMEM_LIMIT = 32 * 1024 * 1024
NOWHERE = -(1 << 14)

eps_energy = 1e-06

F32 = jnp.float32
BF16 = jnp.bfloat16
HBM = pl.BlockSpec(memory_space=pltpu.HBM)
VMEM = pl.BlockSpec(memory_space=pltpu.VMEM)


def z_blocks(block_count):
    follows = lax.rem(lax.axis_index("col"), 2)
    near = follows * (block_count - 1)
    away = 2 * follows - 1
    return near, near - away, near + away, near + 2 * away


def core_side(block_count):
    follows = 1 - lax.rem(lax.axis_index("col"), 2)
    return follows * (block_count - REACH), follows * (block_count + REACH) - REACH


def lanes(block, count=1):
    return pl.ds(pl.multiple_of(block * BCOLS, BCOLS), count * BCOLS)


def split(value):
    high = value.astype(BF16)
    return high, (value - high.astype(F32)).astype(BF16)


def target_columns(points, routes, step, block, block_count, all_blocks):
    slots = points // BCOLS
    here = lax.axis_index("col") * block_count + block
    found = jnp.zeros_like(points)
    for slot in range(SLOTS):
        offset = lax.rem(routes[step, block, slot] - here + REACH + all_blocks, all_blocks) - REACH
        found = jnp.where(slots == slot, (block + offset) * BCOLS, found)
    return found + points % BCOLS


def merge_points(targets, weights):
    targets = [targets[p : p + 1] for p in range(POINTS)]
    weights = [weights[p : p + 1] for p in range(POINTS)]
    for point in range(1, POINTS):
        for earlier in range(point):
            same = targets[point] == targets[earlier]
            weights[earlier] = weights[earlier] + jnp.where(same, weights[point], 0.0)
            targets[point] = jnp.where(same, NOWHERE, targets[point])
    return jnp.concatenate(targets, axis=0), jnp.concatenate(weights, axis=0)


def spread_matrix(targets, weights, first_column, rows=BCOLS):
    row = lax.broadcasted_iota(jnp.int32, (rows, targets.shape[1]), 0) + first_column
    total = jnp.zeros(row.shape, F32)
    for point in range(POINTS):
        total = jnp.where(row == targets[point : point + 1], weights[point : point + 1], total)
    return split(total)


def product(left, right, dims):
    return lax.dot_general(left, right, (dims, ((), ())), preferred_element_type=F32)


def diffuse(inverse, field, out, cols):
    variables = field.shape[1]
    wide = split(jnp.concatenate([field[:, v, :] for v in range(variables)], axis=1))
    turned = split(inverse.T)
    dims = ((1,), (0,))
    result = product(turned[0], wide[0], dims) + (
        product(turned[0], wide[1], dims) + product(turned[1], wide[0], dims)
    )
    for v in range(variables):
        out[:, v, cols] = result[:, v * BCOLS : (v + 1) * BCOLS]


def rows_of(value):
    return value.reshape(value.shape[0] * value.shape[1], value.shape[2])


def spread(diffused, matrix):
    levels, variables, _ = diffused.shape
    high, low = split(rows_of(diffused))
    left = jnp.concatenate([high, low, high], axis=1)
    right = jnp.concatenate([matrix[0], matrix[0], matrix[1]], axis=1)
    sums = product(left, right, ((1,), (1,)))
    return sums.reshape(levels, variables, sums.shape[1])


def side_matrix(targets, weights, step, blocks, first_columns):
    parts = []
    for block in blocks:
        cols = lanes(block)
        halves = [spread_matrix(targets[step, :, cols], weights[step, :, cols], column) for column in first_columns]
        parts.append([jnp.concatenate(half, axis=0) for half in zip(*halves)])
    return [jnp.concatenate(part, axis=1) for part in zip(*parts)]


def call(kernel, operands, in_specs, outs, out_specs, scratch, flops, name, limit=VMEM_LIMIT):
    return pl.pallas_call(
        kernel,
        out_shape=outs,
        in_specs=in_specs,
        out_specs=out_specs,
        scratch_shapes=scratch,
        compiler_params=pltpu.CompilerParams(vmem_limit_bytes=limit),
        cost_estimate=pl.CostEstimate(flops=flops, bytes_accessed=1_000_000, transcendentals=0),
        name=name,
    )(*operands)


def start_copies(sems, pairs):
    copies = [pltpu.make_async_copy(source, target, sems.at[i]) for i, (source, target) in enumerate(pairs)]
    for copy in copies:
        copy.start()
    return copies


def first_kernel(
    step, all_blocks, fields, inverses, routes, points, weights,
    to_near, to_far, to_core, diffused, targets, merged, field, inverse, route, point, weight, tall, sems,
):
    block_count = inverses.shape[2]
    near, far, target_near, target_far = z_blocks(block_count)
    first, first_target = core_side(block_count)
    copies = start_copies(
        sems,
        [
            (routes, route),
            (points, point),
            (weights, weight),
            (inverses.at[step], inverse),
            (fields, field),
        ],
    )
    for copy in copies[:3]:
        copy.wait()
    for number in range(STEPS):
        for j in range(block_count):
            cols = slice(j * BCOLS, (j + 1) * BCOLS)
            found = target_columns(point[number, :, cols], route, number, j, block_count, all_blocks)
            targets[number, :, cols], merged[number, :, cols] = merge_points(found, weight[number, :, cols])
    z_matrix = side_matrix(targets, merged, step, (near, far), (target_near * BCOLS, target_far * BCOLS))
    core_columns = (first_target * BCOLS, (first_target + 1) * BCOLS)
    core_matrix = side_matrix(targets, merged, step, (first, first + 1), core_columns)
    for copy in copies[3:]:
        copy.wait()
    for j in range(block_count):
        cols = slice(j * BCOLS, (j + 1) * BCOLS)
        diffuse(inverse[:, j, :], field.at[:, :, cols], diffused, cols)
    tall[:, :, :BCOLS] = diffused[:, :, lanes(near)]
    tall[:, :, BCOLS:] = diffused[:, :, lanes(far)]
    sums = spread(tall[...], z_matrix)
    to_near[...] = sums[:, :, :BCOLS]
    to_far[...] = sums[:, :, BCOLS:]
    to_core[...] = spread(diffused[:, :, lanes(first, REACH)], core_matrix)


def shape(like, columns):
    return jax.ShapeDtypeStruct((like.shape[0], like.shape[1], columns), F32)


def first(step, all_blocks, fields, inverses, routes, points, weights):
    one, two, whole = (shape(fields, n) for n in (BCOLS, REACH * BCOLS, fields.shape[2]))
    return call(
        functools.partial(first_kernel, step, all_blocks),
        (fields, inverses, routes, points, weights),
        [HBM] * 5,
        (
            one,
            one,
            two,
            whole,
            jax.ShapeDtypeStruct(points.shape, jnp.int32),
            jax.ShapeDtypeStruct(weights.shape, F32),
        ),
        (VMEM,) * 6,
        [
            pltpu.VMEM(fields.shape, F32),
            pltpu.VMEM(inverses.shape[1:], F32),
            pltpu.SMEM(routes.shape, jnp.int32),
            pltpu.VMEM(points.shape, jnp.int32),
            pltpu.VMEM(weights.shape, F32),
            pltpu.VMEM(two.shape, F32),
            pltpu.SemaphoreType.DMA((5,)),
        ],
        400_000_000,
        f"first_step{step}",
    )


def inner_kernel(
    step, diffused, targets, weights, core_in, inverses, own, inverse, to_core, diffused_core, sems
):
    block_count = inverses.shape[2]
    side_first, first_target = core_side(block_count)
    (copy,) = start_copies(sems, [(inverses.at[step - 1], inverse)])
    matrix = spread_matrix(targets[step], weights[step], 0, own.shape[2])
    own[...] = spread(diffused[...], matrix)
    side = lanes(side_first, REACH)
    own[:, :, side] += core_in[...]
    columns = (first_target * BCOLS, (first_target + 1) * BCOLS)
    matrix = side_matrix(targets, weights, step - 1, (side_first, side_first + 1), columns)
    copy.wait()
    for j in range(REACH):
        cols = slice(j * BCOLS, (j + 1) * BCOLS)
        diffuse(inverse[:, side_first + j, :], own.at[:, :, lanes(side_first + j)], diffused_core, cols)
    to_core[...] = spread(diffused_core[...], matrix)


def inner(step, diffused, targets, weights, core_in, inverses):
    two = shape(diffused, REACH * BCOLS)
    return call(
        functools.partial(inner_kernel, step),
        (diffused, targets, weights, core_in, inverses),
        [VMEM] * 4 + [HBM],
        (shape(diffused, diffused.shape[2]), jax.ShapeDtypeStruct(inverses.shape[1:], F32), two, two),
        (VMEM,) * 4,
        [pltpu.SemaphoreType.DMA((1,))],
        2_000_000_000,
        f"inner_step{step}",
    )


def near_kernel(step, own, near_in, inverse, targets, weights, to_far, to_near, diffused, field):
    block_count = inverse.shape[1]
    near, _, target_near, target_far = z_blocks(block_count)
    cols = lanes(near)
    field[...] = own[:, :, cols] + near_in[...]
    diffuse(inverse[:, near, :], field, diffused, slice(0, BCOLS))
    halves = [
        spread_matrix(targets[step, :, cols], weights[step, :, cols], target * BCOLS)
        for target in (target_far, target_near)
    ]
    sums = spread(diffused[...], [jnp.concatenate(half, axis=0) for half in zip(*halves)])
    to_far[...] = sums[:, :, :BCOLS]
    to_near[...] = sums[:, :, BCOLS:]


def near(step, own, near_in, inverse, targets, weights):
    one = shape(own, BCOLS)
    return call(
        functools.partial(near_kernel, step),
        (own, near_in, inverse, targets, weights),
        [VMEM] * 5,
        (one, one, one),
        (VMEM,) * 3,
        [pltpu.VMEM(one.shape, F32)],
        300_000_000,
        f"near_step{step}",
    )


def far_kernel(step, own, far_in, partial, inverse, targets, weights, to_near, diffused, field):
    block_count = inverse.shape[1]
    _, far, target_near, _ = z_blocks(block_count)
    cols = lanes(far)
    field[...] = own[:, :, cols] + far_in[...]
    diffuse(inverse[:, far, :], field, diffused, slice(0, BCOLS))
    matrix = spread_matrix(targets[step, :, cols], weights[step, :, cols], target_near * BCOLS)
    to_near[...] = partial[...] + spread(diffused[...], matrix)


def far(step, own, far_in, partial, inverse, targets, weights):
    one = shape(own, BCOLS)
    return call(
        functools.partial(far_kernel, step),
        (own, far_in, partial, inverse, targets, weights),
        [VMEM] * 6,
        (one, one),
        (VMEM,) * 2,
        [pltpu.VMEM(one.shape, F32)],
        300_000_000,
        f"far_step{step}",
    )


def outer_kernel(
    step, own, near_in, far_in, diffused_core, diffused_near, diffused_far, targets, weights,
    sums, mid, field, tall, sems,
):
    block_count = own.shape[2] // BCOLS
    near, far, _, _ = z_blocks(block_count)
    side = lanes(core_side(block_count)[0], REACH)
    field[:, :, side] = own[:, :, side]
    field[:, :, lanes(near)] = own[:, :, lanes(near)] + near_in[...]
    field[:, :, lanes(far)] = own[:, :, lanes(far)] + far_in[...]
    (copy,) = start_copies(sems, [(field, mid)])
    tall[:, :, side] = diffused_core[...]
    tall[:, :, lanes(near)] = diffused_near[...]
    tall[:, :, lanes(far)] = diffused_far[...]
    sums[...] = spread(tall[...], spread_matrix(targets[step], weights[step], 0, own.shape[2]))
    copy.wait()


def outer(step, own, near_in, far_in, diffused, targets, weights):
    whole = shape(own, own.shape[2])
    return call(
        functools.partial(outer_kernel, step),
        (own, near_in, far_in, *diffused, targets, weights),
        [VMEM] * 8,
        (whole, whole),
        (VMEM, HBM),
        [pltpu.VMEM(own.shape, F32), pltpu.VMEM(own.shape, F32), pltpu.SemaphoreType.DMA((1,))],
        2_000_000_000,
        f"outer_step{step}",
    )


def squares(value):
    return jnp.sum(rows_of(value * value), axis=0, keepdims=True)


def most_kernel(own, core_in, far_in, start, lane_sums):
    block_count = own.shape[2] // BCOLS
    near, far, _, _ = z_blocks(block_count)
    side = lanes(core_side(block_count)[0], REACH)
    core = own[:, :, side] + core_in[...]
    behind = own[:, :, lanes(far)] + far_in[...]
    start[:, :, side] = core
    start[:, :, lanes(far)] = behind
    start[:, :, lanes(near)] = own[:, :, lanes(near)]
    core = squares(core)
    lane_sums[...] = core[:, :BCOLS] + core[:, BCOLS:] + squares(behind)


def most(own, core_in, far_in):
    return call(
        most_kernel,
        (own, core_in, far_in),
        [VMEM] * 3,
        (jax.ShapeDtypeStruct(own.shape, F32), jax.ShapeDtypeStruct((1, BCOLS), F32)),
        (VMEM, VMEM),
        [],
        1_000_000,
        "squares_of_most_blocks",
    )


def last_kernel(start, near_in, lane_sums, shares):
    near = z_blocks(start.shape[2] // BCOLS)[0]
    sums = lane_sums[...] + squares(start[:, :, lanes(near)] + near_in[...])
    shares[...] = jnp.broadcast_to(sums, shares.shape)


def last(count, start, near_in, lane_sums):
    return call(
        last_kernel,
        (start, near_in, lane_sums),
        [VMEM] * 3,
        jax.ShapeDtypeStruct((count, BCOLS), F32),
        VMEM,
        [],
        1_000_000,
        "squares_of_last_block",
    )


def scale_kernel(cells, start, near_in, shares, out, held, sems):
    block_count = start.shape[2] // BCOLS
    near = z_blocks(block_count)[0]
    energy = jnp.sum(shares[...]) / cells
    root = jnp.sqrt(jnp.full((1, 1, 1), energy + eps_energy, F32))
    copies = []
    for j in range(block_count):
        cols = slice(j * BCOLS, (j + 1) * BCOLS)
        held[:, :, cols] = (start[:, :, cols] + jnp.where(near == j, near_in[...], 0.0)) / root
        copies.append(pltpu.make_async_copy(held.at[:, :, cols], out.at[:, :, cols], sems.at[j]))
        copies[-1].start()
    for copy in copies:
        copy.wait()


def scale(start, near_in, shares, cells):
    return call(
        functools.partial(scale_kernel, cells),
        (start, near_in, shares),
        [VMEM] * 3,
        jax.ShapeDtypeStruct(start.shape, F32),
        HBM,
        [pltpu.VMEM(start.shape, F32), pltpu.SemaphoreType.DMA((start.shape[2] // BCOLS,))],
        1_000_000,
        "scale_start",
    )


def core_exchange(value):
    count = lax.axis_size("col")
    return lax.ppermute(value, "col", [(i, i ^ 1) for i in range(count)])


def z_exchange(value):
    count = lax.axis_size("col")
    pairs = [(i, (i + 1) % count if i % 2 else (i - 1) % count) for i in range(count)]
    return lax.ppermute(value, "col", pairs)


def shards(adj_final, inverses, dep_lists, dep_points, weights):
    count = lax.axis_size("col")
    all_blocks = count * inverses.shape[1]
    fields = jnp.transpose(adj_final, (1, 0, 2))
    inverses = jnp.transpose(inverses, (0, 2, 1, 3))
    fields, inverses, dep_lists, dep_points, weights = (
        pltpu.with_memory_space_constraint(value, pltpu.HBM)
        for value in (fields, inverses, dep_lists, dep_points, weights)
    )

    to_near, to_far, to_core, diffused, targets, merged = first(
        1, all_blocks, fields, inverses, dep_lists, dep_points, weights
    )
    near_in = z_exchange(to_near)
    far_in = z_exchange(to_far)
    own, inverse, to_core, diffused_core = inner(1, diffused, targets, merged, core_exchange(to_core), inverses)

    next_core_in = core_exchange(to_core)
    to_far, partial, diffused_near = near(0, own, near_in, inverse, targets, merged)
    next_far_in = z_exchange(to_far)
    to_near, diffused_far = far(0, own, far_in, partial, inverse, targets, merged)
    next_near_in = z_exchange(to_near)
    own, mid = outer(
        0, own, near_in, far_in, (diffused_core, diffused_near, diffused_far), targets, merged
    )

    start, lane_sums = most(own, next_core_in, next_far_in)
    shares = last(count, start, next_near_in, lane_sums)
    shares = lax.all_to_all(shares, "col", 0, 0, tiled=True)
    lanczos = scale(start, next_near_in, shares, adj_final.size * count)
    return jnp.transpose(mid, (1, 0, 2)), jnp.transpose(lanczos, (1, 0, 2))


def solution(mesh):
    in_specs = (
        P("mem", None, "col"),
        P("mem", "col", None, None),
        P("mem", "col", None),
        P("mem", None, "col"),
        P("mem", None, "col"),
    )
    out_specs = (P("mem", None, "col"), P("mem", None, "col"))
    return jax.shard_map(shards, mesh=mesh, in_specs=in_specs, out_specs=out_specs, check_vma=False)
```

time: 63.8 us -> 45.3 us (0.71)
  waiting for transfers between devices: 23.5 us -> 9.56 us
  local copies, waits for them, and re-layouts: 4.64 us -> 0 us
  starting transfers between devices: 8.94 us -> 12.9 us
  Pallas kernels: 17.4 us -> 13.5 us
    ppermute x4, waiting for transfers between devices: 23.5 us -> 9.55 us  [z_exchange(): return lax.ppermute(value, 'col', pairs)]
    unnamed x18 -> x0, local copies, waits for them, and re-layouts: 4.64 us -> none
    ppermute x4, starting transfers between devices: 8.35 us -> 12.3 us  [z_exchange(): return lax.ppermute(value, 'col', pairs)]
    pallas_call x8, Pallas kernels: 17.4 us -> 13.5 us  [call(): pl.pallas_call(kernel, out_shape=outs, in_specs=in_specs, out_specs=out_s...]
  transfers between devices with their start and end apart: 6 -> 6, of which waited for: 4 -> 3; matrix products, arithmetic and copies ran while one was open for 0% -> 0% of each run, Pallas kernels for 5% -> 18%
where the time goes in v4:
time: 45.3 us; the launch traced here: 45.1 us
  Pallas kernels  13.5 us (30%)
  starting transfers between devices  12.9 us (28%)
  waiting for transfers between devices  9.56 us (21%)
  blocking collectives  8.43 us (19%)
  between operations  0.7 us (2%)
    pallas_call x8, Pallas kernels, call(): pl.pallas_call(kernel, out_shape=outs, in_specs=in_specs, out_specs=out_s...  13.5 us
    ppermute x4, starting transfers between devices, z_exchange(): return lax.ppermute(value, 'col', pairs)  12.3 us
    ppermute x4, waiting for transfers between devices, z_exchange(): return lax.ppermute(value, 'col', pairs)  9.55 us
    all_to_all x1, blocking collectives, shards(): shares = lax.all_to_all(shares, 'col', 0, 0, tiled=True)  8.43 us
  transfers between devices with their start and end apart: 6, of which 3 were waited for; matrix products, arithmetic and copies ran while one was open for 0% of the time, Pallas kernels for 18%

profile of v4, /device:TPU:0, one launch (start us, length us, event | category | flops | bytes accessed | tf_op | source)
XLA Modules:
  0.0 45.1 jit_solution(9476908700416682530)
XLA Ops:
  0.6 4.2 %first_step1.1 = (f32[137,4,128]{2,1,0:T(4,128)S(1)}, f32[137,4,128]{2,1,0:T(4,128)S(1)}, f32[137,4,256]{2,1,0:T(4,128)S(1)}, f32[137,4,512]{2,1,0:T(4,128)S(1)}...) custom-call(f32[137,4,512]{2,1,0:T(4,128)} %bitcast.10, f32[2,137,4,137]{3,2,1,0:T(4,128)} %bitcast.11, ...), custom_call_target="tpu_custom_call" | custom-call | flops 400000000 | bytes 1000000 | tf_op jit(solution)/shard_map/first_step1/pallas_call | solution.py:115
  4.8 0.5 %collective-permute-start = (f32[137,4,256]{2,1,0:T(4,128)S(1)}, f32[137,4,256]{2,1,0:T(4,128)S(1)}, u32[]{:S(2)}, u32[]{:S(2)}) collective-permute-start(f32[137,4,256]{2,1,0:T(4,128)S(1)} %get-tuple-element.24), channel_id=1, source_target_pairs={{0,1},{1,0},{2,3},{3,2},{4,5},{5,4},{6,7},{7,6},{8,9},{9,8},{10,11... | collective-permute-start | bytes 1683464 | tf_op jit(solution)/shard_map/ppermute | solution.py:404
  5.3 4.7 %collective-permute-start.1 = (f32[137,4,128]{2,1,0:T(4,128)S(1)}, f32[137,4,128]{2,1,0:T(4,128)S(1)}, u32[]{:S(2)}, u32[]{:S(2)}) collective-permute-start(f32[137,4,128]{2,1,0:T(4,128)S(1)} %get-tuple-element.26), channel_id=1, source_target_pairs={{0,7},{1,2},{2,1},{3,4},{4,3},{5,6},{6,5},{7,0},{8,15},{9,10},{10,... | collective-permute-start | bytes 841736 | tf_op jit(solution)/shard_map/ppermute | solution.py:410
  10.0 0.0 collective-permute-start.2
  10.1 0.0 collective-permute-done.core_in
  10.1 3.3 %inner_step1.1 = (f32[137,4,512]{2,1,0:T(4,128)S(1)}, f32[137,4,137]{2,1,0:T(4,128)S(1)}, f32[137,4,256]{2,1,0:T(4,128)S(1)}, f32[137,4,256]{2,1,0:T(4,128)S(1)}) custom-call(f32[137,4,512]{2,1,0:T(4,128)S(1)} %get-tuple-element.21.diffused, s32[2,4,512]{2,1,0:T(4,128)S(1)} %get-tuple-element.22.targets, f32[2,4,512]{2,1,0:T(4,128)S(1)} %get-tuple-element.23.weights, ...), custom_call_target="tpu_custom_call" | custom-call | flops 2000000000 | bytes 1000000 | tf_op jit(solution)/shard_map/inner_step1/pallas_call | solution.py:115
  13.3 0.1 collective-permute-start.3
  13.4 3.8 %collective-permute-done.1.near_in = f32[137,4,128]{2,1,0:T(4,128)S(1)} collective-permute-done((f32[137,4,128]{2,1,0:T(4,128)S(1)}, f32[137,4,128]{2,1,0:T(4,128)S(1)}, u32[]{:S(2)}, u32[]{:S(2)}) %collective-permute-start.1) | collective-permute-done | bytes 280608 | tf_op jit(solution)/shard_map/ppermute | solution.py:410
  17.2 0.9 %near_step0.1 = (f32[137,4,128]{2,1,0:T(4,128)S(1)}, f32[137,4,128]{2,1,0:T(4,128)S(1)}, f32[137,4,128]{2,1,0:T(4,128)S(1)}) custom-call(f32[137,4,512]{2,1,0:T(4,128)S(1)} %get-tuple-element.25.own, f32[137,4,128]{2,1,0:T(4,128)S(1)} %collective-permute-done.1.near_in, f32[137,4,137]{2,1,0:T(4,128)S(1)} %get-tuple-element.29.inverse, ...), custom_call_target="tpu_custom_call" | custom-call | flops 300000000 | bytes 1000000 | tf_op jit(solution)/shard_map/near_step0/pallas_call | solution.py:115
  18.1 3.8 %collective-permute-start.4 = (f32[137,4,128]{2,1,0:T(4,128)S(1)}, f32[137,4,128]{2,1,0:T(4,128)S(1)}, u32[]{:S(2)}, u32[]{:S(2)}) collective-permute-start(f32[137,4,128]{2,1,0:T(4,128)S(1)} %get-tuple-element.36), channel_id=1, source_target_pairs={{0,7},{1,2},{2,1},{3,4},{4,3},{5,6},{6,5},{7,0},{8,15},{9,10},{10,... | collective-permute-start | bytes 841736 | tf_op jit(solution)/shard_map/ppermute | solution.py:410
  21.9 1.3 %collective-permute-done.2.far_in = f32[137,4,128]{2,1,0:T(4,128)S(1)} collective-permute-done((f32[137,4,128]{2,1,0:T(4,128)S(1)}, f32[137,4,128]{2,1,0:T(4,128)S(1)}, u32[]{:S(2)}, u32[]{:S(2)}) %collective-permute-start.2) | collective-permute-done | bytes 280608 | tf_op jit(solution)/shard_map/ppermute | solution.py:410
  23.2 0.9 %far_step0.1 = (f32[137,4,128]{2,1,0:T(4,128)S(1)}, f32[137,4,128]{2,1,0:T(4,128)S(1)}) custom-call(f32[137,4,512]{2,1,0:T(4,128)S(1)} %get-tuple-element.25.own, f32[137,4,128]{2,1,0:T(4,128)S(1)} %collective-permute-done.2.far_in, f32[137,4,128]{2,1,0:T(4,128)S(1)} %get-tuple-element.31.partial, f32[137,4,137]{2,1,0:T(4,128)S(1)} %get-tuple-element.29.inverse, ...), custom_call_target="tpu_custom_call" | custom-call | flops 300000000 | bytes 1000000 | tf_op jit(solution)/shard_map/far_step0/pallas_call | solution.py:115
  24.1 3.8 %collective-permute-start.5 = (f32[137,4,128]{2,1,0:T(4,128)S(1)}, f32[137,4,128]{2,1,0:T(4,128)S(1)}, u32[]{:S(2)}, u32[]{:S(2)}) collective-permute-start(f32[137,4,128]{2,1,0:T(4,128)S(1)} %get-tuple-element.38), channel_id=1, source_target_pairs={{0,7},{1,2},{2,1},{3,4},{4,3},{5,6},{6,5},{7,0},{8,15},{9,10},{10,... | collective-permute-start | bytes 841736 | tf_op jit(solution)/shard_map/ppermute | solution.py:410
  27.9 2.5 %outer_step0.1 = (f32[137,4,512]{2,1,0:T(4,128)S(1)}, f32[137,4,512]{2,1,0:T(4,128)}) custom-call(f32[137,4,512]{2,1,0:T(4,128)S(1)} %get-tuple-element.25.own, f32[137,4,128]{2,1,0:T(4,128)S(1)} %collective-permute-done.1.near_in, f32[137,4,128]{2,1,0:T(4,128)S(1)} %collective-permute-done.2.far_in, f32[137,4,256]{2,1,0:T(4,128)S(1)} %get-tuple-element.28.diffused_core, ...), custom_call_target="tpu_custom_call" | custom-call | flops 2000000000 | bytes 1000000 | tf_op jit(solution)/shard_map/outer_step0/pallas_call | solution.py:115
  30.4 0.0 collective-permute-done.4.far_in
  30.4 0.0 collective-permute-done.3.core_in
  30.4 0.3 squares_of_most_blocks.1
  30.7 4.5 %collective-permute-done.5.near_in = f32[137,4,128]{2,1,0:T(4,128)S(1)} collective-permute-done((f32[137,4,128]{2,1,0:T(4,128)S(1)}, f32[137,4,128]{2,1,0:T(4,128)S(1)}, u32[]{:S(2)}, u32[]{:S(2)}) %collective-permute-start.5) | collective-permute-done | bytes 280608 | tf_op jit(solution)/shard_map/ppermute | solution.py:410
  35.2 0.1 squares_of_last_block.1
  35.3 8.4 %all_to_all.11 = f32[8,1,128]{2,1,0:T(1,128)S(1)} all-to-all(f32[8,1,128]{2,1,0:T(1,128)S(1)} %bitcast.9), channel_id=1, replica_groups=mesh['mem'=4,'col'=8] {'col'}, dimensions={0} | all-to-all | bytes 8192 | tf_op jit(solution)/shard_map/all_to_all | solution.py:441
  43.7 1.4 %scale_start.1 = f32[137,4,512]{2,1,0:T(4,128)} custom-call(f32[137,4,512]{2,1,0:T(4,128)S(1)} %get-tuple-element.37.start, f32[137,4,128]{2,1,0:T(4,128)S(1)} %collective-permute-done.5.near_in, f32[8,128]{1,0:T(8,128)S(1)} %bitcast.8), custom_call_target="tpu_custom_call" | custom-call | flops 1000000 | bytes 1000000 | tf_op jit(solution)/shard_map/scale_start/pallas_call | solution.py:115
Async XLA Ops:
  4.8 5.3 %collective-permute-start = (f32[137,4,256]{2,1,0:T(4,128)S(1)}, f32[137,4,256]{2,1,0:T(4,128)S(1)}, u32[]{:S(2)}, u32[]{:S(2)}) collective-permute-start(f32[137,4,256]{2,1,0:T(4,128)S(1)} %get-tuple-element.24), channel_id=1, source_target_pairs={{0,1},{1,0},{2,3},{3,2},{4,5},{5,4},{6,7},{7,6},{8,9},{9,8},{10,11... | collective-permute-start | bytes 1683464 | tf_op jit(solution)/shard_map/ppermute | solution.py:404
  5.3 11.8 %collective-permute-start.1 = (f32[137,4,128]{2,1,0:T(4,128)S(1)}, f32[137,4,128]{2,1,0:T(4,128)S(1)}, u32[]{:S(2)}, u32[]{:S(2)}) collective-permute-start(f32[137,4,128]{2,1,0:T(4,128)S(1)} %get-tuple-element.26), channel_id=1, source_target_pairs={{0,7},{1,2},{2,1},{3,4},{4,3},{5,6},{6,5},{7,0},{8,15},{9,10},{10,... | collective-permute-start | bytes 841736 | tf_op jit(solution)/shard_map/ppermute | solution.py:410
  10.0 13.2 %collective-permute-start.2 = (f32[137,4,128]{2,1,0:T(4,128)S(1)}, f32[137,4,128]{2,1,0:T(4,128)S(1)}, u32[]{:S(2)}, u32[]{:S(2)}) collective-permute-start(f32[137,4,128]{2,1,0:T(4,128)S(1)} %get-tuple-element.27), channel_id=1, source_target_pairs={{0,7},{1,2},{2,1},{3,4},{4,3},{5,6},{6,5},{7,0},{8,15},{9,10},{10,... | collective-permute-start | bytes 841736 | tf_op jit(solution)/shard_map/ppermute | solution.py:410
  13.3 17.1 %collective-permute-start.3 = (f32[137,4,256]{2,1,0:T(4,128)S(1)}, f32[137,4,256]{2,1,0:T(4,128)S(1)}, u32[]{:S(2)}, u32[]{:S(2)}) collective-permute-start(f32[137,4,256]{2,1,0:T(4,128)S(1)} %get-tuple-element.35), channel_id=1, source_target_pairs={{0,1},{1,0},{2,3},{3,2},{4,5},{5,4},{6,7},{7,6},{8,9},{9,8},{10,11... | collective-permute-start | bytes 1683464 | tf_op jit(solution)/shard_map/ppermute | solution.py:404
  18.1 12.3 %collective-permute-start.4 = (f32[137,4,128]{2,1,0:T(4,128)S(1)}, f32[137,4,128]{2,1,0:T(4,128)S(1)}, u32[]{:S(2)}, u32[]{:S(2)}) collective-permute-start(f32[137,4,128]{2,1,0:T(4,128)S(1)} %get-tuple-element.36), channel_id=1, source_target_pairs={{0,7},{1,2},{2,1},{3,4},{4,3},{5,6},{6,5},{7,0},{8,15},{9,10},{10,... | collective-permute-start | bytes 841736 | tf_op jit(solution)/shard_map/ppermute | solution.py:410
  24.1 11.1 %collective-permute-start.5 = (f32[137,4,128]{2,1,0:T(4,128)S(1)}, f32[137,4,128]{2,1,0:T(4,128)S(1)}, u32[]{:S(2)}, u32[]{:S(2)}) collective-permute-start(f32[137,4,128]{2,1,0:T(4,128)S(1)} %get-tuple-element.38), channel_id=1, source_target_pairs={{0,7},{1,2},{2,1},{3,4},{4,3},{5,6},{6,5},{7,0},{8,15},{9,10},{10,... | collective-permute-start | bytes 841736 | tf_op jit(solution)/shard_map/ppermute | solution.py:410

commit v5 on v4

--- a/solution.py
+++ b/solution.py
@@ -77,29 +77,30 @@
     return lax.dot_general(left, right, (dims, ((), ())), preferred_element_type=F32)
 
 
-def diffuse(inverse, field, out, cols):
-    variables = field.shape[1]
-    wide = split(jnp.concatenate([field[:, v, :] for v in range(variables)], axis=1))
+def rows_of(ref):
+    levels, variables, columns = ref.shape
+    return ref.reshape(levels * variables, columns)
+
+
+def diffuse(inverse, field, out):
+    levels, variables, columns = field.shape
+    source, result = rows_of(field), rows_of(out)
+    every = [pl.ds(v, levels, stride=variables) for v in range(variables)]
+    wide = split(jnp.concatenate([source[rows, :] for rows in every], axis=1))
     turned = split(inverse.T)
     dims = ((1,), (0,))
-    result = product(turned[0], wide[0], dims) + (
+    total = product(turned[0], wide[0], dims) + (
         product(turned[0], wide[1], dims) + product(turned[1], wide[0], dims)
     )
-    for v in range(variables):
-        out[:, v, cols] = result[:, v * BCOLS : (v + 1) * BCOLS]
-
-
-def rows_of(value):
-    return value.reshape(value.shape[0] * value.shape[1], value.shape[2])
+    for v, rows in enumerate(every):
+        result[rows, :] = total[:, v * columns : (v + 1) * columns]
 
 
 def spread(diffused, matrix):
-    levels, variables, _ = diffused.shape
-    high, low = split(rows_of(diffused))
+    high, low = split(jnp.concatenate([rows_of(block)[...] for block in diffused], axis=1))
     left = jnp.concatenate([high, low, high], axis=1)
     right = jnp.concatenate([matrix[0], matrix[0], matrix[1]], axis=1)
-    sums = product(left, right, ((1,), (1,)))
-    return sums.reshape(levels, variables, sums.shape[1])
+    return product(left, right, ((1,), (1,)))
 
 
 def side_matrix(targets, weights, step, blocks, first_columns):
@@ -133,7 +134,7 @@
 
 def first_kernel(
     step, all_blocks, fields, inverses, routes, points, weights,
-    to_near, to_far, to_core, diffused, targets, merged, field, inverse, route, point, weight, tall, sems,
+    to_near, to_far, to_core, diffused, targets, merged, field, inverse, route, point, weight, sems,
 ):
     block_count = inverses.shape[2]
     near, far, target_near, target_far = z_blocks(block_count)
@@ -145,8 +146,8 @@
             (points, point),
             (weights, weight),
             (inverses.at[step], inverse),
-            (fields, field),
-        ],
+        ]
+        + [(fields.at[:, :, lanes(j)], field.at[j]) for j in range(block_count)],
     )
     for copy in copies[:3]:
         copy.wait()
@@ -158,25 +159,24 @@
     z_matrix = side_matrix(targets, merged, step, (near, far), (target_near * BCOLS, target_far * BCOLS))
     core_columns = (first_target * BCOLS, (first_target + 1) * BCOLS)
     core_matrix = side_matrix(targets, merged, step, (first, first + 1), core_columns)
-    for copy in copies[3:]:
-        copy.wait()
+    copies[3].wait()
     for j in range(block_count):
-        cols = slice(j * BCOLS, (j + 1) * BCOLS)
-        diffuse(inverse[:, j, :], field.at[:, :, cols], diffused, cols)
-    tall[:, :, :BCOLS] = diffused[:, :, lanes(near)]
-    tall[:, :, BCOLS:] = diffused[:, :, lanes(far)]
-    sums = spread(tall[...], z_matrix)
-    to_near[...] = sums[:, :, :BCOLS]
-    to_far[...] = sums[:, :, BCOLS:]
-    to_core[...] = spread(diffused[:, :, lanes(first, REACH)], core_matrix)
-
-
-def shape(like, columns):
-    return jax.ShapeDtypeStruct((like.shape[0], like.shape[1], columns), F32)
+        copies[4 + j].wait()
+        diffuse(inverse[:, j, :], field.at[j], diffused.at[j])
+    sums = spread([diffused.at[near], diffused.at[far]], z_matrix)
+    rows_of(to_near)[...] = sums[:, :BCOLS]
+    rows_of(to_far)[...] = sums[:, BCOLS:]
+    sums = spread([diffused.at[first], diffused.at[first + 1]], core_matrix)
+    for j in range(REACH):
+        rows_of(to_core.at[j])[...] = sums[:, j * BCOLS : (j + 1) * BCOLS]
+
+
+def blocks(like, *count):
+    return jax.ShapeDtypeStruct((*count, *like.shape[-3:-1], BCOLS), F32)
 
 
 def first(step, all_blocks, fields, inverses, routes, points, weights):
-    one, two, whole = (shape(fields, n) for n in (BCOLS, REACH * BCOLS, fields.shape[2]))
+    one, two, whole = blocks(fields), blocks(fields, REACH), blocks(fields, inverses.shape[2])
     return call(
         functools.partial(first_kernel, step, all_blocks),
         (fields, inverses, routes, points, weights),
@@ -191,13 +191,12 @@
         ),
         (VMEM,) * 6,
         [
-            pltpu.VMEM(fields.shape, F32),
+            pltpu.VMEM(whole.shape, F32),
             pltpu.VMEM(inverses.shape[1:], F32),
             pltpu.SMEM(routes.shape, jnp.int32),
             pltpu.VMEM(points.shape, jnp.int32),
             pltpu.VMEM(weights.shape, F32),
-            pltpu.VMEM(two.shape, F32),
-            pltpu.SemaphoreType.DMA((5,)),
+            pltpu.SemaphoreType.DMA((4 + inverses.shape[2],)),
         ],
         400_000_000,
         f"first_step{step}",
@@ -210,26 +209,29 @@
     block_count = inverses.shape[2]
     side_first, first_target = core_side(block_count)
     (copy,) = start_copies(sems, [(inverses.at[step - 1], inverse)])
-    matrix = spread_matrix(targets[step], weights[step], 0, own.shape[2])
-    own[...] = spread(diffused[...], matrix)
-    side = lanes(side_first, REACH)
-    own[:, :, side] += core_in[...]
+    matrix = spread_matrix(targets[step], weights[step], 0, block_count * BCOLS)
+    sums = spread([diffused.at[j] for j in range(block_count)], matrix)
+    for j in range(block_count):
+        rows_of(own.at[j])[...] = sums[:, j * BCOLS : (j + 1) * BCOLS]
+    for j in range(REACH):
+        own[side_first + j] += core_in[j]
     columns = (first_target * BCOLS, (first_target + 1) * BCOLS)
     matrix = side_matrix(targets, weights, step - 1, (side_first, side_first + 1), columns)
     copy.wait()
     for j in range(REACH):
-        cols = slice(j * BCOLS, (j + 1) * BCOLS)
-        diffuse(inverse[:, side_first + j, :], own.at[:, :, lanes(side_first + j)], diffused_core, cols)
-    to_core[...] = spread(diffused_core[...], matrix)
+        diffuse(inverse[:, side_first + j, :], own.at[side_first + j], diffused_core.at[j])
+    sums = spread([diffused_core.at[j] for j in range(REACH)], matrix)
+    for j in range(REACH):
+        rows_of(to_core.at[j])[...] = sums[:, j * BCOLS : (j + 1) * BCOLS]
 
 
 def inner(step, diffused, targets, weights, core_in, inverses):
-    two = shape(diffused, REACH * BCOLS)
+    two = blocks(diffused, REACH)
     return call(
         functools.partial(inner_kernel, step),
         (diffused, targets, weights, core_in, inverses),
         [VMEM] * 4 + [HBM],
-        (shape(diffused, diffused.shape[2]), jax.ShapeDtypeStruct(inverses.shape[1:], F32), two, two),
+        (blocks(diffused, diffused.shape[0]), jax.ShapeDtypeStruct(inverses.shape[1:], F32), two, two),
         (VMEM,) * 4,
         [pltpu.SemaphoreType.DMA((1,))],
         2_000_000_000,
@@ -241,19 +243,19 @@
     block_count = inverse.shape[1]
     near, _, target_near, target_far = z_blocks(block_count)
     cols = lanes(near)
-    field[...] = own[:, :, cols] + near_in[...]
-    diffuse(inverse[:, near, :], field, diffused, slice(0, BCOLS))
+    field[...] = own[near] + near_in[...]
+    diffuse(inverse[:, near, :], field, diffused)
     halves = [
         spread_matrix(targets[step, :, cols], weights[step, :, cols], target * BCOLS)
         for target in (target_far, target_near)
     ]
-    sums = spread(diffused[...], [jnp.concatenate(half, axis=0) for half in zip(*halves)])
-    to_far[...] = sums[:, :, :BCOLS]
-    to_near[...] = sums[:, :, BCOLS:]
+    sums = spread([diffused], [jnp.concatenate(half, axis=0) for half in zip(*halves)])
+    rows_of(to_far)[...] = sums[:, :BCOLS]
+    rows_of(to_near)[...] = sums[:, BCOLS:]
 
 
 def near(step, own, near_in, inverse, targets, weights):
-    one = shape(own, BCOLS)
+    one = blocks(own)
     return call(
         functools.partial(near_kernel, step),
         (own, near_in, inverse, targets, weights),
@@ -270,14 +272,14 @@
     block_count = inverse.shape[1]
     _, far, target_near, _ = z_blocks(block_count)
     cols = lanes(far)
-    field[...] = own[:, :, cols] + far_in[...]
-    diffuse(inverse[:, far, :], field, diffused, slice(0, BCOLS))
+    field[...] = own[far] + far_in[...]
+    diffuse(inverse[:, far, :], field, diffused)
     matrix = spread_matrix(targets[step, :, cols], weights[step, :, cols], target_near * BCOLS)
-    to_near[...] = partial[...] + spread(diffused[...], matrix)
+    rows_of(to_near)[...] = rows_of(partial)[...] + spread([diffused], matrix)
 
 
 def far(step, own, far_in, partial, inverse, targets, weights):
-    one = shape(own, BCOLS)
+    one = blocks(own)
     return call(
         functools.partial(far_kernel, step),
         (own, far_in, partial, inverse, targets, weights),
@@ -294,49 +296,64 @@
     step, own, near_in, far_in, diffused_core, diffused_near, diffused_far, targets, weights,
     sums, mid, field, tall, sems,
 ):
-    block_count = own.shape[2] // BCOLS
+    block_count = own.shape[0]
     near, far, _, _ = z_blocks(block_count)
-    side = lanes(core_side(block_count)[0], REACH)
-    field[:, :, side] = own[:, :, side]
-    field[:, :, lanes(near)] = own[:, :, lanes(near)] + near_in[...]
-    field[:, :, lanes(far)] = own[:, :, lanes(far)] + far_in[...]
-    (copy,) = start_copies(sems, [(field, mid)])
-    tall[:, :, side] = diffused_core[...]
-    tall[:, :, lanes(near)] = diffused_near[...]
-    tall[:, :, lanes(far)] = diffused_far[...]
-    sums[...] = spread(tall[...], spread_matrix(targets[step], weights[step], 0, own.shape[2]))
-    copy.wait()
+    side = core_side(block_count)[0]
+    for j in range(REACH):
+        field[side + j] = own[side + j]
+        tall[side + j] = diffused_core[j]
+    field[near] = own[near] + near_in[...]
+    field[far] = own[far] + far_in[...]
+    tall[near] = diffused_near[...]
+    tall[far] = diffused_far[...]
+    copies = start_copies(sems, [(field.at[j], mid.at[:, :, lanes(j)]) for j in range(block_count)])
+    matrix = spread_matrix(targets[step], weights[step], 0, block_count * BCOLS)
+    total = spread([tall.at[j] for j in range(block_count)], matrix)
+    for j in range(block_count):
+        rows_of(sums.at[j])[...] = total[:, j * BCOLS : (j + 1) * BCOLS]
+    for copy in copies:
+        copy.wait()
 
 
 def outer(step, own, near_in, far_in, diffused, targets, weights):
-    whole = shape(own, own.shape[2])
+    block_count, levels, variables, _ = own.shape
     return call(
         functools.partial(outer_kernel, step),
         (own, near_in, far_in, *diffused, targets, weights),
         [VMEM] * 8,
-        (whole, whole),
+        (
+            blocks(own, block_count),
+            jax.ShapeDtypeStruct((levels, variables, block_count * BCOLS), F32),
+        ),
         (VMEM, HBM),
-        [pltpu.VMEM(own.shape, F32), pltpu.VMEM(own.shape, F32), pltpu.SemaphoreType.DMA((1,))],
+        [
+            pltpu.VMEM(own.shape, F32),
+            pltpu.VMEM(own.shape, F32),
+            pltpu.SemaphoreType.DMA((block_count,)),
+        ],
         2_000_000_000,
         f"outer_step{step}",
     )
 
 
 def squares(value):
-    return jnp.sum(rows_of(value * value), axis=0, keepdims=True)
+    rows = value.reshape(value.shape[0] * value.shape[1], value.shape[2])
+    return jnp.sum(rows * rows, axis=0, keepdims=True)
 
 
 def most_kernel(own, core_in, far_in, start, lane_sums):
-    block_count = own.shape[2] // BCOLS
+    block_count = own.shape[0]
     near, far, _, _ = z_blocks(block_count)
-    side = lanes(core_side(block_count)[0], REACH)
-    core = own[:, :, side] + core_in[...]
-    behind = own[:, :, lanes(far)] + far_in[...]
-    start[:, :, side] = core
-    start[:, :, lanes(far)] = behind
-    start[:, :, lanes(near)] = own[:, :, lanes(near)]
-    core = squares(core)
-    lane_sums[...] = core[:, :BCOLS] + core[:, BCOLS:] + squares(behind)
+    side = core_side(block_count)[0]
+    value = own[far] + far_in[...]
+    start[far] = value
+    start[near] = own[near]
+    total = squares(value)
+    for j in range(REACH):
+        value = own[side + j] + core_in[j]
+        start[side + j] = value
+        total += squares(value)
+    lane_sums[...] = total
 
 
 def most(own, core_in, far_in):
@@ -353,8 +370,8 @@
 
 
 def last_kernel(start, near_in, lane_sums, shares):
-    near = z_blocks(start.shape[2] // BCOLS)[0]
-    sums = lane_sums[...] + squares(start[:, :, lanes(near)] + near_in[...])
+    near = z_blocks(start.shape[0])[0]
+    sums = lane_sums[...] + squares(start[near] + near_in[...])
     shares[...] = jnp.broadcast_to(sums, shares.shape)
 
 
@@ -372,15 +389,14 @@
 
 
 def scale_kernel(cells, start, near_in, shares, out, held, sems):
-    block_count = start.shape[2] // BCOLS
+    block_count = start.shape[0]
     near = z_blocks(block_count)[0]
     energy = jnp.sum(shares[...]) / cells
     root = jnp.sqrt(jnp.full((1, 1, 1), energy + eps_energy, F32))
     copies = []
     for j in range(block_count):
-        cols = slice(j * BCOLS, (j + 1) * BCOLS)
-        held[:, :, cols] = (start[:, :, cols] + jnp.where(near == j, near_in[...], 0.0)) / root
-        copies.append(pltpu.make_async_copy(held.at[:, :, cols], out.at[:, :, cols], sems.at[j]))
+        held[j] = (start[j] + jnp.where(near == j, near_in[...], 0.0)) / root
+        copies.append(pltpu.make_async_copy(held.at[j], out.at[:, :, lanes(j)], sems.at[j]))
         copies[-1].start()
     for copy in copies:
         copy.wait()
@@ -391,9 +407,9 @@
         functools.partial(scale_kernel, cells),
         (start, near_in, shares),
         [VMEM] * 3,
-        jax.ShapeDtypeStruct(start.shape, F32),
+        jax.ShapeDtypeStruct((*start.shape[1:3], start.shape[0] * BCOLS), F32),
         HBM,
-        [pltpu.VMEM(start.shape, F32), pltpu.SemaphoreType.DMA((start.shape[2] // BCOLS,))],
+        [pltpu.VMEM(start.shape, F32), pltpu.SemaphoreType.DMA(start.shape[:1])],
         1_000_000,
         "scale_start",
     )

time: 45.3 us -> 44.5 us (0.982)
  Pallas kernels: 13.5 us -> 11.8 us
  waiting for transfers between devices: 9.56 us -> 10.2 us
    pallas_call x8, Pallas kernels: 13.5 us -> 11.8 us  [call(): pl.pallas_call(kernel, out_shape=outs, in_specs=in_specs, out_specs=out_s...]
    ppermute x4, waiting for transfers between devices: 9.55 us -> 10.1 us  [z_exchange(): return lax.ppermute(value, 'col', pairs)]
  transfers between devices with their start and end apart: 6 -> 6, of which waited for: 3 -> 3; matrix products, arithmetic and copies ran while one was open for 0% -> 0% of each run, Pallas kernels for 18% -> 16%
where the time goes in v5:
time: 44.5 us; the launch traced here: 44.2 us
  starting transfers between devices  12.9 us (29%)
  Pallas kernels  11.8 us (27%)
  waiting for transfers between devices  10.2 us (23%)
  blocking collectives  8.69 us (20%)
  between operations  0.7 us (2%)
    ppermute x4, starting transfers between devices, z_exchange(): return lax.ppermute(value, 'col', pairs)  12.3 us
    pallas_call x8, Pallas kernels, call(): pl.pallas_call(kernel, out_shape=outs, in_specs=in_specs, out_specs=out_s...  11.8 us
    ppermute x4, waiting for transfers between devices, z_exchange(): return lax.ppermute(value, 'col', pairs)  10.1 us
    all_to_all x1, blocking collectives, shards(): shares = lax.all_to_all(shares, 'col', 0, 0, tiled=True)  8.69 us
  transfers between devices with their start and end apart: 6, of which 3 were waited for; matrix products, arithmetic and copies ran while one was open for 0% of the time, Pallas kernels for 16%

profile of v5, /device:TPU:0, one launch (start us, length us, event | category | flops | bytes accessed | tf_op | source)
XLA Modules:
  0.0 44.2 jit_solution(1106406132069249996)
XLA Ops:
  0.6 3.3 %first_step1.1 = (f32[137,4,128]{2,1,0:T(4,128)S(1)}, f32[137,4,128]{2,1,0:T(4,128)S(1)}, f32[2,137,4,128]{3,2,1,0:T(4,128)S(1)}, f32[4,137,4,128]{3,2,1,0:T(4,1...) custom-call(f32[137,4,512]{2,1,0:T(4,128)} %bitcast.10, f32[2,137,4,137]{3,2,1,0:T(4,128)} %bitcast.11, ...), custom_call_target="tpu_custom_call" | custom-call | flops 400000000 | bytes 1000000 | tf_op jit(solution)/shard_map/first_step1/pallas_call | solution.py:116
  3.9 0.5 %collective-permute-start = (f32[2,137,4,128]{3,2,1,0:T(4,128)S(1)}, f32[2,137,4,128]{3,2,1,0:T(4,128)S(1)}, u32[]{:S(2)}, u32[]{:S(2)}) collective-permute-start(f32[2,137,4,128]{3,2,1,0:T(4,128)S(1)} %get-tuple-element.24), channel_id=1, source_target_pairs={{0,1},{1,0},{2,3},{3,2},{4,5},{5,4},{6,7},{7,6},{8,9},{9,8},{10,11... | collective-permute-start | bytes 1683464 | tf_op jit(solution)/shard_map/ppermute | solution.py:420
  4.5 4.7 %collective-permute-start.1 = (f32[137,4,128]{2,1,0:T(4,128)S(1)}, f32[137,4,128]{2,1,0:T(4,128)S(1)}, u32[]{:S(2)}, u32[]{:S(2)}) collective-permute-start(f32[137,4,128]{2,1,0:T(4,128)S(1)} %get-tuple-element.26), channel_id=1, source_target_pairs={{0,7},{1,2},{2,1},{3,4},{4,3},{5,6},{6,5},{7,0},{8,15},{9,10},{10,... | collective-permute-start | bytes 841736 | tf_op jit(solution)/shard_map/ppermute | solution.py:426
  9.2 0.0 collective-permute-start.2
  9.2 0.0 collective-permute-done.core_in
  9.2 2.8 %inner_step1.1 = (f32[4,137,4,128]{3,2,1,0:T(4,128)S(1)}, f32[137,4,137]{2,1,0:T(4,128)S(1)}, f32[2,137,4,128]{3,2,1,0:T(4,128)S(1)}, f32[2,137,4,128]{3,2,1,0:T(4,128)S(1)}) custom-call(f32[4,137,4,128]{3,2,1,0:T(4,128)S(1)} %get-tuple-element.21.diffused, s32[2,4,512]{2,1,0:T(4,128)S(1)} %get-tuple-element.22.targets, ...), custom_call_target="tpu_custom_call" | custom-call | flops 2000000000 | bytes 1000000 | tf_op jit(solution)/shard_map/inner_step1/pallas_call | solution.py:116
  12.0 0.1 collective-permute-start.3
  12.1 4.2 %collective-permute-done.1.near_in = f32[137,4,128]{2,1,0:T(4,128)S(1)} collective-permute-done((f32[137,4,128]{2,1,0:T(4,128)S(1)}, f32[137,4,128]{2,1,0:T(4,128)S(1)}, u32[]{:S(2)}, u32[]{:S(2)}) %collective-permute-start.1) | collective-permute-done | bytes 280608 | tf_op jit(solution)/shard_map/ppermute | solution.py:426
  16.3 0.7 %near_step0.1 = (f32[137,4,128]{2,1,0:T(4,128)S(1)}, f32[137,4,128]{2,1,0:T(4,128)S(1)}, f32[137,4,128]{2,1,0:T(4,128)S(1)}) custom-call(f32[4,137,4,128]{3,2,1,0:T(4,128)S(1)} %get-tuple-element.25.own, f32[137,4,128]{2,1,0:T(4,128)S(1)} %collective-permute-done.1.near_in, f32[137,4,137]{2,1,0:T(4,128)S(1)} %get-tuple-element.29.inverse, ...), custom_call_target="tpu_custom_call" | custom-call | flops 300000000 | bytes 1000000 | tf_op jit(solution)/shard_map/near_step0/pallas_call | solution.py:116
  17.0 3.8 %collective-permute-start.4 = (f32[137,4,128]{2,1,0:T(4,128)S(1)}, f32[137,4,128]{2,1,0:T(4,128)S(1)}, u32[]{:S(2)}, u32[]{:S(2)}) collective-permute-start(f32[137,4,128]{2,1,0:T(4,128)S(1)} %get-tuple-element.36), channel_id=1, source_target_pairs={{0,7},{1,2},{2,1},{3,4},{4,3},{5,6},{6,5},{7,0},{8,15},{9,10},{10,... | collective-permute-start | bytes 841736 | tf_op jit(solution)/shard_map/ppermute | solution.py:426
  20.8 1.6 %collective-permute-done.2.far_in = f32[137,4,128]{2,1,0:T(4,128)S(1)} collective-permute-done((f32[137,4,128]{2,1,0:T(4,128)S(1)}, f32[137,4,128]{2,1,0:T(4,128)S(1)}, u32[]{:S(2)}, u32[]{:S(2)}) %collective-permute-start.2) | collective-permute-done | bytes 280608 | tf_op jit(solution)/shard_map/ppermute | solution.py:426
  22.3 0.7 %far_step0.1 = (f32[137,4,128]{2,1,0:T(4,128)S(1)}, f32[137,4,128]{2,1,0:T(4,128)S(1)}) custom-call(f32[4,137,4,128]{3,2,1,0:T(4,128)S(1)} %get-tuple-element.25.own, f32[137,4,128]{2,1,0:T(4,128)S(1)} %collective-permute-done.2.far_in, f32[137,4,128]{2,1,0:T(4,128)S(1)} %get-tuple-element.31.partial, f32[137,4,137]{2,1,0:T(4,128)S(1)} %get-tuple-element.29.inverse, ...), custom_call_target="tpu_custom_call" | custom-call | flops 300000000 | bytes 1000000 | tf_op jit(solution)/shard_map/far_step0/pallas_call | solution.py:116
  23.0 3.8 %collective-permute-start.5 = (f32[137,4,128]{2,1,0:T(4,128)S(1)}, f32[137,4,128]{2,1,0:T(4,128)S(1)}, u32[]{:S(2)}, u32[]{:S(2)}) collective-permute-start(f32[137,4,128]{2,1,0:T(4,128)S(1)} %get-tuple-element.38), channel_id=1, source_target_pairs={{0,7},{1,2},{2,1},{3,4},{4,3},{5,6},{6,5},{7,0},{8,15},{9,10},{10,... | collective-permute-start | bytes 841736 | tf_op jit(solution)/shard_map/ppermute | solution.py:426
  26.8 2.5 %outer_step0.1 = (f32[4,137,4,128]{3,2,1,0:T(4,128)S(1)}, f32[137,4,512]{2,1,0:T(4,128)}) custom-call(f32[4,137,4,128]{3,2,1,0:T(4,128)S(1)} %get-tuple-element.25.own, f32[137,4,128]{2,1,0:T(4,128)S(1)} %collective-permute-done.1.near_in, f32[137,4,128]{2,1,0:T(4,128)S(1)} %collective-permute-done.2.far_in, ...), custom_call_target="tpu_custom_call" | custom-call | flops 2000000000 | bytes 1000000 | tf_op jit(solution)/shard_map/outer_step0/pallas_call | solution.py:116
  29.3 0.0 collective-permute-done.4.far_in
  29.3 0.0 collective-permute-done.3.core_in
  29.3 0.5 %squares_of_most_blocks.1 = (f32[4,137,4,128]{3,2,1,0:T(4,128)S(1)}, f32[1,128]{1,0:T(1,128)S(1)}) custom-call(f32[4,137,4,128]{3,2,1,0:T(4,128)S(1)} %get-tuple-element.34.own, f32[2,137,4,128]{3,2,1,0:T(4,128)S(1)} %collective-permute-done.3.core_in, f32[137,4,128]{2,1,0:T(4,128)S(1)} %collective-permute-done.4.far_in), custom_call_target="tpu_custom_call" | custom-call | flops 1000000 | bytes 1000000 | tf_op jit(solution)/shard_map/squares_of_most_blocks/pallas_call | solution.py:116
  29.8 4.3 %collective-permute-done.5.near_in = f32[137,4,128]{2,1,0:T(4,128)S(1)} collective-permute-done((f32[137,4,128]{2,1,0:T(4,128)S(1)}, f32[137,4,128]{2,1,0:T(4,128)S(1)}, u32[]{:S(2)}, u32[]{:S(2)}) %collective-permute-start.5) | collective-permute-done | bytes 280608 | tf_op jit(solution)/shard_map/ppermute | solution.py:426
  34.1 0.1 squares_of_last_block.1
  34.2 8.7 %all_to_all.11 = f32[8,1,128]{2,1,0:T(1,128)S(1)} all-to-all(f32[8,1,128]{2,1,0:T(1,128)S(1)} %bitcast.9), channel_id=1, replica_groups=mesh['mem'=4,'col'=8] {'col'}, dimensions={0} | all-to-all | bytes 8192 | tf_op jit(solution)/shard_map/all_to_all | solution.py:457
  42.9 1.3 %scale_start.1 = f32[137,4,512]{2,1,0:T(4,128)} custom-call(f32[4,137,4,128]{3,2,1,0:T(4,128)S(1)} %get-tuple-element.37.start, f32[137,4,128]{2,1,0:T(4,128)S(1)} %collective-permute-done.5.near_in, f32[8,128]{1,0:T(8,128)S(1)} %bitcast.8), custom_call_target="tpu_custom_call" | custom-call | flops 1000000 | bytes 1000000 | tf_op jit(solution)/shard_map/scale_start/pallas_call | solution.py:116
Async XLA Ops:
  3.9 5.3 %collective-permute-start = (f32[2,137,4,128]{3,2,1,0:T(4,128)S(1)}, f32[2,137,4,128]{3,2,1,0:T(4,128)S(1)}, u32[]{:S(2)}, u32[]{:S(2)}) collective-permute-start(f32[2,137,4,128]{3,2,1,0:T(4,128)S(1)} %get-tuple-element.24), channel_id=1, source_target_pairs={{0,1},{1,0},{2,3},{3,2},{4,5},{5,4},{6,7},{7,6},{8,9},{9,8},{10,11... | collective-permute-start | bytes 1683464 | tf_op jit(solution)/shard_map/ppermute | solution.py:420
  4.5 11.9 %collective-permute-start.1 = (f32[137,4,128]{2,1,0:T(4,128)S(1)}, f32[137,4,128]{2,1,0:T(4,128)S(1)}, u32[]{:S(2)}, u32[]{:S(2)}) collective-permute-start(f32[137,4,128]{2,1,0:T(4,128)S(1)} %get-tuple-element.26), channel_id=1, source_target_pairs={{0,7},{1,2},{2,1},{3,4},{4,3},{5,6},{6,5},{7,0},{8,15},{9,10},{10,... | collective-permute-start | bytes 841736 | tf_op jit(solution)/shard_map/ppermute | solution.py:426
  9.2 13.2 %collective-permute-start.2 = (f32[137,4,128]{2,1,0:T(4,128)S(1)}, f32[137,4,128]{2,1,0:T(4,128)S(1)}, u32[]{:S(2)}, u32[]{:S(2)}) collective-permute-start(f32[137,4,128]{2,1,0:T(4,128)S(1)} %get-tuple-element.27), channel_id=1, source_target_pairs={{0,7},{1,2},{2,1},{3,4},{4,3},{5,6},{6,5},{7,0},{8,15},{9,10},{10,... | collective-permute-start | bytes 841736 | tf_op jit(solution)/shard_map/ppermute | solution.py:426
  12.0 17.3 %collective-permute-start.3 = (f32[2,137,4,128]{3,2,1,0:T(4,128)S(1)}, f32[2,137,4,128]{3,2,1,0:T(4,128)S(1)}, u32[]{:S(2)}, u32[]{:S(2)}) collective-permute-start(f32[2,137,4,128]{3,2,1,0:T(4,128)S(1)} %get-tuple-element.35), channel_id=1, source_target_pairs={{0,1},{1,0},{2,3},{3,2},{4,5},{5,4},{6,7},{7,6},{8,9},{9,8},{10,11... | collective-permute-start | bytes 1683464 | tf_op jit(solution)/shard_map/ppermute | solution.py:420
  17.0 12.3 %collective-permute-start.4 = (f32[137,4,128]{2,1,0:T(4,128)S(1)}, f32[137,4,128]{2,1,0:T(4,128)S(1)}, u32[]{:S(2)}, u32[]{:S(2)}) collective-permute-start(f32[137,4,128]{2,1,0:T(4,128)S(1)} %get-tuple-element.36), channel_id=1, source_target_pairs={{0,7},{1,2},{2,1},{3,4},{4,3},{5,6},{6,5},{7,0},{8,15},{9,10},{10,... | collective-permute-start | bytes 841736 | tf_op jit(solution)/shard_map/ppermute | solution.py:426
  23.0 11.1 %collective-permute-start.5 = (f32[137,4,128]{2,1,0:T(4,128)S(1)}, f32[137,4,128]{2,1,0:T(4,128)S(1)}, u32[]{:S(2)}, u32[]{:S(2)}) collective-permute-start(f32[137,4,128]{2,1,0:T(4,128)S(1)} %get-tuple-element.38), channel_id=1, source_target_pairs={{0,7},{1,2},{2,1},{3,4},{4,3},{5,6},{6,5},{7,0},{8,15},{9,10},{10,... | collective-permute-start | bytes 841736 | tf_op jit(solution)/shard_map/ppermute | solution.py:426

commit v6 on v5

--- a/solution.py
+++ b/solution.py
@@ -14,11 +14,13 @@
 STEPS = 2
 VMEM_LIMIT = 32 * 1024 * 1024
 NOWHERE = -(1 << 14)
+PIECES = 3
 
 eps_energy = 1e-06
 
 F32 = jnp.float32
 BF16 = jnp.bfloat16
+ANY = pl.BlockSpec(memory_space=pl.ANY)
 HBM = pl.BlockSpec(memory_space=pltpu.HBM)
 VMEM = pl.BlockSpec(memory_space=pltpu.VMEM)
 
@@ -134,11 +136,10 @@
 
 def first_kernel(
     step, all_blocks, fields, inverses, routes, points, weights,
-    to_near, to_far, to_core, diffused, targets, merged, field, inverse, route, point, weight, sems,
+    to_near, to_far, diffused, inverse, targets, merged, field, route, point, weight, sems,
 ):
     block_count = inverses.shape[2]
     near, far, target_near, target_far = z_blocks(block_count)
-    first, first_target = core_side(block_count)
     copies = start_copies(
         sems,
         [
@@ -146,8 +147,9 @@
             (points, point),
             (weights, weight),
             (inverses.at[step], inverse),
-        ]
-        + [(fields.at[:, :, lanes(j)], field.at[j]) for j in range(block_count)],
+            (fields.at[:, :, lanes(near)], field.at[0]),
+            (fields.at[:, :, lanes(far)], field.at[1]),
+        ],
     )
     for copy in copies[:3]:
         copy.wait()
@@ -156,19 +158,18 @@
             cols = slice(j * BCOLS, (j + 1) * BCOLS)
             found = target_columns(point[number, :, cols], route, number, j, block_count, all_blocks)
             targets[number, :, cols], merged[number, :, cols] = merge_points(found, weight[number, :, cols])
-    z_matrix = side_matrix(targets, merged, step, (near, far), (target_near * BCOLS, target_far * BCOLS))
-    core_columns = (first_target * BCOLS, (first_target + 1) * BCOLS)
-    core_matrix = side_matrix(targets, merged, step, (first, first + 1), core_columns)
+    matrix = side_matrix(targets, merged, step, (near, far), (target_near * BCOLS, target_far * BCOLS))
     copies[3].wait()
-    for j in range(block_count):
+    for j, block in enumerate((near, far)):
         copies[4 + j].wait()
-        diffuse(inverse[:, j, :], field.at[j], diffused.at[j])
-    sums = spread([diffused.at[near], diffused.at[far]], z_matrix)
+        diffuse(inverse[:, block, :], field.at[j], diffused.at[j])
+    sums = spread([diffused.at[0], diffused.at[1]], matrix)
     rows_of(to_near)[...] = sums[:, :BCOLS]
     rows_of(to_far)[...] = sums[:, BCOLS:]
-    sums = spread([diffused.at[first], diffused.at[first + 1]], core_matrix)
-    for j in range(REACH):
-        rows_of(to_core.at[j])[...] = sums[:, j * BCOLS : (j + 1) * BCOLS]
+
+
+def level_pieces(levels):
+    return [slice(levels * part // PIECES, levels * (part + 1) // PIECES) for part in range(PIECES)]
 
 
 def blocks(like, *count):
@@ -176,7 +177,7 @@
 
 
 def first(step, all_blocks, fields, inverses, routes, points, weights):
-    one, two, whole = blocks(fields), blocks(fields, REACH), blocks(fields, inverses.shape[2])
+    one, two = blocks(fields), blocks(fields, REACH)
     return call(
         functools.partial(first_kernel, step, all_blocks),
         (fields, inverses, routes, points, weights),
@@ -185,18 +186,17 @@
             one,
             one,
             two,
-            whole,
+            jax.ShapeDtypeStruct(inverses.shape[1:], F32),
             jax.ShapeDtypeStruct(points.shape, jnp.int32),
             jax.ShapeDtypeStruct(weights.shape, F32),
         ),
         (VMEM,) * 6,
         [
-            pltpu.VMEM(whole.shape, F32),
-            pltpu.VMEM(inverses.shape[1:], F32),
+            pltpu.VMEM(two.shape, F32),
             pltpu.SMEM(routes.shape, jnp.int32),
             pltpu.VMEM(points.shape, jnp.int32),
             pltpu.VMEM(weights.shape, F32),
-            pltpu.SemaphoreType.DMA((4 + inverses.shape[2],)),
+            pltpu.SemaphoreType.DMA((6,)),
         ],
         400_000_000,
         f"first_step{step}",
@@ -204,38 +204,90 @@
 
 
 def inner_kernel(
-    step, diffused, targets, weights, core_in, inverses, own, inverse, to_core, diffused_core, sems
+    step, fields, z_diffused, inverse, targets, weights, inverses, own, next_inverse, *refs
 ):
-    block_count = inverses.shape[2]
-    side_first, first_target = core_side(block_count)
-    (copy,) = start_copies(sems, [(inverses.at[step - 1], inverse)])
+    to_core, (field, tall, sems) = refs[:-3], refs[-3:]
+    block_count = inverse.shape[1]
+    near, far, _, _ = z_blocks(block_count)
+    side, first_target = core_side(block_count)
+    copies = start_copies(
+        sems,
+        [(fields.at[:, :, lanes(side + j)], field.at[j]) for j in range(REACH)]
+        + [(inverses.at[step - 1], next_inverse)],
+    )
+    columns = (first_target * BCOLS, (first_target + 1) * BCOLS)
+    core_matrix = side_matrix(targets, weights, step, (side, side + 1), columns)
     matrix = spread_matrix(targets[step], weights[step], 0, block_count * BCOLS)
-    sums = spread([diffused.at[j] for j in range(block_count)], matrix)
+    tall[near] = z_diffused[0]
+    tall[far] = z_diffused[1]
+    for j in range(REACH):
+        copies[j].wait()
+        diffuse(inverse[:, side + j, :], field.at[j], tall.at[side + j])
+    sums = spread([tall.at[side + j] for j in range(REACH)], core_matrix)
+    variables = field.shape[2]
+    for piece, levels in zip(to_core, level_pieces(field.shape[1])):
+        rows = slice(levels.start * variables, levels.stop * variables)
+        for j in range(REACH):
+            rows_of(piece.at[j])[...] = sums[rows, j * BCOLS : (j + 1) * BCOLS]
+    sums = spread([tall.at[j] for j in range(block_count)], matrix)
     for j in range(block_count):
         rows_of(own.at[j])[...] = sums[:, j * BCOLS : (j + 1) * BCOLS]
+    copies[REACH].wait()
+
+
+def inner(step, fields, z_diffused, inverse, targets, weights, inverses):
+    two, whole = blocks(fields, REACH), blocks(fields, inverse.shape[1])
+    pieces = [
+        jax.ShapeDtypeStruct((REACH, levels.stop - levels.start, *two.shape[2:]), F32)
+        for levels in level_pieces(fields.shape[0])
+    ]
+    own, inverse, *pieces = call(
+        functools.partial(inner_kernel, step),
+        (fields, z_diffused, inverse, targets, weights, inverses),
+        [HBM] + [VMEM] * 4 + [HBM],
+        (whole, jax.ShapeDtypeStruct(inverse.shape, F32), *pieces),
+        (VMEM,) * (2 + PIECES),
+        [
+            pltpu.VMEM(two.shape, F32),
+            pltpu.VMEM(whole.shape, F32),
+            pltpu.SemaphoreType.DMA((REACH + 1,)),
+        ],
+        2_000_000_000,
+        f"inner_step{step}",
+    )
+    return own, inverse, pieces
+
+
+def add_pieces(pieces, block, out):
+    for piece, levels in zip(pieces, level_pieces(out.shape[0])):
+        out[levels] += piece[block]
+
+
+def core_kernel(step, own, inverse, targets, weights, _, *refs):
+    core_in, (to_core, diffused, field) = refs[:PIECES], refs[PIECES:]
+    side, first_target = core_side(own.shape[0])
+    columns = (first_target * BCOLS, (first_target + 1) * BCOLS)
+    matrix = side_matrix(targets, weights, step, (side, side + 1), columns)
     for j in range(REACH):
-        own[side_first + j] += core_in[j]
-    columns = (first_target * BCOLS, (first_target + 1) * BCOLS)
-    matrix = side_matrix(targets, weights, step - 1, (side_first, side_first + 1), columns)
-    copy.wait()
-    for j in range(REACH):
-        diffuse(inverse[:, side_first + j, :], own.at[side_first + j], diffused_core.at[j])
-    sums = spread([diffused_core.at[j] for j in range(REACH)], matrix)
+        field[j] = own[side + j]
+        add_pieces(core_in, j, field.at[j])
+        diffuse(inverse[:, side + j, :], field.at[j], diffused.at[j])
+    sums = spread([diffused.at[j] for j in range(REACH)], matrix)
     for j in range(REACH):
         rows_of(to_core.at[j])[...] = sums[:, j * BCOLS : (j + 1) * BCOLS]
 
 
-def inner(step, diffused, targets, weights, core_in, inverses):
-    two = blocks(diffused, REACH)
-    return call(
-        functools.partial(inner_kernel, step),
-        (diffused, targets, weights, core_in, inverses),
-        [VMEM] * 4 + [HBM],
-        (blocks(diffused, diffused.shape[0]), jax.ShapeDtypeStruct(inverses.shape[1:], F32), two, two),
-        (VMEM,) * 4,
-        [pltpu.SemaphoreType.DMA((1,))],
-        2_000_000_000,
-        f"inner_step{step}",
+def core(step, own, core_in, inverse, targets, weights, behind):
+    two = blocks(own, REACH)
+    return call(
+        functools.partial(core_kernel, step),
+        (own, inverse, targets, weights, behind, *core_in),
+        [VMEM] * 4 + [ANY] + [VMEM] * PIECES,
+        (two, two),
+        (VMEM,) * 2,
+        [pltpu.VMEM(two.shape, F32)],
+        300_000_000,
+        f"core_step{step}",
     )
 
 
@@ -268,7 +320,7 @@
     )
 
 
-def far_kernel(step, own, far_in, partial, inverse, targets, weights, to_near, diffused, field):
+def far_kernel(step, own, far_in, partial, inverse, targets, weights, _, to_near, diffused, field):
     block_count = inverse.shape[1]
     _, far, target_near, _ = z_blocks(block_count)
     cols = lanes(far)
@@ -278,12 +330,12 @@
     rows_of(to_near)[...] = rows_of(partial)[...] + spread([diffused], matrix)
 
 
-def far(step, own, far_in, partial, inverse, targets, weights):
+def far(step, own, far_in, partial, inverse, targets, weights, behind):
     one = blocks(own)
     return call(
         functools.partial(far_kernel, step),
-        (own, far_in, partial, inverse, targets, weights),
-        [VMEM] * 6,
+        (own, far_in, partial, inverse, targets, weights, behind),
+        [VMEM] * 6 + [ANY],
         (one, one),
         (VMEM,) * 2,
         [pltpu.VMEM(one.shape, F32)],
@@ -293,14 +345,15 @@
 
 
 def outer_kernel(
-    step, own, near_in, far_in, diffused_core, diffused_near, diffused_far, targets, weights,
-    sums, mid, field, tall, sems,
+    step, own, near_in, far_in, diffused_core, diffused_near, diffused_far, targets, weights, *refs
 ):
+    core_in, (sums, mid, field, tall, sems) = refs[:PIECES], refs[PIECES:]
     block_count = own.shape[0]
     near, far, _, _ = z_blocks(block_count)
     side = core_side(block_count)[0]
     for j in range(REACH):
         field[side + j] = own[side + j]
+        add_pieces(core_in, j, field.at[side + j])
         tall[side + j] = diffused_core[j]
     field[near] = own[near] + near_in[...]
     field[far] = own[far] + far_in[...]
@@ -315,12 +368,12 @@
         copy.wait()
 
 
-def outer(step, own, near_in, far_in, diffused, targets, weights):
+def outer(step, own, near_in, far_in, core_in, diffused, targets, weights):
     block_count, levels, variables, _ = own.shape
     return call(
         functools.partial(outer_kernel, step),
-        (own, near_in, far_in, *diffused, targets, weights),
-        [VMEM] * 8,
+        (own, near_in, far_in, *diffused, targets, weights, *core_in),
+        [VMEM] * (8 + PIECES),
         (
             blocks(own, block_count),
             jax.ShapeDtypeStruct((levels, variables, block_count * BCOLS), F32),
@@ -371,16 +424,15 @@
 
 def last_kernel(start, near_in, lane_sums, shares):
     near = z_blocks(start.shape[0])[0]
-    sums = lane_sums[...] + squares(start[near] + near_in[...])
-    shares[...] = jnp.broadcast_to(sums, shares.shape)
-
-
-def last(count, start, near_in, lane_sums):
+    shares[...] = lane_sums[...] + squares(start[near] + near_in[...])
+
+
+def last(start, near_in, lane_sums):
     return call(
         last_kernel,
         (start, near_in, lane_sums),
         [VMEM] * 3,
-        jax.ShapeDtypeStruct((count, BCOLS), F32),
+        jax.ShapeDtypeStruct(lane_sums.shape, F32),
         VMEM,
         [],
         1_000_000,
@@ -388,15 +440,24 @@
     )
 
 
-def scale_kernel(cells, start, near_in, shares, out, held, sems):
+def scale_kernel(cells, start, near_in, *refs):
+    *shares, out, held, sems = refs
     block_count = start.shape[0]
     near = z_blocks(block_count)[0]
-    energy = jnp.sum(shares[...]) / cells
-    root = jnp.sqrt(jnp.full((1, 1, 1), energy + eps_energy, F32))
+    total = shares[0][...]
+    for share in shares[1:]:
+        total += share[...]
+    energy = jnp.sum(total) / cells
+    factor = 1.0 / jnp.sqrt(jnp.full((1, 1, 1), energy + eps_energy, F32))
+    levels = start.shape[1]
+    parts = 5
     copies = []
-    for j in range(block_count):
-        held[j] = (start[j] + jnp.where(near == j, near_in[...], 0.0)) / root
-        copies.append(pltpu.make_async_copy(held.at[j], out.at[:, :, lanes(j)], sems.at[j]))
+    for part in range(parts):
+        rows = slice(levels * part // parts, levels * (part + 1) // parts)
+        for j in range(block_count):
+            cols = slice(j * BCOLS, (j + 1) * BCOLS)
+            held[rows, :, cols] = (start[j, rows] + jnp.where(near == j, near_in[rows], 0.0)) * factor
+        copies.append(pltpu.make_async_copy(held.at[rows], out.at[rows], sems.at[part]))
         copies[-1].start()
     for copy in copies:
         copy.wait()
@@ -405,14 +466,36 @@
 def scale(start, near_in, shares, cells):
     return call(
         functools.partial(scale_kernel, cells),
-        (start, near_in, shares),
-        [VMEM] * 3,
+        (start, near_in, *shares),
+        [VMEM] * (2 + len(shares)),
         jax.ShapeDtypeStruct((*start.shape[1:3], start.shape[0] * BCOLS), F32),
         HBM,
-        [pltpu.VMEM(start.shape, F32), pltpu.SemaphoreType.DMA(start.shape[:1])],
+        [pltpu.VMEM((*start.shape[1:3], start.shape[0] * BCOLS), F32), pltpu.SemaphoreType.DMA((5,))],
         1_000_000,
         "scale_start",
     )
+
+
+def add_kernel(*refs):
+    *parts, out = refs
+    total = parts[0][...]
+    for part in parts[1:]:
+        total += part[...]
+    out[...] = total
+
+
+def add(parts):
+    return call(
+        add_kernel, parts, [VMEM] * len(parts), jax.ShapeDtypeStruct(parts[0].shape, F32), VMEM, [], 1, "add_shares"
+    )
+
+
+def share_out(share):
+    count = lax.axis_size("col")
+    if count > 8:
+        return [lax.all_to_all(jnp.broadcast_to(share, (count, BCOLS)), "col", 0, 0, tiled=True)]
+    share = add([share, core_exchange(share)])
+    return [share] + [lax.ppermute(share, "col", [(i, i ^ s) for i in range(count)]) for s in (2, 4, 6)]
 
 
 def core_exchange(value):
@@ -436,25 +519,25 @@
         for value in (fields, inverses, dep_lists, dep_points, weights)
     )
 
-    to_near, to_far, to_core, diffused, targets, merged = first(
+    to_near, to_far, z_diffused, inverse, targets, merged = first(
         1, all_blocks, fields, inverses, dep_lists, dep_points, weights
     )
     near_in = z_exchange(to_near)
     far_in = z_exchange(to_far)
-    own, inverse, to_core, diffused_core = inner(1, diffused, targets, merged, core_exchange(to_core), inverses)
-
-    next_core_in = core_exchange(to_core)
+    own, inverse, pieces = inner(1, fields, z_diffused, inverse, targets, merged, inverses)
+    core_in = [core_exchange(piece) for piece in pieces]
+
     to_far, partial, diffused_near = near(0, own, near_in, inverse, targets, merged)
     next_far_in = z_exchange(to_far)
-    to_near, diffused_far = far(0, own, far_in, partial, inverse, targets, merged)
+    to_core, diffused_core = core(0, own, core_in, inverse, targets, merged, partial)
+    next_core_in = core_exchange(to_core)
+    to_near, diffused_far = far(0, own, far_in, partial, inverse, targets, merged, diffused_core)
     next_near_in = z_exchange(to_near)
-    own, mid = outer(
-        0, own, near_in, far_in, (diffused_core, diffused_near, diffused_far), targets, merged
-    )
+    diffused = (diffused_core, diffused_near, diffused_far)
+    own, mid = outer(0, own, near_in, far_in, core_in, diffused, targets, merged)
 
     start, lane_sums = most(own, next_core_in, next_far_in)
-    shares = last(count, start, next_near_in, lane_sums)
-    shares = lax.all_to_all(shares, "col", 0, 0, tiled=True)
+    shares = share_out(last(start, next_near_in, lane_sums))
     lanczos = scale(start, next_near_in, shares, adj_final.size * count)
     return jnp.transpose(mid, (1, 0, 2)), jnp.transpose(lanczos, (1, 0, 2))
 

time: 44.5 us -> 42.2 us (0.948)
  blocking collectives: 8.69 us -> 0 us
  waiting for transfers between devices: 10.2 us -> 14.5 us
  starting transfers between devices: 12.9 us -> 14.8 us
    all_to_all x1 -> x0, blocking collectives: 8.69 us -> none  [shards(): shares = lax.all_to_all(shares, 'col', 0, 0, tiled=True)]
    ppermute x0 -> x3, starting transfers between devices: none -> 4.39 us  [share_out(): lax.ppermute(share, 'col', [(i, i ^ s) for i in range(count)])]
    ppermute x4, starting transfers between devices: 12.3 us -> 9.6 us  [z_exchange(): return lax.ppermute(value, 'col', pairs)]
    ppermute x0 -> x3, waiting for transfers between devices: none -> 2.09 us  [share_out(): lax.ppermute(share, 'col', [(i, i ^ s) for i in range(count)])]
    ppermute x4, waiting for transfers between devices: 10.1 us -> 11.3 us  [z_exchange(): return lax.ppermute(value, 'col', pairs)]
    ppermute x2 -> x5, waiting for transfers between devices: 0.01 us -> 1.12 us  [core_exchange(): return lax.ppermute(value, 'col', [(i, i ^ 1) for i in range(count)])]
    pallas_call x8 -> x10, Pallas kernels: 11.8 us -> 12 us  [call(): pl.pallas_call(kernel, out_shape=outs, in_specs=in_specs, out_specs=out_s...]
  transfers between devices with their start and end apart: 6 -> 12, of which waited for: 3 -> 7; matrix products, arithmetic and copies ran while one was open for 0% -> 0% of each run, Pallas kernels for 16% -> 20%
where the time goes in v6:
time: 42.2 us; the launch traced here: 42 us
  starting transfers between devices  14.8 us (35%)
  waiting for transfers between devices  14.5 us (34%)
  Pallas kernels  12 us (28%)
  between operations  0.73 us (2%)
    pallas_call x10, Pallas kernels, call(): pl.pallas_call(kernel, out_shape=outs, in_specs=in_specs, out_specs=out_s...  12 us
    ppermute x4, waiting for transfers between devices, z_exchange(): return lax.ppermute(value, 'col', pairs)  11.3 us
    ppermute x4, starting transfers between devices, z_exchange(): return lax.ppermute(value, 'col', pairs)  9.6 us
    ppermute x3, starting transfers between devices, share_out(): lax.ppermute(share, 'col', [(i, i ^ s) for i in range(count)])  4.39 us
    ppermute x3, waiting for transfers between devices, share_out(): lax.ppermute(share, 'col', [(i, i ^ s) for i in range(count)])  2.09 us
    ppermute x5, waiting for transfers between devices, core_exchange(): return lax.ppermute(value, 'col', [(i, i ^ 1) for i in range(count)])  1.12 us
  transfers between devices with their start and end apart: 12, of which 7 were waited for; matrix products, arithmetic and copies ran while one was open for 0% of the time, Pallas kernels for 20%

profile of v6, /device:TPU:0, one launch (start us, length us, event | category | flops | bytes accessed | tf_op | source)
XLA Modules:
  0.0 42.0 jit_solution(986359644923606753)
XLA Ops:
  0.6 2.3 %first_step1.1 = (f32[137,4,128]{2,1,0:T(4,128)S(1)}, f32[137,4,128]{2,1,0:T(4,128)S(1)}, f32[2,137,4,128]{3,2,1,0:T(4,128)S(1)}, f32[137,4,137]{2,1,0:T(4,128)S...) custom-call(f32[137,4,512]{2,1,0:T(4,128)} %bitcast.5, f32[2,137,4,137]{3,2,1,0:T(4,128)} %bitcast.7, ...), custom_call_target="tpu_custom_call" | custom-call | flops 400000000 | bytes 1000000 | tf_op jit(solution)/shard_map/first_step1/pallas_call | solution.py:118
  2.9 4.6 %collective-permute-start = (f32[137,4,128]{2,1,0:T(4,128)S(1)}, f32[137,4,128]{2,1,0:T(4,128)S(1)}, u32[]{:S(2)}, u32[]{:S(2)}) collective-permute-start(f32[137,4,128]{2,1,0:T(4,128)S(1)} %get-tuple-element.29), channel_id=1, source_target_pairs={{0,7},{1,2},{2,1},{3,4},{4,3},{5,6},{6,5},{7,0},{8,15},{9,10},{10,... | collective-permute-start | bytes 841736 | tf_op jit(solution)/shard_map/ppermute | solution.py:509
  7.4 3.0 %inner_step1.1 = (f32[4,137,4,128]{3,2,1,0:T(4,128)S(1)}, f32[137,4,137]{2,1,0:T(4,128)S(1)}, f32[2,45,4,128]{3,2,1,0:T(4,128)S(1)}, f32[2,46,4,128]{3,2,1,0:T(4,128)S(1)}, f32[2,46,4,128]{3,2,1,0:T(4,128)S(1)}) custom-call(f32[137,4,512]{2,1,0:T(4,128)} %bitcast.6, f32[2,137,4,128]{3,2,1,0:T(4,128)S(1)} %get-tuple-element.24.z_diffused, ...), custom_call_target="tpu_custom_call" | custom-call | flops 2000000000 | bytes 1000000 | tf_op jit(solution)/shard_map/inner_step1/pallas_call | solution.py:118
  10.5 0.1 collective-permute-start.3
  10.6 0.5 %collective-permute-start.4 = (f32[2,46,4,128]{3,2,1,0:T(4,128)S(1)}, f32[2,46,4,128]{3,2,1,0:T(4,128)S(1)}, u32[]{:S(2)}, u32[]{:S(2)}) collective-permute-start(f32[2,46,4,128]{3,2,1,0:T(4,128)S(1)} %get-tuple-element.35), channel_id=1, source_target_pairs={{0,1},{1,0},{2,3},{3,2},{4,5},{5,4},{6,7},{7,6},{8,9},{9,8},{10,11... | collective-permute-start | bytes 565256 | tf_op jit(solution)/shard_map/ppermute | solution.py:503
  11.0 0.1 collective-permute-start.2
  11.1 0.6 %collective-permute-start.1 = (f32[137,4,128]{2,1,0:T(4,128)S(1)}, f32[137,4,128]{2,1,0:T(4,128)S(1)}, u32[]{:S(2)}, u32[]{:S(2)}) collective-permute-start(f32[137,4,128]{2,1,0:T(4,128)S(1)} %get-tuple-element.30), channel_id=1, source_target_pairs={{0,7},{1,2},{2,1},{3,4},{4,3},{5,6},{6,5},{7,0},{8,15},{9,10},{10,... | collective-permute-start | bytes 841736 | tf_op jit(solution)/shard_map/ppermute | solution.py:509
  11.8 2.1 %collective-permute-done.near_in = f32[137,4,128]{2,1,0:T(4,128)S(1)} collective-permute-done((f32[137,4,128]{2,1,0:T(4,128)S(1)}, f32[137,4,128]{2,1,0:T(4,128)S(1)}, u32[]{:S(2)}, u32[]{:S(2)}) %collective-permute-start) | collective-permute-done | bytes 280608 | tf_op jit(solution)/shard_map/ppermute | solution.py:509
  13.9 0.7 %near_step0.1 = (f32[137,4,128]{2,1,0:T(4,128)S(1)}, f32[137,4,128]{2,1,0:T(4,128)S(1)}, f32[137,4,128]{2,1,0:T(4,128)S(1)}) custom-call(f32[4,137,4,128]{3,2,1,0:T(4,128)S(1)} %get-tuple-element.28.own, f32[137,4,128]{2,1,0:T(4,128)S(1)} %collective-permute-done.near_in, f32[137,4,137]{2,1,0:T(4,128)S(1)} %get-tuple-element.31.inverse, ...), custom_call_target="tpu_custom_call" | custom-call | flops 300000000 | bytes 1000000 | tf_op jit(solution)/shard_map/near_step0/pallas_call | solution.py:118
  14.5 0.0 collective-permute-done.3.refs_1_
  14.6 0.0 collective-permute-done.4.refs_2_
  14.6 1.0 %core_step0.1 = (f32[2,137,4,128]{3,2,1,0:T(4,128)S(1)}, f32[2,137,4,128]{3,2,1,0:T(4,128)S(1)}) custom-call(f32[4,137,4,128]{3,2,1,0:T(4,128)S(1)} %get-tuple-element.28.own, f32[137,4,137]{2,1,0:T(4,128)S(1)} %get-tuple-element.31.inverse, s32[2,4,512]{2,1,0:T(4,128)S(1)} %get-tuple-element.26.targets, f32[2,4,512]{2,1,0:T(4,128)S(1)} %get-tuple-element.27.weights, ...), custom_call_target="tpu_custom_call" | custom-call | flops 300000000 | bytes 1000000 | tf_op jit(solution)/shard_map/core_step0/pallas_call | solution.py:118
  15.6 0.1 collective-permute-start.5
  15.7 3.0 %collective-permute-start.6 = (f32[137,4,128]{2,1,0:T(4,128)S(1)}, f32[137,4,128]{2,1,0:T(4,128)S(1)}, u32[]{:S(2)}, u32[]{:S(2)}) collective-permute-start(f32[137,4,128]{2,1,0:T(4,128)S(1)} %get-tuple-element.42), channel_id=1, source_target_pairs={{0,7},{1,2},{2,1},{3,4},{4,3},{5,6},{6,5},{7,0},{8,15},{9,10},{10,... | collective-permute-start | bytes 841736 | tf_op jit(solution)/shard_map/ppermute | solution.py:509
  18.6 2.8 %collective-permute-done.1.far_in = f32[137,4,128]{2,1,0:T(4,128)S(1)} collective-permute-done((f32[137,4,128]{2,1,0:T(4,128)S(1)}, f32[137,4,128]{2,1,0:T(4,128)S(1)}, u32[]{:S(2)}, u32[]{:S(2)}) %collective-permute-start.1) | collective-permute-done | bytes 280608 | tf_op jit(solution)/shard_map/ppermute | solution.py:509
  21.4 0.7 %far_step0.1 = (f32[137,4,128]{2,1,0:T(4,128)S(1)}, f32[137,4,128]{2,1,0:T(4,128)S(1)}) custom-call(f32[4,137,4,128]{3,2,1,0:T(4,128)S(1)} %get-tuple-element.28.own, f32[137,4,128]{2,1,0:T(4,128)S(1)} %collective-permute-done.1.far_in, f32[137,4,128]{2,1,0:T(4,128)S(1)} %get-tuple-element.32._.partial, f32[137,4,137]{2,1,0:T(4,128)S(1)} %get-tuple-element.31.inverse, ...), custom_call_target="tpu_custom_call" | custom-call | flops 300000000 | bytes 1000000 | tf_op jit(solution)/shard_map/far_step0/pallas_call | solution.py:118
  22.1 1.4 %collective-permute-start.7 = (f32[137,4,128]{2,1,0:T(4,128)S(1)}, f32[137,4,128]{2,1,0:T(4,128)S(1)}, u32[]{:S(2)}, u32[]{:S(2)}) collective-permute-start(f32[137,4,128]{2,1,0:T(4,128)S(1)} %get-tuple-element.44), channel_id=1, source_target_pairs={{0,7},{1,2},{2,1},{3,4},{4,3},{5,6},{6,5},{7,0},{8,15},{9,10},{10,... | collective-permute-start | bytes 841736 | tf_op jit(solution)/shard_map/ppermute | solution.py:509
  23.5 2.6 %outer_step0.1 = (f32[4,137,4,128]{3,2,1,0:T(4,128)S(1)}, f32[137,4,512]{2,1,0:T(4,128)}) custom-call(f32[4,137,4,128]{3,2,1,0:T(4,128)S(1)} %get-tuple-element.28.own, f32[137,4,128]{2,1,0:T(4,128)S(1)} %collective-permute-done.near_in, f32[137,4,128]{2,1,0:T(4,128)S(1)} %collective-permute-done.1.far_in, ...), custom_call_target="tpu_custom_call" | custom-call | flops 2000000000 | bytes 1000000 | tf_op jit(solution)/shard_map/outer_step0/pallas_call | solution.py:118
  26.2 1.3 %collective-permute-done.6.far_in = f32[137,4,128]{2,1,0:T(4,128)S(1)} collective-permute-done((f32[137,4,128]{2,1,0:T(4,128)S(1)}, f32[137,4,128]{2,1,0:T(4,128)S(1)}, u32[]{:S(2)}, u32[]{:S(2)}) %collective-permute-start.6) | collective-permute-done | bytes 280608 | tf_op jit(solution)/shard_map/ppermute | solution.py:509
  27.4 0.0 collective-permute-done.5.core_in
  27.4 0.5 %squares_of_most_blocks.1 = (f32[4,137,4,128]{3,2,1,0:T(4,128)S(1)}, f32[1,128]{1,0:T(1,128)S(1)}) custom-call(f32[4,137,4,128]{3,2,1,0:T(4,128)S(1)} %get-tuple-element.40.own, f32[2,137,4,128]{3,2,1,0:T(4,128)S(1)} %collective-permute-done.5.core_in, f32[137,4,128]{2,1,0:T(4,128)S(1)} %collective-permute-done.6.far_in), custom_call_target="tpu_custom_call" | custom-call | flops 1000000 | bytes 1000000 | tf_op jit(solution)/shard_map/squares_of_most_blocks/pallas_call | solution.py:118
  27.9 5.1 %collective-permute-done.7.near_in = f32[137,4,128]{2,1,0:T(4,128)S(1)} collective-permute-done((f32[137,4,128]{2,1,0:T(4,128)S(1)}, f32[137,4,128]{2,1,0:T(4,128)S(1)}, u32[]{:S(2)}, u32[]{:S(2)}) %collective-permute-start.7) | collective-permute-done | bytes 280608 | tf_op jit(solution)/shard_map/ppermute | solution.py:509
  33.0 0.1 squares_of_last_block.1.refs_0_
  33.1 0.1 collective-permute-start.8
  33.2 1.1 %collective-permute-done.8.refs_1_ = f32[1,128]{1,0:T(1,128)S(1)} collective-permute-done((f32[1,128]{1,0:T(1,128)S(1)}, f32[1,128]{1,0:T(1,128)S(1)}, u32[]{:S(2)}, u32[]{:S(2)}) %collective-permute-start.8) | collective-permute-done | bytes 544 | tf_op jit(solution)/shard_map/ppermute | solution.py:503
  34.3 2.0 %collective-permute-start.11 = (f32[1,128]{1,0:T(1,128)S(1)}, f32[1,128]{1,0:T(1,128)S(1)}, u32[]{:S(2)}, u32[]{:S(2)}) collective-permute-start(f32[1,128]{1,0:T(1,128)S(1)} %add_shares.1.refs_0_), channel_id=1, source_target_pairs={{0,6},{1,7},{2,4},{3,5},{4,2},{5,3},{6,0},{7,1},{8,14},{9,15},{10,... | collective-permute-start | bytes 1544 | tf_op jit(solution)/shard_map/ppermute | solution.py:498
  36.3 0.0 collective-permute-start.10
  36.3 2.4 %collective-permute-start.9 = (f32[1,128]{1,0:T(1,128)S(1)}, f32[1,128]{1,0:T(1,128)S(1)}, u32[]{:S(2)}, u32[]{:S(2)}) collective-permute-start(f32[1,128]{1,0:T(1,128)S(1)} %add_shares.1.refs_0_), channel_id=1, source_target_pairs={{0,2},{1,3},{2,0},{3,1},{4,6},{5,7},{6,4},{7,5},{8,10},{9,11},{10,... | collective-permute-start | bytes 1544 | tf_op jit(solution)/shard_map/ppermute | solution.py:498
  38.7 0.9 %collective-permute-done.11.refs_3_ = f32[1,128]{1,0:T(1,128)S(1)} collective-permute-done((f32[1,128]{1,0:T(1,128)S(1)}, f32[1,128]{1,0:T(1,128)S(1)}, u32[]{:S(2)}, u32[]{:S(2)}) %collective-permute-start.11) | collective-permute-done | bytes 544 | tf_op jit(solution)/shard_map/ppermute | solution.py:498
  39.6 1.1 %collective-permute-done.10.refs_2_ = f32[1,128]{1,0:T(1,128)S(1)} collective-permute-done((f32[1,128]{1,0:T(1,128)S(1)}, f32[1,128]{1,0:T(1,128)S(1)}, u32[]{:S(2)}, u32[]{:S(2)}) %collective-permute-start.10) | collective-permute-done | bytes 544 | tf_op jit(solution)/shard_map/ppermute | solution.py:498
  40.8 0.0 collective-permute-done.9.refs_1_
  40.8 1.2 %scale_start.1 = f32[137,4,512]{2,1,0:T(4,128)} custom-call(f32[4,137,4,128]{3,2,1,0:T(4,128)S(1)} %get-tuple-element.43.start, f32[137,4,128]{2,1,0:T(4,128)S(1)} %collective-permute-done.7.near_in, f32[1,128]{1,0:T(1,128)S(1)} %add_shares.1.refs_0_, f32[1,128]{1,0:T(1,128)S(1)} %collective-permute-done.9.refs_1_, ...), custom_call_target="tpu_custom_call" | custom-call | flops 1000000 | bytes 1000000 | tf_op jit(solution)/shard_map/scale_start/pallas_call | solution.py:118
  (2 shorter events, 0.0 us)
Async XLA Ops:
  2.9 11.0 %collective-permute-start = (f32[137,4,128]{2,1,0:T(4,128)S(1)}, f32[137,4,128]{2,1,0:T(4,128)S(1)}, u32[]{:S(2)}, u32[]{:S(2)}) collective-permute-start(f32[137,4,128]{2,1,0:T(4,128)S(1)} %get-tuple-element.29), channel_id=1, source_target_pairs={{0,7},{1,2},{2,1},{3,4},{4,3},{5,6},{6,5},{7,0},{8,15},{9,10},{10,... | collective-permute-start | bytes 841736 | tf_op jit(solution)/shard_map/ppermute | solution.py:509
  10.5 4.1 %collective-permute-start.3 = (f32[2,46,4,128]{3,2,1,0:T(4,128)S(1)}, f32[2,46,4,128]{3,2,1,0:T(4,128)S(1)}, u32[]{:S(2)}, u32[]{:S(2)}) collective-permute-start(f32[2,46,4,128]{3,2,1,0:T(4,128)S(1)} %get-tuple-element.34), channel_id=1, source_target_pairs={{0,1},{1,0},{2,3},{3,2},{4,5},{5,4},{6,7},{7,6},{8,9},{9,8},{10,11... | collective-permute-start | bytes 565256 | tf_op jit(solution)/shard_map/ppermute | solution.py:503
  10.6 4.0 %collective-permute-start.4 = (f32[2,46,4,128]{3,2,1,0:T(4,128)S(1)}, f32[2,46,4,128]{3,2,1,0:T(4,128)S(1)}, u32[]{:S(2)}, u32[]{:S(2)}) collective-permute-start(f32[2,46,4,128]{3,2,1,0:T(4,128)S(1)} %get-tuple-element.35), channel_id=1, source_target_pairs={{0,1},{1,0},{2,3},{3,2},{4,5},{5,4},{6,7},{7,6},{8,9},{9,8},{10,11... | collective-permute-start | bytes 565256 | tf_op jit(solution)/shard_map/ppermute | solution.py:503
  11.0 3.5 %collective-permute-start.2 = (f32[2,45,4,128]{3,2,1,0:T(4,128)S(1)}, f32[2,45,4,128]{3,2,1,0:T(4,128)S(1)}, u32[]{:S(2)}, u32[]{:S(2)}) collective-permute-start(f32[2,45,4,128]{3,2,1,0:T(4,128)S(1)} %get-tuple-element.33), channel_id=1, source_target_pairs={{0,1},{1,0},{2,3},{3,2},{4,5},{5,4},{6,7},{7,6},{8,9},{9,8},{10,11... | collective-permute-start | bytes 552968 | tf_op jit(solution)/shard_map/ppermute | solution.py:503
  11.1 10.3 %collective-permute-start.1 = (f32[137,4,128]{2,1,0:T(4,128)S(1)}, f32[137,4,128]{2,1,0:T(4,128)S(1)}, u32[]{:S(2)}, u32[]{:S(2)}) collective-permute-start(f32[137,4,128]{2,1,0:T(4,128)S(1)} %get-tuple-element.30), channel_id=1, source_target_pairs={{0,7},{1,2},{2,1},{3,4},{4,3},{5,6},{6,5},{7,0},{8,15},{9,10},{10,... | collective-permute-start | bytes 841736 | tf_op jit(solution)/shard_map/ppermute | solution.py:509
  15.6 11.8 %collective-permute-start.5 = (f32[2,137,4,128]{3,2,1,0:T(4,128)S(1)}, f32[2,137,4,128]{3,2,1,0:T(4,128)S(1)}, u32[]{:S(2)}, u32[]{:S(2)}) collective-permute-start(f32[2,137,4,128]{3,2,1,0:T(4,128)S(1)} %get-tuple-element.41), channel_id=1, source_target_pairs={{0,1},{1,0},{2,3},{3,2},{4,5},{5,4},{6,7},{7,6},{8,9},{9,8},{10,11... | collective-permute-start | bytes 1683464 | tf_op jit(solution)/shard_map/ppermute | solution.py:503
  15.7 11.8 %collective-permute-start.6 = (f32[137,4,128]{2,1,0:T(4,128)S(1)}, f32[137,4,128]{2,1,0:T(4,128)S(1)}, u32[]{:S(2)}, u32[]{:S(2)}) collective-permute-start(f32[137,4,128]{2,1,0:T(4,128)S(1)} %get-tuple-element.42), channel_id=1, source_target_pairs={{0,7},{1,2},{2,1},{3,4},{4,3},{5,6},{6,5},{7,0},{8,15},{9,10},{10,... | collective-permute-start | bytes 841736 | tf_op jit(solution)/shard_map/ppermute | solution.py:509
  22.1 10.9 %collective-permute-start.7 = (f32[137,4,128]{2,1,0:T(4,128)S(1)}, f32[137,4,128]{2,1,0:T(4,128)S(1)}, u32[]{:S(2)}, u32[]{:S(2)}) collective-permute-start(f32[137,4,128]{2,1,0:T(4,128)S(1)} %get-tuple-element.44), channel_id=1, source_target_pairs={{0,7},{1,2},{2,1},{3,4},{4,3},{5,6},{6,5},{7,0},{8,15},{9,10},{10,... | collective-permute-start | bytes 841736 | tf_op jit(solution)/shard_map/ppermute | solution.py:509
  33.1 1.2 %collective-permute-start.8 = (f32[1,128]{1,0:T(1,128)S(1)}, f32[1,128]{1,0:T(1,128)S(1)}, u32[]{:S(2)}, u32[]{:S(2)}) collective-permute-start(f32[1,128]{1,0:T(1,128)S(1)} %squares_of_last_block.1.refs_0_), channel_id=1, source_target_pairs={{0,1},{1,0},{2,3},{3,2},{4,5},{5,4},{6,7},{7,6},{8,9},{9,8},{10,11... | collective-permute-start | bytes 1544 | tf_op jit(solution)/shard_map/ppermute | solution.py:503
  34.3 5.3 %collective-permute-start.11 = (f32[1,128]{1,0:T(1,128)S(1)}, f32[1,128]{1,0:T(1,128)S(1)}, u32[]{:S(2)}, u32[]{:S(2)}) collective-permute-start(f32[1,128]{1,0:T(1,128)S(1)} %add_shares.1.refs_0_), channel_id=1, source_target_pairs={{0,6},{1,7},{2,4},{3,5},{4,2},{5,3},{6,0},{7,1},{8,14},{9,15},{10,... | collective-permute-start | bytes 1544 | tf_op jit(solution)/shard_map/ppermute | solution.py:498
  36.3 4.4 %collective-permute-start.10 = (f32[1,128]{1,0:T(1,128)S(1)}, f32[1,128]{1,0:T(1,128)S(1)}, u32[]{:S(2)}, u32[]{:S(2)}) collective-permute-start(f32[1,128]{1,0:T(1,128)S(1)} %add_shares.1.refs_0_), channel_id=1, source_target_pairs={{0,4},{1,5},{2,6},{3,7},{4,0},{5,1},{6,2},{7,3},{8,12},{9,13},{10,... | collective-permute-start | bytes 1544 | tf_op jit(solution)/shard_map/ppermute | solution.py:498
  36.3 4.4 %collective-permute-start.9 = (f32[1,128]{1,0:T(1,128)S(1)}, f32[1,128]{1,0:T(1,128)S(1)}, u32[]{:S(2)}, u32[]{:S(2)}) collective-permute-start(f32[1,128]{1,0:T(1,128)S(1)} %add_shares.1.refs_0_), channel_id=1, source_target_pairs={{0,2},{1,3},{2,0},{3,1},{4,6},{5,7},{6,4},{7,5},{8,10},{9,11},{10,... | collective-permute-start | bytes 1544 | tf_op jit(solution)/shard_map/ppermute | solution.py:498

commit v7 on v6

--- a/solution.py
+++ b/solution.py
@@ -84,12 +84,12 @@
     return ref.reshape(levels * variables, columns)
 
 
-def diffuse(inverse, field, out):
+def diffuse(turned, field, out):
     levels, variables, columns = field.shape
     source, result = rows_of(field), rows_of(out)
     every = [pl.ds(v, levels, stride=variables) for v in range(variables)]
     wide = split(jnp.concatenate([source[rows, :] for rows in every], axis=1))
-    turned = split(inverse.T)
+    turned = split(turned)
     dims = ((1,), (0,))
     total = product(turned[0], wide[0], dims) + (
         product(turned[0], wide[1], dims) + product(turned[1], wide[0], dims)
@@ -122,7 +122,7 @@
         out_specs=out_specs,
         scratch_shapes=scratch,
         compiler_params=pltpu.CompilerParams(vmem_limit_bytes=limit),
-        cost_estimate=pl.CostEstimate(flops=flops, bytes_accessed=1_000_000, transcendentals=0),
+        cost_estimate=pl.CostEstimate(flops=flops, bytes_accessed=min(flops, 1_000_000), transcendentals=0),
         name=name,
     )(*operands)
 
@@ -162,7 +162,7 @@
     copies[3].wait()
     for j, block in enumerate((near, far)):
         copies[4 + j].wait()
-        diffuse(inverse[:, block, :], field.at[j], diffused.at[j])
+        diffuse(inverse[:, block, :].T, field.at[j], diffused.at[j])
     sums = spread([diffused.at[0], diffused.at[1]], matrix)
     rows_of(to_near)[...] = sums[:, :BCOLS]
     rows_of(to_far)[...] = sums[:, BCOLS:]
@@ -170,6 +170,26 @@
 
 def level_pieces(levels):
     return [slice(levels * part // PIECES, levels * (part + 1) // PIECES) for part in range(PIECES)]
+
+
+def piece_shapes(whole):
+    return [
+        jax.ShapeDtypeStruct((whole.shape[0], levels.stop - levels.start, *whole.shape[2:]), F32)
+        for levels in level_pieces(whole.shape[1])
+    ]
+
+
+def store_pieces(sums, pieces, levels):
+    for piece, part in zip(pieces, level_pieces(levels)):
+        variables = piece.shape[2]
+        rows = slice(part.start * variables, part.stop * variables)
+        for j in range(REACH):
+            rows_of(piece.at[j])[...] = sums[rows, j * BCOLS : (j + 1) * BCOLS]
+
+
+def add_pieces(pieces, block, out):
+    for piece, levels in zip(pieces, level_pieces(out.shape[0])):
+        out[levels] += piece[block]
 
 
 def blocks(like, *count):
@@ -203,12 +223,9 @@
     )
 
 
-def inner_kernel(
-    step, fields, z_diffused, inverse, targets, weights, inverses, own, next_inverse, *refs
-):
-    to_core, (field, tall, sems) = refs[:-3], refs[-3:]
+def side_kernel(step, fields, inverse, targets, weights, inverses, diffused, turned, *refs):
+    to_core, (field, next_inverse, sems) = refs[:-3], refs[-3:]
     block_count = inverse.shape[1]
-    near, far, _, _ = z_blocks(block_count)
     side, first_target = core_side(block_count)
     copies = start_copies(
         sems,
@@ -216,87 +233,70 @@
         + [(inverses.at[step - 1], next_inverse)],
     )
     columns = (first_target * BCOLS, (first_target + 1) * BCOLS)
-    core_matrix = side_matrix(targets, weights, step, (side, side + 1), columns)
-    matrix = spread_matrix(targets[step], weights[step], 0, block_count * BCOLS)
+    matrix = side_matrix(targets, weights, step, (side, side + 1), columns)
+    for j in range(REACH):
+        copies[j].wait()
+        diffuse(inverse[:, side + j, :].T, field.at[j], diffused.at[j])
+    store_pieces(spread([diffused.at[j] for j in range(REACH)], matrix), to_core, field.shape[1])
+    copies[REACH].wait()
+    for j in range(block_count):
+        turned[j] = next_inverse[:, j, :].T
+
+
+def side(step, fields, inverse, targets, weights, inverses):
+    two = blocks(fields, REACH)
+    levels, block_count, _ = inverse.shape
+    diffused, turned, *pieces = call(
+        functools.partial(side_kernel, step),
+        (fields, inverse, targets, weights, inverses),
+        [HBM] + [VMEM] * 3 + [HBM],
+        (two, jax.ShapeDtypeStruct((block_count, levels, levels), F32), *piece_shapes(two)),
+        (VMEM,) * (2 + PIECES),
+        [
+            pltpu.VMEM(two.shape, F32),
+            pltpu.VMEM(inverse.shape, F32),
+            pltpu.SemaphoreType.DMA((REACH + 1,)),
+        ],
+        2_000_000_000,
+        f"side_step{step}",
+    )
+    return diffused, turned, pieces
+
+
+def inner_kernel(step, z_diffused, core_diffused, targets, weights, own, tall):
+    block_count = own.shape[0]
+    near, far, _, _ = z_blocks(block_count)
+    first = core_side(block_count)[0]
     tall[near] = z_diffused[0]
     tall[far] = z_diffused[1]
     for j in range(REACH):
-        copies[j].wait()
-        diffuse(inverse[:, side + j, :], field.at[j], tall.at[side + j])
-    sums = spread([tall.at[side + j] for j in range(REACH)], core_matrix)
-    variables = field.shape[2]
-    for piece, levels in zip(to_core, level_pieces(field.shape[1])):
-        rows = slice(levels.start * variables, levels.stop * variables)
-        for j in range(REACH):
-            rows_of(piece.at[j])[...] = sums[rows, j * BCOLS : (j + 1) * BCOLS]
+        tall[first + j] = core_diffused[j]
+    matrix = spread_matrix(targets[step], weights[step], 0, block_count * BCOLS)
     sums = spread([tall.at[j] for j in range(block_count)], matrix)
     for j in range(block_count):
         rows_of(own.at[j])[...] = sums[:, j * BCOLS : (j + 1) * BCOLS]
-    copies[REACH].wait()
-
-
-def inner(step, fields, z_diffused, inverse, targets, weights, inverses):
-    two, whole = blocks(fields, REACH), blocks(fields, inverse.shape[1])
-    pieces = [
-        jax.ShapeDtypeStruct((REACH, levels.stop - levels.start, *two.shape[2:]), F32)
-        for levels in level_pieces(fields.shape[0])
-    ]
-    own, inverse, *pieces = call(
+
+
+def inner(step, z_diffused, core_diffused, targets, weights):
+    whole = blocks(z_diffused, targets.shape[2] // BCOLS)
+    return call(
         functools.partial(inner_kernel, step),
-        (fields, z_diffused, inverse, targets, weights, inverses),
-        [HBM] + [VMEM] * 4 + [HBM],
-        (whole, jax.ShapeDtypeStruct(inverse.shape, F32), *pieces),
-        (VMEM,) * (2 + PIECES),
-        [
-            pltpu.VMEM(two.shape, F32),
-            pltpu.VMEM(whole.shape, F32),
-            pltpu.SemaphoreType.DMA((REACH + 1,)),
-        ],
+        (z_diffused, core_diffused, targets, weights),
+        [VMEM] * 4,
+        whole,
+        VMEM,
+        [pltpu.VMEM(whole.shape, F32)],
         2_000_000_000,
         f"inner_step{step}",
     )
-    return own, inverse, pieces
-
-
-def add_pieces(pieces, block, out):
-    for piece, levels in zip(pieces, level_pieces(out.shape[0])):
-        out[levels] += piece[block]
-
-
-def core_kernel(step, own, inverse, targets, weights, _, *refs):
-    core_in, (to_core, diffused, field) = refs[:PIECES], refs[PIECES:]
-    side, first_target = core_side(own.shape[0])
-    columns = (first_target * BCOLS, (first_target + 1) * BCOLS)
-    matrix = side_matrix(targets, weights, step, (side, side + 1), columns)
-    for j in range(REACH):
-        field[j] = own[side + j]
-        add_pieces(core_in, j, field.at[j])
-        diffuse(inverse[:, side + j, :], field.at[j], diffused.at[j])
-    sums = spread([diffused.at[j] for j in range(REACH)], matrix)
-    for j in range(REACH):
-        rows_of(to_core.at[j])[...] = sums[:, j * BCOLS : (j + 1) * BCOLS]
-
-
-def core(step, own, core_in, inverse, targets, weights, behind):
-    two = blocks(own, REACH)
-    return call(
-        functools.partial(core_kernel, step),
-        (own, inverse, targets, weights, behind, *core_in),
-        [VMEM] * 4 + [ANY] + [VMEM] * PIECES,
-        (two, two),
-        (VMEM,) * 2,
-        [pltpu.VMEM(two.shape, F32)],
-        300_000_000,
-        f"core_step{step}",
-    )
-
-
-def near_kernel(step, own, near_in, inverse, targets, weights, to_far, to_near, diffused, field):
-    block_count = inverse.shape[1]
+
+
+def near_kernel(step, own, near_in, turned, targets, weights, to_far, to_near, diffused, field):
+    block_count = own.shape[0]
     near, _, target_near, target_far = z_blocks(block_count)
     cols = lanes(near)
     field[...] = own[near] + near_in[...]
-    diffuse(inverse[:, near, :], field, diffused)
+    diffuse(turned[near], field, diffused)
     halves = [
         spread_matrix(targets[step, :, cols], weights[step, :, cols], target * BCOLS)
         for target in (target_far, target_near)
@@ -306,11 +306,11 @@
     rows_of(to_near)[...] = sums[:, BCOLS:]
 
 
-def near(step, own, near_in, inverse, targets, weights):
+def near(step, own, near_in, turned, targets, weights):
     one = blocks(own)
     return call(
         functools.partial(near_kernel, step),
-        (own, near_in, inverse, targets, weights),
+        (own, near_in, turned, targets, weights),
         [VMEM] * 5,
         (one, one, one),
         (VMEM,) * 3,
@@ -320,28 +320,55 @@
     )
 
 
-def far_kernel(step, own, far_in, partial, inverse, targets, weights, _, to_near, diffused, field):
-    block_count = inverse.shape[1]
+def far_kernel(step, own, far_in, partial, turned, targets, weights, to_near, diffused, field):
+    block_count = own.shape[0]
     _, far, target_near, _ = z_blocks(block_count)
     cols = lanes(far)
     field[...] = own[far] + far_in[...]
-    diffuse(inverse[:, far, :], field, diffused)
+    diffuse(turned[far], field, diffused)
     matrix = spread_matrix(targets[step, :, cols], weights[step, :, cols], target_near * BCOLS)
     rows_of(to_near)[...] = rows_of(partial)[...] + spread([diffused], matrix)
 
 
-def far(step, own, far_in, partial, inverse, targets, weights, behind):
+def far(step, own, far_in, partial, turned, targets, weights):
     one = blocks(own)
     return call(
         functools.partial(far_kernel, step),
-        (own, far_in, partial, inverse, targets, weights, behind),
-        [VMEM] * 6 + [ANY],
+        (own, far_in, partial, turned, targets, weights),
+        [VMEM] * 6,
         (one, one),
         (VMEM,) * 2,
         [pltpu.VMEM(one.shape, F32)],
         300_000_000,
         f"far_step{step}",
     )
+
+
+def core_kernel(step, own, turned, targets, weights, _, *refs):
+    core_in, (diffused, *to_core, field) = refs[:PIECES], refs[PIECES:]
+    side, first_target = core_side(own.shape[0])
+    columns = (first_target * BCOLS, (first_target + 1) * BCOLS)
+    matrix = side_matrix(targets, weights, step, (side, side + 1), columns)
+    for j in range(REACH):
+        field[...] = own[side + j]
+        add_pieces(core_in, j, field)
+        diffuse(turned[side + j], field, diffused.at[j])
+    store_pieces(spread([diffused.at[j] for j in range(REACH)], matrix), to_core, own.shape[1])
+
+
+def core(step, own, turned, targets, weights, core_in, behind):
+    one, two = blocks(own), blocks(own, REACH)
+    diffused, *to_core = call(
+        functools.partial(core_kernel, step),
+        (own, turned, targets, weights, behind, *core_in),
+        [VMEM] * 4 + [ANY] + [VMEM] * PIECES,
+        (two, *piece_shapes(two)),
+        (VMEM,) * (1 + PIECES),
+        [pltpu.VMEM(one.shape, F32)],
+        1,
+        f"core_step{step}",
+    )
+    return diffused, to_core
 
 
 def outer_kernel(
@@ -384,7 +411,7 @@
             pltpu.VMEM(own.shape, F32),
             pltpu.SemaphoreType.DMA((block_count,)),
         ],
-        2_000_000_000,
+        1,
         f"outer_step{step}",
     )
 
@@ -394,7 +421,8 @@
     return jnp.sum(rows * rows, axis=0, keepdims=True)
 
 
-def most_kernel(own, core_in, far_in, start, lane_sums):
+def most_kernel(own, far_in, *refs):
+    core_in, (start, lane_sums) = refs[:PIECES], refs[PIECES:]
     block_count = own.shape[0]
     near, far, _, _ = z_blocks(block_count)
     side = core_side(block_count)[0]
@@ -403,17 +431,17 @@
     start[near] = own[near]
     total = squares(value)
     for j in range(REACH):
-        value = own[side + j] + core_in[j]
-        start[side + j] = value
-        total += squares(value)
+        start[side + j] = own[side + j]
+        add_pieces(core_in, j, start.at[side + j])
+        total += squares(start[side + j])
     lane_sums[...] = total
 
 
 def most(own, core_in, far_in):
     return call(
         most_kernel,
-        (own, core_in, far_in),
-        [VMEM] * 3,
+        (own, far_in, *core_in),
+        [VMEM] * (2 + PIECES),
         (jax.ShapeDtypeStruct(own.shape, F32), jax.ShapeDtypeStruct((1, BCOLS), F32)),
         (VMEM, VMEM),
         [],
@@ -492,11 +520,12 @@
 
 def share_out(share):
     count = lax.axis_size("col")
-    if count > 8:
+    if count != 8:
         return [lax.all_to_all(jnp.broadcast_to(share, (count, BCOLS)), "col", 0, 0, tiled=True)]
     share = add([share, core_exchange(share)])
-    return [share] + [lax.ppermute(share, "col", [(i, i ^ s) for i in range(count)]) for s in (2, 4, 6)]
-
+    beside = lax.ppermute(share, "col", [(i, i ^ (6 if i % 2 else 6)) for i in range(count)])
+    apart = lax.ppermute(share, "col", [(i, i ^ (4 if i % 2 else 2)) for i in range(count)])
+    return [share, beside, apart, core_exchange(apart)]
 
 def core_exchange(value):
     count = lax.axis_size("col")
@@ -524,15 +553,16 @@
     )
     near_in = z_exchange(to_near)
     far_in = z_exchange(to_far)
-    own, inverse, pieces = inner(1, fields, z_diffused, inverse, targets, merged, inverses)
+    core_diffused, turned, pieces = side(1, fields, inverse, targets, merged, inverses)
     core_in = [core_exchange(piece) for piece in pieces]
-
-    to_far, partial, diffused_near = near(0, own, near_in, inverse, targets, merged)
+    own = inner(1, z_diffused, core_diffused, targets, merged)
+
+    to_far, partial, diffused_near = near(0, own, near_in, turned, targets, merged)
     next_far_in = z_exchange(to_far)
-    to_core, diffused_core = core(0, own, core_in, inverse, targets, merged, partial)
-    next_core_in = core_exchange(to_core)
-    to_near, diffused_far = far(0, own, far_in, partial, inverse, targets, merged, diffused_core)
+    to_near, diffused_far = far(0, own, far_in, partial, turned, targets, merged)
     next_near_in = z_exchange(to_near)
+    diffused_core, pieces = core(0, own, turned, targets, merged, core_in, to_near)
+    next_core_in = [core_exchange(piece) for piece in pieces]
     diffused = (diffused_core, diffused_near, diffused_far)
     own, mid = outer(0, own, near_in, far_in, core_in, diffused, targets, merged)
 

time: 42.2 us -> 40.7 us (0.964)
  waiting for transfers between devices: 14.5 us -> 10.6 us
  starting transfers between devices: 14.8 us -> 16.7 us
    ppermute x4, waiting for transfers between devices: 11.3 us -> 7 us  [z_exchange(): return lax.ppermute(value, 'col', pairs)]
    ppermute x4, starting transfers between devices: 9.6 us -> 12.2 us  [z_exchange(): return lax.ppermute(value, 'col', pairs)]
    ppermute x3 -> x2, starting transfers between devices: 4.39 us -> 3.13 us  [the longest x1 2.82 us: share_out(): lax.ppermute(share, 'col', [(i, i ^ (6 if i % 2 else 6)) for i in range(c...]
    ppermute x5 -> x8, starting transfers between devices: 0.78 us -> 1.36 us  [core_exchange(): return lax.ppermute(value, 'col', [(i, i ^ 1) for i in range(count)])]
    pallas_call x10 -> x11, Pallas kernels: 12 us -> 12.4 us  [call(): pl.pallas_call(kernel, out_shape=outs, in_specs=in_specs, out_specs=out_s...]
    ppermute x3 -> x2, waiting for transfers between devices: 2.09 us -> 2.51 us  [the longest x1 2.1 us: share_out(): lax.ppermute(share, 'col', [(i, i ^ (6 if i % 2 else 6)) for i in range(c...]
    ppermute x5 -> x8, waiting for transfers between devices: 1.12 us -> 1.13 us  [core_exchange(): return lax.ppermute(value, 'col', [(i, i ^ 1) for i in range(count)])]
  transfers between devices with their start and end apart: 12 -> 14, of which waited for: 7 -> 6; matrix products, arithmetic and copies ran while one was open for 0% -> 0% of each run, Pallas kernels for 20% -> 22%
where the time goes in v7:
time: 40.7 us; the launch traced here: 40.5 us
  starting transfers between devices  16.7 us (41%)
  Pallas kernels  12.4 us (30%)
  waiting for transfers between devices  10.6 us (26%)
  between operations  0.75 us (2%)
    pallas_call x11, Pallas kernels, call(): pl.pallas_call(kernel, out_shape=outs, in_specs=in_specs, out_specs=out_s...  12.4 us
    ppermute x4, starting transfers between devices, z_exchange(): return lax.ppermute(value, 'col', pairs)  12.2 us
    ppermute x4, waiting for transfers between devices, z_exchange(): return lax.ppermute(value, 'col', pairs)  7 us
    ppermute x1, starting transfers between devices, share_out(): lax.ppermute(share, 'col', [(i, i ^ (6 if i % 2 else 6)) for i in range(c...  2.82 us
    ppermute x1, waiting for transfers between devices, share_out(): lax.ppermute(share, 'col', [(i, i ^ (6 if i % 2 else 6)) for i in range(c...  2.1 us
    ppermute x8, starting transfers between devices, core_exchange(): return lax.ppermute(value, 'col', [(i, i ^ 1) for i in range(count)])  1.36 us
    ppermute x8, waiting for transfers between devices, core_exchange(): return lax.ppermute(value, 'col', [(i, i ^ 1) for i in range(count)])  1.13 us
  transfers between devices with their start and end apart: 14, of which 6 were waited for; matrix products, arithmetic and copies ran while one was open for 0% of the time, Pallas kernels for 22%

profile of v7, /device:TPU:0, one launch (start us, length us, event | category | flops | bytes accessed | tf_op | source)
XLA Modules:
  0.0 40.5 jit_solution(6537960792987825349)
XLA Ops:
  0.6 2.3 %first_step1.1 = (f32[137,4,128]{2,1,0:T(4,128)S(1)}, f32[137,4,128]{2,1,0:T(4,128)S(1)}, f32[2,137,4,128]{3,2,1,0:T(4,128)S(1)}, f32[137,4,137]{2,1,0:T(4,128)S...) custom-call(f32[137,4,512]{2,1,0:T(4,128)} %bitcast.5, f32[2,137,4,137]{3,2,1,0:T(4,128)} %bitcast.7, ...), custom_call_target="tpu_custom_call" | custom-call | flops 400000000 | bytes 1000000 | tf_op jit(solution)/shard_map/first_step1/pallas_call | solution.py:118
  2.9 4.6 %collective-permute-start = (f32[137,4,128]{2,1,0:T(4,128)S(1)}, f32[137,4,128]{2,1,0:T(4,128)S(1)}, u32[]{:S(2)}, u32[]{:S(2)}) collective-permute-start(f32[137,4,128]{2,1,0:T(4,128)S(1)} %get-tuple-element.31), channel_id=1, source_target_pairs={{0,7},{1,2},{2,1},{3,4},{4,3},{5,6},{6,5},{7,0},{8,15},{9,10},{10,... | collective-permute-start | bytes 841736 | tf_op jit(solution)/shard_map/ppermute | solution.py:538
  7.4 0.1 collective-permute-start.1
  7.5 2.3 %side_step1.1 = (f32[2,137,4,128]{3,2,1,0:T(4,128)S(1)}, f32[4,137,137]{2,1,0:T(8,128)S(1)}, f32[2,45,4,128]{3,2,1,0:T(4,128)S(1)}, f32[2,46,4,128]{3,2,1,0:T(4,128)S(1)}, f32[2,46,4,128]{3,2,1,0:T(4,128)S(1)}) custom-call(f32[137,4,512]{2,1,0:T(4,128)} %bitcast.6, f32[137,4,137]{2,1,0:T(4,128)S(1)} %get-tuple-element.27.inverse, ...), custom_call_target="tpu_custom_call" | custom-call | flops 2000000000 | bytes 1000000 | tf_op jit(solution)/shard_map/side_step1/pallas_call | solution.py:118
  9.9 0.1 collective-permute-start.2
  9.9 0.5 %collective-permute-start.3 = (f32[2,46,4,128]{3,2,1,0:T(4,128)S(1)}, f32[2,46,4,128]{3,2,1,0:T(4,128)S(1)}, u32[]{:S(2)}, u32[]{:S(2)}) collective-permute-start(f32[2,46,4,128]{3,2,1,0:T(4,128)S(1)} %get-tuple-element.37), channel_id=1, source_target_pairs={{0,1},{1,0},{2,3},{3,2},{4,5},{5,4},{6,7},{7,6},{8,9},{9,8},{10,11... | collective-permute-start | bytes 565256 | tf_op jit(solution)/shard_map/ppermute | solution.py:532
  10.4 0.1 collective-permute-start.4
  10.5 1.3 %inner_step1.1.own = f32[4,137,4,128]{3,2,1,0:T(4,128)S(1)} custom-call(f32[2,137,4,128]{3,2,1,0:T(4,128)S(1)} %get-tuple-element.26.z_diffused, f32[2,137,4,128]{3,2,1,0:T(4,128)S(1)} %get-tuple-element.30.core_diffused, s32[2,4,512]{2,1,0:T(4,128)S(1)} %get-tuple-element.28.targets, f32[2,4,512]{2,1,0:T(4,128)S(1)} %get-tuple-element.29.weights), custom_call_target="tpu_custom_call" | custom-call | flops 2000000000 | bytes 1000000 | tf_op jit(solution)/shard_map/inner_step1/pallas_call | solution.py:118
  11.9 2.7 %collective-permute-done.near_in = f32[137,4,128]{2,1,0:T(4,128)S(1)} collective-permute-done((f32[137,4,128]{2,1,0:T(4,128)S(1)}, f32[137,4,128]{2,1,0:T(4,128)S(1)}, u32[]{:S(2)}, u32[]{:S(2)}) %collective-permute-start) | collective-permute-done | bytes 280608 | tf_op jit(solution)/shard_map/ppermute | solution.py:538
  14.6 0.6 %near_step0.1 = (f32[137,4,128]{2,1,0:T(4,128)S(1)}, f32[137,4,128]{2,1,0:T(4,128)S(1)}, f32[137,4,128]{2,1,0:T(4,128)S(1)}) custom-call(f32[4,137,4,128]{3,2,1,0:T(4,128)S(1)} %inner_step1.1.own, f32[137,4,128]{2,1,0:T(4,128)S(1)} %collective-permute-done.near_in, f32[4,137,137]{2,1,0:T(8,128)S(1)} %get-tuple-element.33.turned, ...), custom_call_target="tpu_custom_call" | custom-call | flops 300000000 | bytes 1000000 | tf_op jit(solution)/shard_map/near_step0/pallas_call | solution.py:118
  15.2 3.8 %collective-permute-start.5 = (f32[137,4,128]{2,1,0:T(4,128)S(1)}, f32[137,4,128]{2,1,0:T(4,128)S(1)}, u32[]{:S(2)}, u32[]{:S(2)}) collective-permute-start(f32[137,4,128]{2,1,0:T(4,128)S(1)} %get-tuple-element.44), channel_id=1, source_target_pairs={{0,7},{1,2},{2,1},{3,4},{4,3},{5,6},{6,5},{7,0},{8,15},{9,10},{10,... | collective-permute-start | bytes 841736 | tf_op jit(solution)/shard_map/ppermute | solution.py:538
  19.0 1.6 %collective-permute-done.1.far_in = f32[137,4,128]{2,1,0:T(4,128)S(1)} collective-permute-done((f32[137,4,128]{2,1,0:T(4,128)S(1)}, f32[137,4,128]{2,1,0:T(4,128)S(1)}, u32[]{:S(2)}, u32[]{:S(2)}) %collective-permute-start.1) | collective-permute-done | bytes 280608 | tf_op jit(solution)/shard_map/ppermute | solution.py:538
  20.6 0.6 %far_step0.1 = (f32[137,4,128]{2,1,0:T(4,128)S(1)}, f32[137,4,128]{2,1,0:T(4,128)S(1)}) custom-call(f32[4,137,4,128]{3,2,1,0:T(4,128)S(1)} %inner_step1.1.own, f32[137,4,128]{2,1,0:T(4,128)S(1)} %collective-permute-done.1.far_in, f32[137,4,128]{2,1,0:T(4,128)S(1)} %get-tuple-element.34.partial, f32[4,137,137]{2,1,0:T(8,128)S(1)} %get-tuple-element.33.turned, ...), custom_call_target="tpu_custom_call" | custom-call | flops 300000000 | bytes 1000000 | tf_op jit(solution)/shard_map/far_step0/pallas_call | solution.py:118
  21.2 3.8 %collective-permute-start.9 = (f32[137,4,128]{2,1,0:T(4,128)S(1)}, f32[137,4,128]{2,1,0:T(4,128)S(1)}, u32[]{:S(2)}, u32[]{:S(2)}) collective-permute-start(f32[137,4,128]{2,1,0:T(4,128)S(1)} %get-tuple-element.35._), channel_id=1, source_target_pairs={{0,7},{1,2},{2,1},{3,4},{4,3},{5,6},{6,5},{7,0},{8,15},{9,10},{10,... | collective-permute-start | bytes 841736 | tf_op jit(solution)/shard_map/ppermute | solution.py:538
  25.0 0.0 collective-permute-done.3.refs_1_
  25.0 0.0 collective-permute-done.4.refs_2_
  25.0 0.9 %core_step0.1 = (f32[2,137,4,128]{3,2,1,0:T(4,128)S(1)}, f32[2,45,4,128]{3,2,1,0:T(4,128)S(1)}, f32[2,46,4,128]{3,2,1,0:T(4,128)S(1)}, f32[2,46,4,128]{3,2,1,0:T(4,128)S(1)}) custom-call(f32[4,137,4,128]{3,2,1,0:T(4,128)S(1)} %inner_step1.1.own, f32[4,137,137]{2,1,0:T(8,128)S(1)} %get-tuple-element.33.turned, s32[2,4,512]{2,1,0:T(4,128)S(1)} %get-tuple-element.28.targets, ...), custom_call_target="tpu_custom_call" | custom-call | flops 1 | bytes 1 | tf_op jit(solution)/shard_map/core_step0/pallas_call | solution.py:118
  25.9 0.1 collective-permute-start.7
  26.0 0.5 %collective-permute-start.8 = (f32[2,46,4,128]{3,2,1,0:T(4,128)S(1)}, f32[2,46,4,128]{3,2,1,0:T(4,128)S(1)}, u32[]{:S(2)}, u32[]{:S(2)}) collective-permute-start(f32[2,46,4,128]{3,2,1,0:T(4,128)S(1)} %get-tuple-element.47), channel_id=1, source_target_pairs={{0,1},{1,0},{2,3},{3,2},{4,5},{5,4},{6,7},{7,6},{8,9},{9,8},{10,11... | collective-permute-start | bytes 565256 | tf_op jit(solution)/shard_map/ppermute | solution.py:532
  26.5 0.1 collective-permute-start.6
  26.6 2.6 %outer_step0.1 = (f32[4,137,4,128]{3,2,1,0:T(4,128)S(1)}, f32[137,4,512]{2,1,0:T(4,128)}) custom-call(f32[4,137,4,128]{3,2,1,0:T(4,128)S(1)} %inner_step1.1.own, f32[137,4,128]{2,1,0:T(4,128)S(1)} %collective-permute-done.near_in, f32[137,4,128]{2,1,0:T(4,128)S(1)} %collective-permute-done.1.far_in, f32[2,137,4,128]{3,2,1,0:T(4,128)S(1)} %get-tuple-element.39.diffused_core, ...), custom_call_target="tpu_custom_call" | custom-call | flops 1 | bytes 1 | tf_op jit(solution)/shard_map/outer_step0/pallas_call | solution.py:118
  29.2 0.0 collective-permute-done.7.refs_1_
  29.3 0.4 %squares_of_most_blocks.1 = (f32[4,137,4,128]{3,2,1,0:T(4,128)S(1)}, f32[1,128]{1,0:T(1,128)S(1)}) custom-call(f32[4,137,4,128]{3,2,1,0:T(4,128)S(1)} %get-tuple-element.43.own, f32[137,4,128]{2,1,0:T(4,128)S(1)} %collective-permute-done.5.far_in, f32[2,45,4,128]{3,2,1,0:T(4,128)S(1)} %collective-permute-done.6.refs_0_, ...), custom_call_target="tpu_custom_call" | custom-call | flops 1000000 | bytes 1000000 | tf_op jit(solution)/shard_map/squares_of_most_blocks/pallas_call | solution.py:118
  29.7 2.7 %collective-permute-done.9.near_in = f32[137,4,128]{2,1,0:T(4,128)S(1)} collective-permute-done((f32[137,4,128]{2,1,0:T(4,128)S(1)}, f32[137,4,128]{2,1,0:T(4,128)S(1)}, u32[]{:S(2)}, u32[]{:S(2)}) %collective-permute-start.9) | collective-permute-done | bytes 280608 | tf_op jit(solution)/shard_map/ppermute | solution.py:538
  32.4 0.1 squares_of_last_block.1.refs_0_
  32.4 0.1 collective-permute-start.10
  32.5 1.1 %collective-permute-done.10.refs_1_ = f32[1,128]{1,0:T(1,128)S(1)} collective-permute-done((f32[1,128]{1,0:T(1,128)S(1)}, f32[1,128]{1,0:T(1,128)S(1)}, u32[]{:S(2)}, u32[]{:S(2)}) %collective-permute-start.10) | collective-permute-done | bytes 544 | tf_op jit(solution)/shard_map/ppermute | solution.py:532
  33.6 0.3 collective-permute-start.12
  33.9 2.8 %collective-permute-start.11 = (f32[1,128]{1,0:T(1,128)S(1)}, f32[1,128]{1,0:T(1,128)S(1)}, u32[]{:S(2)}, u32[]{:S(2)}) collective-permute-start(f32[1,128]{1,0:T(1,128)S(1)} %add_shares.1.refs_0_), channel_id=1, source_target_pairs={{0,6},{1,7},{2,4},{3,5},{4,2},{5,3},{6,0},{7,1},{8,14},{9,15},{10,... | collective-permute-start | bytes 1544 | tf_op jit(solution)/shard_map/ppermute | solution.py:526
  36.8 0.4 %collective-permute-done.12.refs_2_ = f32[1,128]{1,0:T(1,128)S(1)} collective-permute-done((f32[1,128]{1,0:T(1,128)S(1)}, f32[1,128]{1,0:T(1,128)S(1)}, u32[]{:S(2)}, u32[]{:S(2)}) %collective-permute-start.12) | collective-permute-done | bytes 544 | tf_op jit(solution)/shard_map/ppermute | solution.py:527
  37.2 2.1 %collective-permute-done.11.refs_1_ = f32[1,128]{1,0:T(1,128)S(1)} collective-permute-done((f32[1,128]{1,0:T(1,128)S(1)}, f32[1,128]{1,0:T(1,128)S(1)}, u32[]{:S(2)}, u32[]{:S(2)}) %collective-permute-start.11) | collective-permute-done | bytes 544 | tf_op jit(solution)/shard_map/ppermute | solution.py:526
  39.3 1.2 %scale_start.1 = f32[137,4,512]{2,1,0:T(4,128)} custom-call(f32[4,137,4,128]{3,2,1,0:T(4,128)S(1)} %get-tuple-element.48.start, f32[137,4,128]{2,1,0:T(4,128)S(1)} %collective-permute-done.9.near_in, f32[1,128]{1,0:T(1,128)S(1)} %add_shares.1.refs_0_, f32[1,128]{1,0:T(1,128)S(1)} %collective-permute-done.11.refs_1_, ...), custom_call_target="tpu_custom_call" | custom-call | flops 1000000 | bytes 1000000 | tf_op jit(solution)/shard_map/scale_start/pallas_call | solution.py:118
  (7 shorter events, 0.0 us)
Async XLA Ops:
  2.9 11.7 %collective-permute-start = (f32[137,4,128]{2,1,0:T(4,128)S(1)}, f32[137,4,128]{2,1,0:T(4,128)S(1)}, u32[]{:S(2)}, u32[]{:S(2)}) collective-permute-start(f32[137,4,128]{2,1,0:T(4,128)S(1)} %get-tuple-element.31), channel_id=1, source_target_pairs={{0,7},{1,2},{2,1},{3,4},{4,3},{5,6},{6,5},{7,0},{8,15},{9,10},{10,... | collective-permute-start | bytes 841736 | tf_op jit(solution)/shard_map/ppermute | solution.py:538
  7.4 13.2 %collective-permute-start.1 = (f32[137,4,128]{2,1,0:T(4,128)S(1)}, f32[137,4,128]{2,1,0:T(4,128)S(1)}, u32[]{:S(2)}, u32[]{:S(2)}) collective-permute-start(f32[137,4,128]{2,1,0:T(4,128)S(1)} %get-tuple-element.32), channel_id=1, source_target_pairs={{0,7},{1,2},{2,1},{3,4},{4,3},{5,6},{6,5},{7,0},{8,15},{9,10},{10,... | collective-permute-start | bytes 841736 | tf_op jit(solution)/shard_map/ppermute | solution.py:538
  9.9 15.1 %collective-permute-start.2 = (f32[2,45,4,128]{3,2,1,0:T(4,128)S(1)}, f32[2,45,4,128]{3,2,1,0:T(4,128)S(1)}, u32[]{:S(2)}, u32[]{:S(2)}) collective-permute-start(f32[2,45,4,128]{3,2,1,0:T(4,128)S(1)} %get-tuple-element.36), channel_id=1, source_target_pairs={{0,1},{1,0},{2,3},{3,2},{4,5},{5,4},{6,7},{7,6},{8,9},{9,8},{10,11... | collective-permute-start | bytes 552968 | tf_op jit(solution)/shard_map/ppermute | solution.py:532
  9.9 15.1 %collective-permute-start.3 = (f32[2,46,4,128]{3,2,1,0:T(4,128)S(1)}, f32[2,46,4,128]{3,2,1,0:T(4,128)S(1)}, u32[]{:S(2)}, u32[]{:S(2)}) collective-permute-start(f32[2,46,4,128]{3,2,1,0:T(4,128)S(1)} %get-tuple-element.37), channel_id=1, source_target_pairs={{0,1},{1,0},{2,3},{3,2},{4,5},{5,4},{6,7},{7,6},{8,9},{9,8},{10,11... | collective-permute-start | bytes 565256 | tf_op jit(solution)/shard_map/ppermute | solution.py:532
  10.4 14.6 %collective-permute-start.4 = (f32[2,46,4,128]{3,2,1,0:T(4,128)S(1)}, f32[2,46,4,128]{3,2,1,0:T(4,128)S(1)}, u32[]{:S(2)}, u32[]{:S(2)}) collective-permute-start(f32[2,46,4,128]{3,2,1,0:T(4,128)S(1)} %get-tuple-element.38), channel_id=1, source_target_pairs={{0,1},{1,0},{2,3},{3,2},{4,5},{5,4},{6,7},{7,6},{8,9},{9,8},{10,11... | collective-permute-start | bytes 565256 | tf_op jit(solution)/shard_map/ppermute | solution.py:532
  15.2 14.0 %collective-permute-start.5 = (f32[137,4,128]{2,1,0:T(4,128)S(1)}, f32[137,4,128]{2,1,0:T(4,128)S(1)}, u32[]{:S(2)}, u32[]{:S(2)}) collective-permute-start(f32[137,4,128]{2,1,0:T(4,128)S(1)} %get-tuple-element.44), channel_id=1, source_target_pairs={{0,7},{1,2},{2,1},{3,4},{4,3},{5,6},{6,5},{7,0},{8,15},{9,10},{10,... | collective-permute-start | bytes 841736 | tf_op jit(solution)/shard_map/ppermute | solution.py:538
  21.2 11.1 %collective-permute-start.9 = (f32[137,4,128]{2,1,0:T(4,128)S(1)}, f32[137,4,128]{2,1,0:T(4,128)S(1)}, u32[]{:S(2)}, u32[]{:S(2)}) collective-permute-start(f32[137,4,128]{2,1,0:T(4,128)S(1)} %get-tuple-element.35._), channel_id=1, source_target_pairs={{0,7},{1,2},{2,1},{3,4},{4,3},{5,6},{6,5},{7,0},{8,15},{9,10},{10,... | collective-permute-start | bytes 841736 | tf_op jit(solution)/shard_map/ppermute | solution.py:538
  25.9 3.3 %collective-permute-start.7 = (f32[2,46,4,128]{3,2,1,0:T(4,128)S(1)}, f32[2,46,4,128]{3,2,1,0:T(4,128)S(1)}, u32[]{:S(2)}, u32[]{:S(2)}) collective-permute-start(f32[2,46,4,128]{3,2,1,0:T(4,128)S(1)} %get-tuple-element.46), channel_id=1, source_target_pairs={{0,1},{1,0},{2,3},{3,2},{4,5},{5,4},{6,7},{7,6},{8,9},{9,8},{10,11... | collective-permute-start | bytes 565256 | tf_op jit(solution)/shard_map/ppermute | solution.py:532
  26.0 3.2 %collective-permute-start.8 = (f32[2,46,4,128]{3,2,1,0:T(4,128)S(1)}, f32[2,46,4,128]{3,2,1,0:T(4,128)S(1)}, u32[]{:S(2)}, u32[]{:S(2)}) collective-permute-start(f32[2,46,4,128]{3,2,1,0:T(4,128)S(1)} %get-tuple-element.47), channel_id=1, source_target_pairs={{0,1},{1,0},{2,3},{3,2},{4,5},{5,4},{6,7},{7,6},{8,9},{9,8},{10,11... | collective-permute-start | bytes 565256 | tf_op jit(solution)/shard_map/ppermute | solution.py:532
  26.5 2.7 %collective-permute-start.6 = (f32[2,45,4,128]{3,2,1,0:T(4,128)S(1)}, f32[2,45,4,128]{3,2,1,0:T(4,128)S(1)}, u32[]{:S(2)}, u32[]{:S(2)}) collective-permute-start(f32[2,45,4,128]{3,2,1,0:T(4,128)S(1)} %get-tuple-element.45), channel_id=1, source_target_pairs={{0,1},{1,0},{2,3},{3,2},{4,5},{5,4},{6,7},{7,6},{8,9},{9,8},{10,11... | collective-permute-start | bytes 552968 | tf_op jit(solution)/shard_map/ppermute | solution.py:532
  32.4 1.2 %collective-permute-start.10 = (f32[1,128]{1,0:T(1,128)S(1)}, f32[1,128]{1,0:T(1,128)S(1)}, u32[]{:S(2)}, u32[]{:S(2)}) collective-permute-start(f32[1,128]{1,0:T(1,128)S(1)} %squares_of_last_block.1.refs_0_), channel_id=1, source_target_pairs={{0,1},{1,0},{2,3},{3,2},{4,5},{5,4},{6,7},{7,6},{8,9},{9,8},{10,11... | collective-permute-start | bytes 1544 | tf_op jit(solution)/shard_map/ppermute | solution.py:532
  33.6 3.5 %collective-permute-start.12 = (f32[1,128]{1,0:T(1,128)S(1)}, f32[1,128]{1,0:T(1,128)S(1)}, u32[]{:S(2)}, u32[]{:S(2)}) collective-permute-start(f32[1,128]{1,0:T(1,128)S(1)} %add_shares.1.refs_0_), channel_id=1, source_target_pairs={{0,2},{1,5},{2,0},{3,7},{4,6},{5,1},{6,4},{7,3},{8,10},{9,13},{10,... | collective-permute-start | bytes 1544 | tf_op jit(solution)/shard_map/ppermute | solution.py:527
  33.9 5.3 %collective-permute-start.11 = (f32[1,128]{1,0:T(1,128)S(1)}, f32[1,128]{1,0:T(1,128)S(1)}, u32[]{:S(2)}, u32[]{:S(2)}) collective-permute-start(f32[1,128]{1,0:T(1,128)S(1)} %add_shares.1.refs_0_), channel_id=1, source_target_pairs={{0,6},{1,7},{2,4},{3,5},{4,2},{5,3},{6,0},{7,1},{8,14},{9,15},{10,... | collective-permute-start | bytes 1544 | tf_op jit(solution)/shard_map/ppermute | solution.py:526
  37.2 2.1 %collective-permute-start.13 = (f32[1,128]{1,0:T(1,128)S(1)}, f32[1,128]{1,0:T(1,128)S(1)}, u32[]{:S(2)}, u32[]{:S(2)}) collective-permute-start(f32[1,128]{1,0:T(1,128)S(1)} %collective-permute-done.12.refs_2_), channel_id=1, source_target_pairs={{0,1},{1,0},{2,3},{3,2},{4,5},{5,4},{6,7},{7,6},{8,9},{9,8},{10,11... | collective-permute-start | bytes 1544 | tf_op jit(solution)/shard_map/ppermute | solution.py:532

commit v8 on v7

--- a/solution.py
+++ b/solution.py
@@ -136,7 +136,7 @@
 
 def first_kernel(
     step, all_blocks, fields, inverses, routes, points, weights,
-    to_near, to_far, diffused, inverse, targets, merged, field, route, point, weight, sems,
+    to_near, to_far, diffused, targets, merged, field, inverse, route, point, weight, sems,
 ):
     block_count = inverses.shape[2]
     near, far, target_near, target_far = z_blocks(block_count)
@@ -146,7 +146,8 @@
             (routes, route),
             (points, point),
             (weights, weight),
-            (inverses.at[step], inverse),
+            (inverses.at[step, :, near], inverse.at[0]),
+            (inverses.at[step, :, far], inverse.at[1]),
             (fields.at[:, :, lanes(near)], field.at[0]),
             (fields.at[:, :, lanes(far)], field.at[1]),
         ],
@@ -159,10 +160,12 @@
             found = target_columns(point[number, :, cols], route, number, j, block_count, all_blocks)
             targets[number, :, cols], merged[number, :, cols] = merge_points(found, weight[number, :, cols])
     matrix = side_matrix(targets, merged, step, (near, far), (target_near * BCOLS, target_far * BCOLS))
-    copies[3].wait()
-    for j, block in enumerate((near, far)):
-        copies[4 + j].wait()
-        diffuse(inverse[:, block, :].T, field.at[j], diffused.at[j])
+    for copy in copies[3:5]:
+        copy.wait()
+    turned = [inverse[j].T for j in range(REACH)]
+    for j in range(REACH):
+        copies[5 + j].wait()
+        diffuse(turned[j], field.at[j], diffused.at[j])
     sums = spread([diffused.at[0], diffused.at[1]], matrix)
     rows_of(to_near)[...] = sums[:, :BCOLS]
     rows_of(to_far)[...] = sums[:, BCOLS:]
@@ -206,56 +209,58 @@
             one,
             one,
             two,
-            jax.ShapeDtypeStruct(inverses.shape[1:], F32),
             jax.ShapeDtypeStruct(points.shape, jnp.int32),
             jax.ShapeDtypeStruct(weights.shape, F32),
         ),
-        (VMEM,) * 6,
+        (VMEM,) * 5,
         [
             pltpu.VMEM(two.shape, F32),
+            pltpu.VMEM((REACH, inverses.shape[1], inverses.shape[3]), F32),
             pltpu.SMEM(routes.shape, jnp.int32),
             pltpu.VMEM(points.shape, jnp.int32),
             pltpu.VMEM(weights.shape, F32),
-            pltpu.SemaphoreType.DMA((6,)),
+            pltpu.SemaphoreType.DMA((7,)),
         ],
         400_000_000,
         f"first_step{step}",
     )
 
 
-def side_kernel(step, fields, inverse, targets, weights, inverses, diffused, turned, *refs):
-    to_core, (field, next_inverse, sems) = refs[:-3], refs[-3:]
+def side_kernel(step, fields, targets, weights, inverses, diffused, turned, *refs):
+    to_core, (field, inverse, next_inverse, sems) = refs[:-4], refs[-4:]
     block_count = inverse.shape[1]
     side, first_target = core_side(block_count)
     copies = start_copies(
         sems,
         [(fields.at[:, :, lanes(side + j)], field.at[j]) for j in range(REACH)]
-        + [(inverses.at[step - 1], next_inverse)],
+        + [(inverses.at[step], inverse), (inverses.at[step - 1], next_inverse)],
     )
     columns = (first_target * BCOLS, (first_target + 1) * BCOLS)
     matrix = side_matrix(targets, weights, step, (side, side + 1), columns)
+    copies[REACH].wait()
     for j in range(REACH):
         copies[j].wait()
         diffuse(inverse[:, side + j, :].T, field.at[j], diffused.at[j])
     store_pieces(spread([diffused.at[j] for j in range(REACH)], matrix), to_core, field.shape[1])
-    copies[REACH].wait()
+    copies[REACH + 1].wait()
     for j in range(block_count):
         turned[j] = next_inverse[:, j, :].T
 
 
-def side(step, fields, inverse, targets, weights, inverses):
+def side(step, fields, targets, weights, inverses):
     two = blocks(fields, REACH)
-    levels, block_count, _ = inverse.shape
+    _, levels, block_count, _ = inverses.shape
     diffused, turned, *pieces = call(
         functools.partial(side_kernel, step),
-        (fields, inverse, targets, weights, inverses),
-        [HBM] + [VMEM] * 3 + [HBM],
+        (fields, targets, weights, inverses),
+        [HBM] + [VMEM] * 2 + [HBM],
         (two, jax.ShapeDtypeStruct((block_count, levels, levels), F32), *piece_shapes(two)),
         (VMEM,) * (2 + PIECES),
         [
             pltpu.VMEM(two.shape, F32),
-            pltpu.VMEM(inverse.shape, F32),
-            pltpu.SemaphoreType.DMA((REACH + 1,)),
+            pltpu.VMEM(inverses.shape[1:], F32),
+            pltpu.VMEM(inverses.shape[1:], F32),
+            pltpu.SemaphoreType.DMA((REACH + 2,)),
         ],
         2_000_000_000,
         f"side_step{step}",
@@ -523,8 +528,8 @@
     if count != 8:
         return [lax.all_to_all(jnp.broadcast_to(share, (count, BCOLS)), "col", 0, 0, tiled=True)]
     share = add([share, core_exchange(share)])
-    beside = lax.ppermute(share, "col", [(i, i ^ (6 if i % 2 else 6)) for i in range(count)])
-    apart = lax.ppermute(share, "col", [(i, i ^ (4 if i % 2 else 2)) for i in range(count)])
+    beside = lax.ppermute(share, "col", [(i, (i - 2) % count) for i in range(count)])
+    apart = lax.ppermute(share, "col", [(i, (i + 2) % count if i % 2 else i ^ 4) for i in range(count)])
     return [share, beside, apart, core_exchange(apart)]
 
 def core_exchange(value):
@@ -548,12 +553,12 @@
         for value in (fields, inverses, dep_lists, dep_points, weights)
     )
 
-    to_near, to_far, z_diffused, inverse, targets, merged = first(
+    to_near, to_far, z_diffused, targets, merged = first(
         1, all_blocks, fields, inverses, dep_lists, dep_points, weights
     )
     near_in = z_exchange(to_near)
     far_in = z_exchange(to_far)
-    core_diffused, turned, pieces = side(1, fields, inverse, targets, merged, inverses)
+    core_diffused, turned, pieces = side(1, fields, targets, merged, inverses)
     core_in = [core_exchange(piece) for piece in pieces]
     own = inner(1, z_diffused, core_diffused, targets, merged)
 

time: 40.7 us -> 40.5 us (level)
  starting transfers between devices: 16.7 us -> 16.2 us
    ppermute x2, starting transfers between devices: 3.13 us -> 2.69 us  [the longest x1 1.67 us: share_out(): lax.ppermute(share, 'col', [(i, (i + 2) % count if i % 2 else i ^ 4) for...]
  transfers between devices with their start and end apart: 14 -> 14, of which waited for: 6 -> 7; matrix products, arithmetic and copies ran while one was open for 0% -> 0% of each run, Pallas kernels for 22% -> 23%
where the time goes in v8:
time: 40.5 us; the launch traced here: 40.3 us
  starting transfers between devices  16.2 us (40%)
  Pallas kernels  12.6 us (31%)
  waiting for transfers between devices  10.7 us (26%)
  between operations  0.75 us (2%)
    pallas_call x11, Pallas kernels, call(): pl.pallas_call(kernel, out_shape=outs, in_specs=in_specs, out_specs=out_s...  12.6 us
    ppermute x4, starting transfers between devices, z_exchange(): return lax.ppermute(value, 'col', pairs)  12.2 us
    ppermute x4, waiting for transfers between devices, z_exchange(): return lax.ppermute(value, 'col', pairs)  6.7 us
    ppermute x1, waiting for transfers between devices, share_out(): lax.ppermute(share, 'col', [(i, (i + 2) % count if i % 2 else i ^ 4) for...  1.75 us
    ppermute x1, starting transfers between devices, share_out(): lax.ppermute(share, 'col', [(i, (i + 2) % count if i % 2 else i ^ 4) for...  1.67 us
    ppermute x8, waiting for transfers between devices, core_exchange(): return lax.ppermute(value, 'col', [(i, i ^ 1) for i in range(count)])  1.47 us
    ppermute x8, starting transfers between devices, core_exchange(): return lax.ppermute(value, 'col', [(i, i ^ 1) for i in range(count)])  1.36 us
    ppermute x1, starting transfers between devices, share_out(): lax.ppermute(share, 'col', [(i, (i - 2) % count) for i in range(count)])  1.02 us
  transfers between devices with their start and end apart: 14, of which 7 were waited for; matrix products, arithmetic and copies ran while one was open for 0% of the time, Pallas kernels for 23%

profile of v8, /device:TPU:0, one launch (start us, length us, event | category | flops | bytes accessed | tf_op | source)
XLA Modules:
  0.0 40.3 jit_solution(14512897808711543313)
XLA Ops:
  0.6 2.2 %first_step1.1 = (f32[137,4,128]{2,1,0:T(4,128)S(1)}, f32[137,4,128]{2,1,0:T(4,128)S(1)}, f32[2,137,4,128]{3,2,1,0:T(4,128)S(1)}, s32[2,4,512]{2,1,0:T(4,128)S(1)}, f32[2,4,512]{2,1,0:T(4,128)S(1)}) custom-call(f32[137,4,512]{2,1,0:T(4,128)} %bitcast.5, f32[2,137,4,137]{3,2,1,0:T(4,128)} %bitcast.7, s32[2,4,5]{2,1,0:T(4,128)} %routes.1, ...), custom_call_target="tpu_custom_call" | custom-call | flops 400000000 | bytes 1000000 | tf_op jit(solution)/shard_map/first_step1/pallas_call | solution.py:118
  2.8 4.6 %collective-permute-start = (f32[137,4,128]{2,1,0:T(4,128)S(1)}, f32[137,4,128]{2,1,0:T(4,128)S(1)}, u32[]{:S(2)}, u32[]{:S(2)}) collective-permute-start(f32[137,4,128]{2,1,0:T(4,128)S(1)} %get-tuple-element.29), channel_id=1, source_target_pairs={{0,7},{1,2},{2,1},{3,4},{4,3},{5,6},{6,5},{7,0},{8,15},{9,10},{10,... | collective-permute-start | bytes 841736 | tf_op jit(solution)/shard_map/ppermute | solution.py:543
  7.3 0.1 collective-permute-start.1
  7.4 2.6 %side_step1.1 = (f32[2,137,4,128]{3,2,1,0:T(4,128)S(1)}, f32[4,137,137]{2,1,0:T(8,128)S(1)}, f32[2,45,4,128]{3,2,1,0:T(4,128)S(1)}, f32[2,46,4,128]{3,2,1,0:T(4,128)S(1)}, f32[2,46,4,128]{3,2,1,0:T(4,128)S(1)}) custom-call(f32[137,4,512]{2,1,0:T(4,128)} %bitcast.6, s32[2,4,512]{2,1,0:T(4,128)S(1)} %get-tuple-element.26.targets, ...), custom_call_target="tpu_custom_call" | custom-call | flops 2000000000 | bytes 1000000 | tf_op jit(solution)/shard_map/side_step1/pallas_call | solution.py:118
  10.1 0.1 collective-permute-start.2
  10.1 0.5 %collective-permute-start.3 = (f32[2,46,4,128]{3,2,1,0:T(4,128)S(1)}, f32[2,46,4,128]{3,2,1,0:T(4,128)S(1)}, u32[]{:S(2)}, u32[]{:S(2)}) collective-permute-start(f32[2,46,4,128]{3,2,1,0:T(4,128)S(1)} %get-tuple-element.35), channel_id=1, source_target_pairs={{0,1},{1,0},{2,3},{3,2},{4,5},{5,4},{6,7},{7,6},{8,9},{9,8},{10,11... | collective-permute-start | bytes 565256 | tf_op jit(solution)/shard_map/ppermute | solution.py:537
  10.6 0.1 collective-permute-start.4
  10.7 1.3 %inner_step1.1.own = f32[4,137,4,128]{3,2,1,0:T(4,128)S(1)} custom-call(f32[2,137,4,128]{3,2,1,0:T(4,128)S(1)} %get-tuple-element.25.z_diffused, f32[2,137,4,128]{3,2,1,0:T(4,128)S(1)} %get-tuple-element.28.core_diffused, s32[2,4,512]{2,1,0:T(4,128)S(1)} %get-tuple-element.26.targets, f32[2,4,512]{2,1,0:T(4,128)S(1)} %get-tuple-element.27.weights), custom_call_target="tpu_custom_call" | custom-call | flops 2000000000 | bytes 1000000 | tf_op jit(solution)/shard_map/inner_step1/pallas_call | solution.py:118
  12.1 2.5 %collective-permute-done.near_in = f32[137,4,128]{2,1,0:T(4,128)S(1)} collective-permute-done((f32[137,4,128]{2,1,0:T(4,128)S(1)}, f32[137,4,128]{2,1,0:T(4,128)S(1)}, u32[]{:S(2)}, u32[]{:S(2)}) %collective-permute-start) | collective-permute-done | bytes 280608 | tf_op jit(solution)/shard_map/ppermute | solution.py:543
  14.5 0.6 %near_step0.1 = (f32[137,4,128]{2,1,0:T(4,128)S(1)}, f32[137,4,128]{2,1,0:T(4,128)S(1)}, f32[137,4,128]{2,1,0:T(4,128)S(1)}) custom-call(f32[4,137,4,128]{3,2,1,0:T(4,128)S(1)} %inner_step1.1.own, f32[137,4,128]{2,1,0:T(4,128)S(1)} %collective-permute-done.near_in, f32[4,137,137]{2,1,0:T(8,128)S(1)} %get-tuple-element.31.turned, ...), custom_call_target="tpu_custom_call" | custom-call | flops 300000000 | bytes 1000000 | tf_op jit(solution)/shard_map/near_step0/pallas_call | solution.py:118
  15.1 3.8 %collective-permute-start.5 = (f32[137,4,128]{2,1,0:T(4,128)S(1)}, f32[137,4,128]{2,1,0:T(4,128)S(1)}, u32[]{:S(2)}, u32[]{:S(2)}) collective-permute-start(f32[137,4,128]{2,1,0:T(4,128)S(1)} %get-tuple-element.42), channel_id=1, source_target_pairs={{0,7},{1,2},{2,1},{3,4},{4,3},{5,6},{6,5},{7,0},{8,15},{9,10},{10,... | collective-permute-start | bytes 841736 | tf_op jit(solution)/shard_map/ppermute | solution.py:543
  18.9 1.6 %collective-permute-done.1.far_in = f32[137,4,128]{2,1,0:T(4,128)S(1)} collective-permute-done((f32[137,4,128]{2,1,0:T(4,128)S(1)}, f32[137,4,128]{2,1,0:T(4,128)S(1)}, u32[]{:S(2)}, u32[]{:S(2)}) %collective-permute-start.1) | collective-permute-done | bytes 280608 | tf_op jit(solution)/shard_map/ppermute | solution.py:543
  20.5 0.6 %far_step0.1 = (f32[137,4,128]{2,1,0:T(4,128)S(1)}, f32[137,4,128]{2,1,0:T(4,128)S(1)}) custom-call(f32[4,137,4,128]{3,2,1,0:T(4,128)S(1)} %inner_step1.1.own, f32[137,4,128]{2,1,0:T(4,128)S(1)} %collective-permute-done.1.far_in, f32[137,4,128]{2,1,0:T(4,128)S(1)} %get-tuple-element.32.partial, f32[4,137,137]{2,1,0:T(8,128)S(1)} %get-tuple-element.31.turned, ...), custom_call_target="tpu_custom_call" | custom-call | flops 300000000 | bytes 1000000 | tf_op jit(solution)/shard_map/far_step0/pallas_call | solution.py:118
  21.1 3.8 %collective-permute-start.9 = (f32[137,4,128]{2,1,0:T(4,128)S(1)}, f32[137,4,128]{2,1,0:T(4,128)S(1)}, u32[]{:S(2)}, u32[]{:S(2)}) collective-permute-start(f32[137,4,128]{2,1,0:T(4,128)S(1)} %get-tuple-element.33._), channel_id=1, source_target_pairs={{0,7},{1,2},{2,1},{3,4},{4,3},{5,6},{6,5},{7,0},{8,15},{9,10},{10,... | collective-permute-start | bytes 841736 | tf_op jit(solution)/shard_map/ppermute | solution.py:543
  24.9 0.9 %core_step0.1 = (f32[2,137,4,128]{3,2,1,0:T(4,128)S(1)}, f32[2,45,4,128]{3,2,1,0:T(4,128)S(1)}, f32[2,46,4,128]{3,2,1,0:T(4,128)S(1)}, f32[2,46,4,128]{3,2,1,0:T(4,128)S(1)}) custom-call(f32[4,137,4,128]{3,2,1,0:T(4,128)S(1)} %inner_step1.1.own, f32[4,137,137]{2,1,0:T(8,128)S(1)} %get-tuple-element.31.turned, s32[2,4,512]{2,1,0:T(4,128)S(1)} %get-tuple-element.26.targets, ...), custom_call_target="tpu_custom_call" | custom-call | flops 1 | bytes 1 | tf_op jit(solution)/shard_map/core_step0/pallas_call | solution.py:118
  25.8 0.1 collective-permute-start.7
  25.9 0.5 %collective-permute-start.8 = (f32[2,46,4,128]{3,2,1,0:T(4,128)S(1)}, f32[2,46,4,128]{3,2,1,0:T(4,128)S(1)}, u32[]{:S(2)}, u32[]{:S(2)}) collective-permute-start(f32[2,46,4,128]{3,2,1,0:T(4,128)S(1)} %get-tuple-element.45), channel_id=1, source_target_pairs={{0,1},{1,0},{2,3},{3,2},{4,5},{5,4},{6,7},{7,6},{8,9},{9,8},{10,11... | collective-permute-start | bytes 565256 | tf_op jit(solution)/shard_map/ppermute | solution.py:537
  26.4 0.1 collective-permute-start.6
  26.5 2.6 %outer_step0.1 = (f32[4,137,4,128]{3,2,1,0:T(4,128)S(1)}, f32[137,4,512]{2,1,0:T(4,128)}) custom-call(f32[4,137,4,128]{3,2,1,0:T(4,128)S(1)} %inner_step1.1.own, f32[137,4,128]{2,1,0:T(4,128)S(1)} %collective-permute-done.near_in, f32[137,4,128]{2,1,0:T(4,128)S(1)} %collective-permute-done.1.far_in, f32[2,137,4,128]{3,2,1,0:T(4,128)S(1)} %get-tuple-element.37.diffused_core, ...), custom_call_target="tpu_custom_call" | custom-call | flops 1 | bytes 1 | tf_op jit(solution)/shard_map/outer_step0/pallas_call | solution.py:118
  29.1 0.0 collective-permute-done.7.refs_1_
  29.2 0.0 collective-permute-done.8.refs_2_
  29.2 0.4 %squares_of_most_blocks.1 = (f32[4,137,4,128]{3,2,1,0:T(4,128)S(1)}, f32[1,128]{1,0:T(1,128)S(1)}) custom-call(f32[4,137,4,128]{3,2,1,0:T(4,128)S(1)} %get-tuple-element.41.own, f32[137,4,128]{2,1,0:T(4,128)S(1)} %collective-permute-done.5.far_in, f32[2,45,4,128]{3,2,1,0:T(4,128)S(1)} %collective-permute-done.6.refs_0_, ...), custom_call_target="tpu_custom_call" | custom-call | flops 1000000 | bytes 1000000 | tf_op jit(solution)/shard_map/squares_of_most_blocks/pallas_call | solution.py:118
  29.6 2.7 %collective-permute-done.9.near_in = f32[137,4,128]{2,1,0:T(4,128)S(1)} collective-permute-done((f32[137,4,128]{2,1,0:T(4,128)S(1)}, f32[137,4,128]{2,1,0:T(4,128)S(1)}, u32[]{:S(2)}, u32[]{:S(2)}) %collective-permute-start.9) | collective-permute-done | bytes 280608 | tf_op jit(solution)/shard_map/ppermute | solution.py:543
  32.3 0.1 squares_of_last_block.1.refs_0_
  32.4 0.1 collective-permute-start.10
  32.4 1.1 %collective-permute-done.10.refs_1_ = f32[1,128]{1,0:T(1,128)S(1)} collective-permute-done((f32[1,128]{1,0:T(1,128)S(1)}, f32[1,128]{1,0:T(1,128)S(1)}, u32[]{:S(2)}, u32[]{:S(2)}) %collective-permute-start.10) | collective-permute-done | bytes 544 | tf_op jit(solution)/shard_map/ppermute | solution.py:537
  33.5 1.7 %collective-permute-start.12 = (f32[1,128]{1,0:T(1,128)S(1)}, f32[1,128]{1,0:T(1,128)S(1)}, u32[]{:S(2)}, u32[]{:S(2)}) collective-permute-start(f32[1,128]{1,0:T(1,128)S(1)} %add_shares.1.refs_0_), channel_id=1, source_target_pairs={{0,4},{1,3},{2,6},{3,5},{4,0},{5,7},{6,2},{7,1},{8,12},{9,11},{10,... | collective-permute-start | bytes 1544 | tf_op jit(solution)/shard_map/ppermute | solution.py:532
  35.2 1.0 %collective-permute-start.11 = (f32[1,128]{1,0:T(1,128)S(1)}, f32[1,128]{1,0:T(1,128)S(1)}, u32[]{:S(2)}, u32[]{:S(2)}) collective-permute-start(f32[1,128]{1,0:T(1,128)S(1)} %add_shares.1.refs_0_), channel_id=1, source_target_pairs={{0,6},{1,7},{2,0},{3,1},{4,2},{5,3},{6,4},{7,5},{8,14},{9,15},{10,... | collective-permute-start | bytes 1544 | tf_op jit(solution)/shard_map/ppermute | solution.py:531
  36.2 1.8 %collective-permute-done.12.refs_2_ = f32[1,128]{1,0:T(1,128)S(1)} collective-permute-done((f32[1,128]{1,0:T(1,128)S(1)}, f32[1,128]{1,0:T(1,128)S(1)}, u32[]{:S(2)}, u32[]{:S(2)}) %collective-permute-start.12) | collective-permute-done | bytes 544 | tf_op jit(solution)/shard_map/ppermute | solution.py:532
  38.0 0.8 %collective-permute-done.11.refs_1_ = f32[1,128]{1,0:T(1,128)S(1)} collective-permute-done((f32[1,128]{1,0:T(1,128)S(1)}, f32[1,128]{1,0:T(1,128)S(1)}, u32[]{:S(2)}, u32[]{:S(2)}) %collective-permute-start.11) | collective-permute-done | bytes 544 | tf_op jit(solution)/shard_map/ppermute | solution.py:531
  38.8 0.3 collective-permute-done.13.refs_3_
  39.1 1.2 %scale_start.1 = f32[137,4,512]{2,1,0:T(4,128)} custom-call(f32[4,137,4,128]{3,2,1,0:T(4,128)S(1)} %get-tuple-element.46.start, f32[137,4,128]{2,1,0:T(4,128)S(1)} %collective-permute-done.9.near_in, f32[1,128]{1,0:T(1,128)S(1)} %add_shares.1.refs_0_, f32[1,128]{1,0:T(1,128)S(1)} %collective-permute-done.11.refs_1_, ...), custom_call_target="tpu_custom_call" | custom-call | flops 1000000 | bytes 1000000 | tf_op jit(solution)/shard_map/scale_start/pallas_call | solution.py:118
  (7 shorter events, 0.0 us)
Async XLA Ops:
  2.8 11.7 %collective-permute-start = (f32[137,4,128]{2,1,0:T(4,128)S(1)}, f32[137,4,128]{2,1,0:T(4,128)S(1)}, u32[]{:S(2)}, u32[]{:S(2)}) collective-permute-start(f32[137,4,128]{2,1,0:T(4,128)S(1)} %get-tuple-element.29), channel_id=1, source_target_pairs={{0,7},{1,2},{2,1},{3,4},{4,3},{5,6},{6,5},{7,0},{8,15},{9,10},{10,... | collective-permute-start | bytes 841736 | tf_op jit(solution)/shard_map/ppermute | solution.py:543
  7.3 13.2 %collective-permute-start.1 = (f32[137,4,128]{2,1,0:T(4,128)S(1)}, f32[137,4,128]{2,1,0:T(4,128)S(1)}, u32[]{:S(2)}, u32[]{:S(2)}) collective-permute-start(f32[137,4,128]{2,1,0:T(4,128)S(1)} %get-tuple-element.30), channel_id=1, source_target_pairs={{0,7},{1,2},{2,1},{3,4},{4,3},{5,6},{6,5},{7,0},{8,15},{9,10},{10,... | collective-permute-start | bytes 841736 | tf_op jit(solution)/shard_map/ppermute | solution.py:543
  10.1 14.8 %collective-permute-start.2 = (f32[2,45,4,128]{3,2,1,0:T(4,128)S(1)}, f32[2,45,4,128]{3,2,1,0:T(4,128)S(1)}, u32[]{:S(2)}, u32[]{:S(2)}) collective-permute-start(f32[2,45,4,128]{3,2,1,0:T(4,128)S(1)} %get-tuple-element.34), channel_id=1, source_target_pairs={{0,1},{1,0},{2,3},{3,2},{4,5},{5,4},{6,7},{7,6},{8,9},{9,8},{10,11... | collective-permute-start | bytes 552968 | tf_op jit(solution)/shard_map/ppermute | solution.py:537
  10.1 14.8 %collective-permute-start.3 = (f32[2,46,4,128]{3,2,1,0:T(4,128)S(1)}, f32[2,46,4,128]{3,2,1,0:T(4,128)S(1)}, u32[]{:S(2)}, u32[]{:S(2)}) collective-permute-start(f32[2,46,4,128]{3,2,1,0:T(4,128)S(1)} %get-tuple-element.35), channel_id=1, source_target_pairs={{0,1},{1,0},{2,3},{3,2},{4,5},{5,4},{6,7},{7,6},{8,9},{9,8},{10,11... | collective-permute-start | bytes 565256 | tf_op jit(solution)/shard_map/ppermute | solution.py:537
  10.6 14.3 %collective-permute-start.4 = (f32[2,46,4,128]{3,2,1,0:T(4,128)S(1)}, f32[2,46,4,128]{3,2,1,0:T(4,128)S(1)}, u32[]{:S(2)}, u32[]{:S(2)}) collective-permute-start(f32[2,46,4,128]{3,2,1,0:T(4,128)S(1)} %get-tuple-element.36), channel_id=1, source_target_pairs={{0,1},{1,0},{2,3},{3,2},{4,5},{5,4},{6,7},{7,6},{8,9},{9,8},{10,11... | collective-permute-start | bytes 565256 | tf_op jit(solution)/shard_map/ppermute | solution.py:537
  15.1 14.0 %collective-permute-start.5 = (f32[137,4,128]{2,1,0:T(4,128)S(1)}, f32[137,4,128]{2,1,0:T(4,128)S(1)}, u32[]{:S(2)}, u32[]{:S(2)}) collective-permute-start(f32[137,4,128]{2,1,0:T(4,128)S(1)} %get-tuple-element.42), channel_id=1, source_target_pairs={{0,7},{1,2},{2,1},{3,4},{4,3},{5,6},{6,5},{7,0},{8,15},{9,10},{10,... | collective-permute-start | bytes 841736 | tf_op jit(solution)/shard_map/ppermute | solution.py:543
  21.1 11.1 %collective-permute-start.9 = (f32[137,4,128]{2,1,0:T(4,128)S(1)}, f32[137,4,128]{2,1,0:T(4,128)S(1)}, u32[]{:S(2)}, u32[]{:S(2)}) collective-permute-start(f32[137,4,128]{2,1,0:T(4,128)S(1)} %get-tuple-element.33._), channel_id=1, source_target_pairs={{0,7},{1,2},{2,1},{3,4},{4,3},{5,6},{6,5},{7,0},{8,15},{9,10},{10,... | collective-permute-start | bytes 841736 | tf_op jit(solution)/shard_map/ppermute | solution.py:543
  25.8 3.3 %collective-permute-start.7 = (f32[2,46,4,128]{3,2,1,0:T(4,128)S(1)}, f32[2,46,4,128]{3,2,1,0:T(4,128)S(1)}, u32[]{:S(2)}, u32[]{:S(2)}) collective-permute-start(f32[2,46,4,128]{3,2,1,0:T(4,128)S(1)} %get-tuple-element.44), channel_id=1, source_target_pairs={{0,1},{1,0},{2,3},{3,2},{4,5},{5,4},{6,7},{7,6},{8,9},{9,8},{10,11... | collective-permute-start | bytes 565256 | tf_op jit(solution)/shard_map/ppermute | solution.py:537
  25.9 3.2 %collective-permute-start.8 = (f32[2,46,4,128]{3,2,1,0:T(4,128)S(1)}, f32[2,46,4,128]{3,2,1,0:T(4,128)S(1)}, u32[]{:S(2)}, u32[]{:S(2)}) collective-permute-start(f32[2,46,4,128]{3,2,1,0:T(4,128)S(1)} %get-tuple-element.45), channel_id=1, source_target_pairs={{0,1},{1,0},{2,3},{3,2},{4,5},{5,4},{6,7},{7,6},{8,9},{9,8},{10,11... | collective-permute-start | bytes 565256 | tf_op jit(solution)/shard_map/ppermute | solution.py:537
  26.4 2.7 %collective-permute-start.6 = (f32[2,45,4,128]{3,2,1,0:T(4,128)S(1)}, f32[2,45,4,128]{3,2,1,0:T(4,128)S(1)}, u32[]{:S(2)}, u32[]{:S(2)}) collective-permute-start(f32[2,45,4,128]{3,2,1,0:T(4,128)S(1)} %get-tuple-element.43), channel_id=1, source_target_pairs={{0,1},{1,0},{2,3},{3,2},{4,5},{5,4},{6,7},{7,6},{8,9},{9,8},{10,11... | collective-permute-start | bytes 552968 | tf_op jit(solution)/shard_map/ppermute | solution.py:537
  32.4 1.2 %collective-permute-start.10 = (f32[1,128]{1,0:T(1,128)S(1)}, f32[1,128]{1,0:T(1,128)S(1)}, u32[]{:S(2)}, u32[]{:S(2)}) collective-permute-start(f32[1,128]{1,0:T(1,128)S(1)} %squares_of_last_block.1.refs_0_), channel_id=1, source_target_pairs={{0,1},{1,0},{2,3},{3,2},{4,5},{5,4},{6,7},{7,6},{8,9},{9,8},{10,11... | collective-permute-start | bytes 1544 | tf_op jit(solution)/shard_map/ppermute | solution.py:537
  33.5 4.4 %collective-permute-start.12 = (f32[1,128]{1,0:T(1,128)S(1)}, f32[1,128]{1,0:T(1,128)S(1)}, u32[]{:S(2)}, u32[]{:S(2)}) collective-permute-start(f32[1,128]{1,0:T(1,128)S(1)} %add_shares.1.refs_0_), channel_id=1, source_target_pairs={{0,4},{1,3},{2,6},{3,5},{4,0},{5,7},{6,2},{7,1},{8,12},{9,11},{10,... | collective-permute-start | bytes 1544 | tf_op jit(solution)/shard_map/ppermute | solution.py:532
  35.2 3.5 %collective-permute-start.11 = (f32[1,128]{1,0:T(1,128)S(1)}, f32[1,128]{1,0:T(1,128)S(1)}, u32[]{:S(2)}, u32[]{:S(2)}) collective-permute-start(f32[1,128]{1,0:T(1,128)S(1)} %add_shares.1.refs_0_), channel_id=1, source_target_pairs={{0,6},{1,7},{2,0},{3,1},{4,2},{5,3},{6,4},{7,5},{8,14},{9,15},{10,... | collective-permute-start | bytes 1544 | tf_op jit(solution)/shard_map/ppermute | solution.py:531
  38.0 1.1 %collective-permute-start.13 = (f32[1,128]{1,0:T(1,128)S(1)}, f32[1,128]{1,0:T(1,128)S(1)}, u32[]{:S(2)}, u32[]{:S(2)}) collective-permute-start(f32[1,128]{1,0:T(1,128)S(1)} %collective-permute-done.12.refs_2_), channel_id=1, source_target_pairs={{0,1},{1,0},{2,3},{3,2},{4,5},{5,4},{6,7},{7,6},{8,9},{9,8},{10,11... | collective-permute-start | bytes 1544 | tf_op jit(solution)/shard_map/ppermute | solution.py:537

commit v9 on v8

--- a/solution.py
+++ b/solution.py
@@ -528,8 +528,8 @@
     if count != 8:
         return [lax.all_to_all(jnp.broadcast_to(share, (count, BCOLS)), "col", 0, 0, tiled=True)]
     share = add([share, core_exchange(share)])
-    beside = lax.ppermute(share, "col", [(i, (i - 2) % count) for i in range(count)])
-    apart = lax.ppermute(share, "col", [(i, (i + 2) % count if i % 2 else i ^ 4) for i in range(count)])
+    beside = lax.ppermute(share, "col", [(i, i ^ 4) for i in range(count)])
+    apart = lax.ppermute(share, "col", [(i, i ^ (6 if i % 2 else 2)) for i in range(count)])
     return [share, beside, apart, core_exchange(apart)]
 
 def core_exchange(value):

time: 40.5 us -> 40.4 us (level)
  waiting for transfers between devices: 10.7 us -> 8.94 us
  starting transfers between devices: 16.2 us -> 17.6 us
    ppermute x2, waiting for transfers between devices: 2.52 us -> 0.66 us  [the longest x1 0.37 us: share_out(): beside = lax.ppermute(share, 'col', [(i, i ^ 4) for i in range(count)])]
    ppermute x8, starting transfers between devices: 1.36 us -> 2.21 us  [core_exchange(): return lax.ppermute(value, 'col', [(i, i ^ 1) for i in range(count)])]
    ppermute x2, starting transfers between devices: 2.69 us -> 3.25 us  [the longest x1 2.94 us: share_out(): beside = lax.ppermute(share, 'col', [(i, i ^ 4) for i in range(count)])]
where the time goes in v9:
time: 40.4 us; the launch traced here: 40 us
  starting transfers between devices  17.6 us (44%)
  Pallas kernels  12.6 us (31%)
  waiting for transfers between devices  8.94 us (22%)
  between operations  0.75 us (2%)
    pallas_call x11, Pallas kernels, call(): pl.pallas_call(kernel, out_shape=outs, in_specs=in_specs, out_specs=out_s...  12.6 us
    ppermute x4, starting transfers between devices, z_exchange(): return lax.ppermute(value, 'col', pairs)  12.2 us
    ppermute x4, waiting for transfers between devices, z_exchange(): return lax.ppermute(value, 'col', pairs)  6.7 us
    ppermute x1, starting transfers between devices, share_out(): beside = lax.ppermute(share, 'col', [(i, i ^ 4) for i in range(count)])  2.94 us
    ppermute x8, starting transfers between devices, core_exchange(): return lax.ppermute(value, 'col', [(i, i ^ 1) for i in range(count)])  2.21 us
    ppermute x8, waiting for transfers between devices, core_exchange(): return lax.ppermute(value, 'col', [(i, i ^ 1) for i in range(count)])  1.58 us
  transfers between devices with their start and end apart: 14, of which 7 were waited for; matrix products, arithmetic and copies ran while one was open for 0% of the time, Pallas kernels for 23%

profile of v9, /device:TPU:0, one launch (start us, length us, event | category | flops | bytes accessed | tf_op | source)
XLA Modules:
  0.0 40.0 jit_solution(2407407475663575529)
XLA Ops:
  0.6 2.2 %first_step1.1 = (f32[137,4,128]{2,1,0:T(4,128)S(1)}, f32[137,4,128]{2,1,0:T(4,128)S(1)}, f32[2,137,4,128]{3,2,1,0:T(4,128)S(1)}, s32[2,4,512]{2,1,0:T(4,128)S(1)}, f32[2,4,512]{2,1,0:T(4,128)S(1)}) custom-call(f32[137,4,512]{2,1,0:T(4,128)} %bitcast.5, f32[2,137,4,137]{3,2,1,0:T(4,128)} %bitcast.7, s32[2,4,5]{2,1,0:T(4,128)} %routes.1, ...), custom_call_target="tpu_custom_call" | custom-call | flops 400000000 | bytes 1000000 | tf_op jit(solution)/shard_map/first_step1/pallas_call | solution.py:118
  2.8 4.6 %collective-permute-start = (f32[137,4,128]{2,1,0:T(4,128)S(1)}, f32[137,4,128]{2,1,0:T(4,128)S(1)}, u32[]{:S(2)}, u32[]{:S(2)}) collective-permute-start(f32[137,4,128]{2,1,0:T(4,128)S(1)} %get-tuple-element.29), channel_id=1, source_target_pairs={{0,7},{1,2},{2,1},{3,4},{4,3},{5,6},{6,5},{7,0},{8,15},{9,10},{10,... | collective-permute-start | bytes 841736 | tf_op jit(solution)/shard_map/ppermute | solution.py:543
  7.3 0.1 collective-permute-start.1
  7.4 2.6 %side_step1.1 = (f32[2,137,4,128]{3,2,1,0:T(4,128)S(1)}, f32[4,137,137]{2,1,0:T(8,128)S(1)}, f32[2,45,4,128]{3,2,1,0:T(4,128)S(1)}, f32[2,46,4,128]{3,2,1,0:T(4,128)S(1)}, f32[2,46,4,128]{3,2,1,0:T(4,128)S(1)}) custom-call(f32[137,4,512]{2,1,0:T(4,128)} %bitcast.6, s32[2,4,512]{2,1,0:T(4,128)S(1)} %get-tuple-element.26.targets, ...), custom_call_target="tpu_custom_call" | custom-call | flops 2000000000 | bytes 1000000 | tf_op jit(solution)/shard_map/side_step1/pallas_call | solution.py:118
  10.1 0.1 collective-permute-start.2
  10.1 0.5 %collective-permute-start.3 = (f32[2,46,4,128]{3,2,1,0:T(4,128)S(1)}, f32[2,46,4,128]{3,2,1,0:T(4,128)S(1)}, u32[]{:S(2)}, u32[]{:S(2)}) collective-permute-start(f32[2,46,4,128]{3,2,1,0:T(4,128)S(1)} %get-tuple-element.35), channel_id=1, source_target_pairs={{0,1},{1,0},{2,3},{3,2},{4,5},{5,4},{6,7},{7,6},{8,9},{9,8},{10,11... | collective-permute-start | bytes 565256 | tf_op jit(solution)/shard_map/ppermute | solution.py:537
  10.6 0.1 collective-permute-start.4
  10.7 1.3 %inner_step1.1.own = f32[4,137,4,128]{3,2,1,0:T(4,128)S(1)} custom-call(f32[2,137,4,128]{3,2,1,0:T(4,128)S(1)} %get-tuple-element.25.z_diffused, f32[2,137,4,128]{3,2,1,0:T(4,128)S(1)} %get-tuple-element.28.core_diffused, s32[2,4,512]{2,1,0:T(4,128)S(1)} %get-tuple-element.26.targets, f32[2,4,512]{2,1,0:T(4,128)S(1)} %get-tuple-element.27.weights), custom_call_target="tpu_custom_call" | custom-call | flops 2000000000 | bytes 1000000 | tf_op jit(solution)/shard_map/inner_step1/pallas_call | solution.py:118
  12.1 2.5 %collective-permute-done.near_in = f32[137,4,128]{2,1,0:T(4,128)S(1)} collective-permute-done((f32[137,4,128]{2,1,0:T(4,128)S(1)}, f32[137,4,128]{2,1,0:T(4,128)S(1)}, u32[]{:S(2)}, u32[]{:S(2)}) %collective-permute-start) | collective-permute-done | bytes 280608 | tf_op jit(solution)/shard_map/ppermute | solution.py:543
  14.5 0.6 %near_step0.1 = (f32[137,4,128]{2,1,0:T(4,128)S(1)}, f32[137,4,128]{2,1,0:T(4,128)S(1)}, f32[137,4,128]{2,1,0:T(4,128)S(1)}) custom-call(f32[4,137,4,128]{3,2,1,0:T(4,128)S(1)} %inner_step1.1.own, f32[137,4,128]{2,1,0:T(4,128)S(1)} %collective-permute-done.near_in, f32[4,137,137]{2,1,0:T(8,128)S(1)} %get-tuple-element.31.turned, ...), custom_call_target="tpu_custom_call" | custom-call | flops 300000000 | bytes 1000000 | tf_op jit(solution)/shard_map/near_step0/pallas_call | solution.py:118
  15.1 3.8 %collective-permute-start.5 = (f32[137,4,128]{2,1,0:T(4,128)S(1)}, f32[137,4,128]{2,1,0:T(4,128)S(1)}, u32[]{:S(2)}, u32[]{:S(2)}) collective-permute-start(f32[137,4,128]{2,1,0:T(4,128)S(1)} %get-tuple-element.42), channel_id=1, source_target_pairs={{0,7},{1,2},{2,1},{3,4},{4,3},{5,6},{6,5},{7,0},{8,15},{9,10},{10,... | collective-permute-start | bytes 841736 | tf_op jit(solution)/shard_map/ppermute | solution.py:543
  18.9 1.6 %collective-permute-done.1.far_in = f32[137,4,128]{2,1,0:T(4,128)S(1)} collective-permute-done((f32[137,4,128]{2,1,0:T(4,128)S(1)}, f32[137,4,128]{2,1,0:T(4,128)S(1)}, u32[]{:S(2)}, u32[]{:S(2)}) %collective-permute-start.1) | collective-permute-done | bytes 280608 | tf_op jit(solution)/shard_map/ppermute | solution.py:543
  20.5 0.6 %far_step0.1 = (f32[137,4,128]{2,1,0:T(4,128)S(1)}, f32[137,4,128]{2,1,0:T(4,128)S(1)}) custom-call(f32[4,137,4,128]{3,2,1,0:T(4,128)S(1)} %inner_step1.1.own, f32[137,4,128]{2,1,0:T(4,128)S(1)} %collective-permute-done.1.far_in, f32[137,4,128]{2,1,0:T(4,128)S(1)} %get-tuple-element.32.partial, f32[4,137,137]{2,1,0:T(8,128)S(1)} %get-tuple-element.31.turned, ...), custom_call_target="tpu_custom_call" | custom-call | flops 300000000 | bytes 1000000 | tf_op jit(solution)/shard_map/far_step0/pallas_call | solution.py:118
  21.1 3.8 %collective-permute-start.9 = (f32[137,4,128]{2,1,0:T(4,128)S(1)}, f32[137,4,128]{2,1,0:T(4,128)S(1)}, u32[]{:S(2)}, u32[]{:S(2)}) collective-permute-start(f32[137,4,128]{2,1,0:T(4,128)S(1)} %get-tuple-element.33._), channel_id=1, source_target_pairs={{0,7},{1,2},{2,1},{3,4},{4,3},{5,6},{6,5},{7,0},{8,15},{9,10},{10,... | collective-permute-start | bytes 841736 | tf_op jit(solution)/shard_map/ppermute | solution.py:543
  24.9 0.0 collective-permute-done.2.refs_0_
  24.9 0.9 %core_step0.1 = (f32[2,137,4,128]{3,2,1,0:T(4,128)S(1)}, f32[2,45,4,128]{3,2,1,0:T(4,128)S(1)}, f32[2,46,4,128]{3,2,1,0:T(4,128)S(1)}, f32[2,46,4,128]{3,2,1,0:T(4,128)S(1)}) custom-call(f32[4,137,4,128]{3,2,1,0:T(4,128)S(1)} %inner_step1.1.own, f32[4,137,137]{2,1,0:T(8,128)S(1)} %get-tuple-element.31.turned, s32[2,4,512]{2,1,0:T(4,128)S(1)} %get-tuple-element.26.targets, ...), custom_call_target="tpu_custom_call" | custom-call | flops 1 | bytes 1 | tf_op jit(solution)/shard_map/core_step0/pallas_call | solution.py:118
  25.8 0.1 collective-permute-start.7
  25.9 0.5 %collective-permute-start.8 = (f32[2,46,4,128]{3,2,1,0:T(4,128)S(1)}, f32[2,46,4,128]{3,2,1,0:T(4,128)S(1)}, u32[]{:S(2)}, u32[]{:S(2)}) collective-permute-start(f32[2,46,4,128]{3,2,1,0:T(4,128)S(1)} %get-tuple-element.45), channel_id=1, source_target_pairs={{0,1},{1,0},{2,3},{3,2},{4,5},{5,4},{6,7},{7,6},{8,9},{9,8},{10,11... | collective-permute-start | bytes 565256 | tf_op jit(solution)/shard_map/ppermute | solution.py:537
  26.4 0.1 collective-permute-start.6
  26.5 2.6 %outer_step0.1 = (f32[4,137,4,128]{3,2,1,0:T(4,128)S(1)}, f32[137,4,512]{2,1,0:T(4,128)}) custom-call(f32[4,137,4,128]{3,2,1,0:T(4,128)S(1)} %inner_step1.1.own, f32[137,4,128]{2,1,0:T(4,128)S(1)} %collective-permute-done.near_in, f32[137,4,128]{2,1,0:T(4,128)S(1)} %collective-permute-done.1.far_in, f32[2,137,4,128]{3,2,1,0:T(4,128)S(1)} %get-tuple-element.37.diffused_core, ...), custom_call_target="tpu_custom_call" | custom-call | flops 1 | bytes 1 | tf_op jit(solution)/shard_map/outer_step0/pallas_call | solution.py:118
  29.2 0.4 %squares_of_most_blocks.1 = (f32[4,137,4,128]{3,2,1,0:T(4,128)S(1)}, f32[1,128]{1,0:T(1,128)S(1)}) custom-call(f32[4,137,4,128]{3,2,1,0:T(4,128)S(1)} %get-tuple-element.41.own, f32[137,4,128]{2,1,0:T(4,128)S(1)} %collective-permute-done.5.far_in, f32[2,45,4,128]{3,2,1,0:T(4,128)S(1)} %collective-permute-done.6.refs_0_, ...), custom_call_target="tpu_custom_call" | custom-call | flops 1000000 | bytes 1000000 | tf_op jit(solution)/shard_map/squares_of_most_blocks/pallas_call | solution.py:118
  29.6 2.7 %collective-permute-done.9.near_in = f32[137,4,128]{2,1,0:T(4,128)S(1)} collective-permute-done((f32[137,4,128]{2,1,0:T(4,128)S(1)}, f32[137,4,128]{2,1,0:T(4,128)S(1)}, u32[]{:S(2)}, u32[]{:S(2)}) %collective-permute-start.9) | collective-permute-done | bytes 280608 | tf_op jit(solution)/shard_map/ppermute | solution.py:543
  32.3 0.1 squares_of_last_block.1.refs_0_
  32.4 0.1 collective-permute-start.10
  32.4 1.1 %collective-permute-done.10.refs_1_ = f32[1,128]{1,0:T(1,128)S(1)} collective-permute-done((f32[1,128]{1,0:T(1,128)S(1)}, f32[1,128]{1,0:T(1,128)S(1)}, u32[]{:S(2)}, u32[]{:S(2)}) %collective-permute-start.10) | collective-permute-done | bytes 544 | tf_op jit(solution)/shard_map/ppermute | solution.py:537
  33.5 0.3 collective-permute-start.12
  33.8 2.9 %collective-permute-start.11 = (f32[1,128]{1,0:T(1,128)S(1)}, f32[1,128]{1,0:T(1,128)S(1)}, u32[]{:S(2)}, u32[]{:S(2)}) collective-permute-start(f32[1,128]{1,0:T(1,128)S(1)} %add_shares.1.refs_0_), channel_id=1, source_target_pairs={{0,4},{1,5},{2,6},{3,7},{4,0},{5,1},{6,2},{7,3},{8,12},{9,13},{10,... | collective-permute-start | bytes 1544 | tf_op jit(solution)/shard_map/ppermute | solution.py:531
  36.8 0.3 collective-permute-done.12.refs_2_
  37.1 0.9 %collective-permute-start.13 = (f32[1,128]{1,0:T(1,128)S(1)}, f32[1,128]{1,0:T(1,128)S(1)}, u32[]{:S(2)}, u32[]{:S(2)}) collective-permute-start(f32[1,128]{1,0:T(1,128)S(1)} %collective-permute-done.12.refs_2_), channel_id=1, source_target_pairs={{0,1},{1,0},{2,3},{3,2},{4,5},{5,4},{6,7},{7,6},{8,9},{9,8},{10,11... | collective-permute-start | bytes 1544 | tf_op jit(solution)/shard_map/ppermute | solution.py:537
  37.9 0.4 collective-permute-done.11.refs_1_
  38.3 0.5 %collective-permute-done.13.refs_3_ = f32[1,128]{1,0:T(1,128)S(1)} collective-permute-done((f32[1,128]{1,0:T(1,128)S(1)}, f32[1,128]{1,0:T(1,128)S(1)}, u32[]{:S(2)}, u32[]{:S(2)}) %collective-permute-start.13) | collective-permute-done | bytes 544 | tf_op jit(solution)/shard_map/ppermute | solution.py:537
  38.8 1.2 %scale_start.1 = f32[137,4,512]{2,1,0:T(4,128)} custom-call(f32[4,137,4,128]{3,2,1,0:T(4,128)S(1)} %get-tuple-element.46.start, f32[137,4,128]{2,1,0:T(4,128)S(1)} %collective-permute-done.9.near_in, f32[1,128]{1,0:T(1,128)S(1)} %add_shares.1.refs_0_, f32[1,128]{1,0:T(1,128)S(1)} %collective-permute-done.11.refs_1_, ...), custom_call_target="tpu_custom_call" | custom-call | flops 1000000 | bytes 1000000 | tf_op jit(solution)/shard_map/scale_start/pallas_call | solution.py:118
  (7 shorter events, 0.0 us)
Async XLA Ops:
  2.8 11.7 %collective-permute-start = (f32[137,4,128]{2,1,0:T(4,128)S(1)}, f32[137,4,128]{2,1,0:T(4,128)S(1)}, u32[]{:S(2)}, u32[]{:S(2)}) collective-permute-start(f32[137,4,128]{2,1,0:T(4,128)S(1)} %get-tuple-element.29), channel_id=1, source_target_pairs={{0,7},{1,2},{2,1},{3,4},{4,3},{5,6},{6,5},{7,0},{8,15},{9,10},{10,... | collective-permute-start | bytes 841736 | tf_op jit(solution)/shard_map/ppermute | solution.py:543
  7.3 13.2 %collective-permute-start.1 = (f32[137,4,128]{2,1,0:T(4,128)S(1)}, f32[137,4,128]{2,1,0:T(4,128)S(1)}, u32[]{:S(2)}, u32[]{:S(2)}) collective-permute-start(f32[137,4,128]{2,1,0:T(4,128)S(1)} %get-tuple-element.30), channel_id=1, source_target_pairs={{0,7},{1,2},{2,1},{3,4},{4,3},{5,6},{6,5},{7,0},{8,15},{9,10},{10,... | collective-permute-start | bytes 841736 | tf_op jit(solution)/shard_map/ppermute | solution.py:543
  10.1 14.8 %collective-permute-start.2 = (f32[2,45,4,128]{3,2,1,0:T(4,128)S(1)}, f32[2,45,4,128]{3,2,1,0:T(4,128)S(1)}, u32[]{:S(2)}, u32[]{:S(2)}) collective-permute-start(f32[2,45,4,128]{3,2,1,0:T(4,128)S(1)} %get-tuple-element.34), channel_id=1, source_target_pairs={{0,1},{1,0},{2,3},{3,2},{4,5},{5,4},{6,7},{7,6},{8,9},{9,8},{10,11... | collective-permute-start | bytes 552968 | tf_op jit(solution)/shard_map/ppermute | solution.py:537
  10.1 14.8 %collective-permute-start.3 = (f32[2,46,4,128]{3,2,1,0:T(4,128)S(1)}, f32[2,46,4,128]{3,2,1,0:T(4,128)S(1)}, u32[]{:S(2)}, u32[]{:S(2)}) collective-permute-start(f32[2,46,4,128]{3,2,1,0:T(4,128)S(1)} %get-tuple-element.35), channel_id=1, source_target_pairs={{0,1},{1,0},{2,3},{3,2},{4,5},{5,4},{6,7},{7,6},{8,9},{9,8},{10,11... | collective-permute-start | bytes 565256 | tf_op jit(solution)/shard_map/ppermute | solution.py:537
  10.6 14.3 %collective-permute-start.4 = (f32[2,46,4,128]{3,2,1,0:T(4,128)S(1)}, f32[2,46,4,128]{3,2,1,0:T(4,128)S(1)}, u32[]{:S(2)}, u32[]{:S(2)}) collective-permute-start(f32[2,46,4,128]{3,2,1,0:T(4,128)S(1)} %get-tuple-element.36), channel_id=1, source_target_pairs={{0,1},{1,0},{2,3},{3,2},{4,5},{5,4},{6,7},{7,6},{8,9},{9,8},{10,11... | collective-permute-start | bytes 565256 | tf_op jit(solution)/shard_map/ppermute | solution.py:537
  15.1 14.0 %collective-permute-start.5 = (f32[137,4,128]{2,1,0:T(4,128)S(1)}, f32[137,4,128]{2,1,0:T(4,128)S(1)}, u32[]{:S(2)}, u32[]{:S(2)}) collective-permute-start(f32[137,4,128]{2,1,0:T(4,128)S(1)} %get-tuple-element.42), channel_id=1, source_target_pairs={{0,7},{1,2},{2,1},{3,4},{4,3},{5,6},{6,5},{7,0},{8,15},{9,10},{10,... | collective-permute-start | bytes 841736 | tf_op jit(solution)/shard_map/ppermute | solution.py:543
  21.1 11.1 %collective-permute-start.9 = (f32[137,4,128]{2,1,0:T(4,128)S(1)}, f32[137,4,128]{2,1,0:T(4,128)S(1)}, u32[]{:S(2)}, u32[]{:S(2)}) collective-permute-start(f32[137,4,128]{2,1,0:T(4,128)S(1)} %get-tuple-element.33._), channel_id=1, source_target_pairs={{0,7},{1,2},{2,1},{3,4},{4,3},{5,6},{6,5},{7,0},{8,15},{9,10},{10,... | collective-permute-start | bytes 841736 | tf_op jit(solution)/shard_map/ppermute | solution.py:543
  25.8 3.3 %collective-permute-start.7 = (f32[2,46,4,128]{3,2,1,0:T(4,128)S(1)}, f32[2,46,4,128]{3,2,1,0:T(4,128)S(1)}, u32[]{:S(2)}, u32[]{:S(2)}) collective-permute-start(f32[2,46,4,128]{3,2,1,0:T(4,128)S(1)} %get-tuple-element.44), channel_id=1, source_target_pairs={{0,1},{1,0},{2,3},{3,2},{4,5},{5,4},{6,7},{7,6},{8,9},{9,8},{10,11... | collective-permute-start | bytes 565256 | tf_op jit(solution)/shard_map/ppermute | solution.py:537
  25.9 3.2 %collective-permute-start.8 = (f32[2,46,4,128]{3,2,1,0:T(4,128)S(1)}, f32[2,46,4,128]{3,2,1,0:T(4,128)S(1)}, u32[]{:S(2)}, u32[]{:S(2)}) collective-permute-start(f32[2,46,4,128]{3,2,1,0:T(4,128)S(1)} %get-tuple-element.45), channel_id=1, source_target_pairs={{0,1},{1,0},{2,3},{3,2},{4,5},{5,4},{6,7},{7,6},{8,9},{9,8},{10,11... | collective-permute-start | bytes 565256 | tf_op jit(solution)/shard_map/ppermute | solution.py:537
  26.4 2.7 %collective-permute-start.6 = (f32[2,45,4,128]{3,2,1,0:T(4,128)S(1)}, f32[2,45,4,128]{3,2,1,0:T(4,128)S(1)}, u32[]{:S(2)}, u32[]{:S(2)}) collective-permute-start(f32[2,45,4,128]{3,2,1,0:T(4,128)S(1)} %get-tuple-element.43), channel_id=1, source_target_pairs={{0,1},{1,0},{2,3},{3,2},{4,5},{5,4},{6,7},{7,6},{8,9},{9,8},{10,11... | collective-permute-start | bytes 552968 | tf_op jit(solution)/shard_map/ppermute | solution.py:537
  32.4 1.2 %collective-permute-start.10 = (f32[1,128]{1,0:T(1,128)S(1)}, f32[1,128]{1,0:T(1,128)S(1)}, u32[]{:S(2)}, u32[]{:S(2)}) collective-permute-start(f32[1,128]{1,0:T(1,128)S(1)} %squares_of_last_block.1.refs_0_), channel_id=1, source_target_pairs={{0,1},{1,0},{2,3},{3,2},{4,5},{5,4},{6,7},{7,6},{8,9},{9,8},{10,11... | collective-permute-start | bytes 1544 | tf_op jit(solution)/shard_map/ppermute | solution.py:537
  33.5 3.5 %collective-permute-start.12 = (f32[1,128]{1,0:T(1,128)S(1)}, f32[1,128]{1,0:T(1,128)S(1)}, u32[]{:S(2)}, u32[]{:S(2)}) collective-permute-start(f32[1,128]{1,0:T(1,128)S(1)} %add_shares.1.refs_0_), channel_id=1, source_target_pairs={{0,2},{1,7},{2,0},{3,5},{4,6},{5,3},{6,4},{7,1},{8,10},{9,15},{10,... | collective-permute-start | bytes 1544 | tf_op jit(solution)/shard_map/ppermute | solution.py:532
  33.8 4.5 %collective-permute-start.11 = (f32[1,128]{1,0:T(1,128)S(1)}, f32[1,128]{1,0:T(1,128)S(1)}, u32[]{:S(2)}, u32[]{:S(2)}) collective-permute-start(f32[1,128]{1,0:T(1,128)S(1)} %add_shares.1.refs_0_), channel_id=1, source_target_pairs={{0,4},{1,5},{2,6},{3,7},{4,0},{5,1},{6,2},{7,3},{8,12},{9,13},{10,... | collective-permute-start | bytes 1544 | tf_op jit(solution)/shard_map/ppermute | solution.py:531
  37.1 1.7 %collective-permute-start.13 = (f32[1,128]{1,0:T(1,128)S(1)}, f32[1,128]{1,0:T(1,128)S(1)}, u32[]{:S(2)}, u32[]{:S(2)}) collective-permute-start(f32[1,128]{1,0:T(1,128)S(1)} %collective-permute-done.12.refs_2_), channel_id=1, source_target_pairs={{0,1},{1,0},{2,3},{3,2},{4,5},{5,4},{6,7},{7,6},{8,9},{9,8},{10,11... | collective-permute-start | bytes 1544 | tf_op jit(solution)/shard_map/ppermute | solution.py:537

commit v10 on v9

--- a/solution.py
+++ b/solution.py
@@ -67,12 +67,16 @@
     return jnp.concatenate(targets, axis=0), jnp.concatenate(weights, axis=0)
 
 
-def spread_matrix(targets, weights, first_column, rows=BCOLS):
+def whole_matrix(targets, weights, first_column, rows=BCOLS):
     row = lax.broadcasted_iota(jnp.int32, (rows, targets.shape[1]), 0) + first_column
     total = jnp.zeros(row.shape, F32)
     for point in range(POINTS):
         total = jnp.where(row == targets[point : point + 1], weights[point : point + 1], total)
-    return split(total)
+    return total
+
+
+def spread_matrix(targets, weights, first_column, rows=BCOLS):
+    return split(whole_matrix(targets, weights, first_column, rows))
 
 
 def product(left, right, dims):
@@ -226,7 +230,7 @@
     )
 
 
-def side_kernel(step, fields, targets, weights, inverses, diffused, turned, *refs):
+def side_kernel(step, fields, targets, weights, inverses, diffused, turned, matrices, *refs):
     to_core, (field, inverse, next_inverse, sems) = refs[:-4], refs[-4:]
     block_count = inverse.shape[1]
     side, first_target = core_side(block_count)
@@ -242,6 +246,12 @@
         copies[j].wait()
         diffuse(inverse[:, side + j, :].T, field.at[j], diffused.at[j])
     store_pieces(spread([diffused.at[j] for j in range(REACH)], matrix), to_core, field.shape[1])
+    near, far, target_near, target_far = z_blocks(block_count)
+    for row, (block, target) in enumerate(((near, target_far), (near, target_near), (far, target_near))):
+        cols = lanes(block)
+        matrices[row * BCOLS : (row + 1) * BCOLS] = whole_matrix(
+            targets[step - 1, :, cols], weights[step - 1, :, cols], target * BCOLS
+        )
     copies[REACH + 1].wait()
     for j in range(block_count):
         turned[j] = next_inverse[:, j, :].T
@@ -250,12 +260,17 @@
 def side(step, fields, targets, weights, inverses):
     two = blocks(fields, REACH)
     _, levels, block_count, _ = inverses.shape
-    diffused, turned, *pieces = call(
+    diffused, turned, matrices, *pieces = call(
         functools.partial(side_kernel, step),
         (fields, targets, weights, inverses),
         [HBM] + [VMEM] * 2 + [HBM],
-        (two, jax.ShapeDtypeStruct((block_count, levels, levels), F32), *piece_shapes(two)),
-        (VMEM,) * (2 + PIECES),
+        (
+            two,
+            jax.ShapeDtypeStruct((block_count, levels, levels), F32),
+            jax.ShapeDtypeStruct((3 * BCOLS, BCOLS), F32),
+            *piece_shapes(two),
+        ),
+        (VMEM,) * (3 + PIECES),
         [
             pltpu.VMEM(two.shape, F32),
             pltpu.VMEM(inverses.shape[1:], F32),
@@ -265,7 +280,7 @@
         2_000_000_000,
         f"side_step{step}",
     )
-    return diffused, turned, pieces
+    return diffused, turned, matrices, pieces
 
 
 def inner_kernel(step, z_diffused, core_diffused, targets, weights, own, tall):
@@ -296,27 +311,21 @@
     )
 
 
-def near_kernel(step, own, near_in, turned, targets, weights, to_far, to_near, diffused, field):
-    block_count = own.shape[0]
-    near, _, target_near, target_far = z_blocks(block_count)
-    cols = lanes(near)
+def near_kernel(own, near_in, turned, matrices, to_far, to_near, diffused, field):
+    near = z_blocks(own.shape[0])[0]
     field[...] = own[near] + near_in[...]
     diffuse(turned[near], field, diffused)
-    halves = [
-        spread_matrix(targets[step, :, cols], weights[step, :, cols], target * BCOLS)
-        for target in (target_far, target_near)
-    ]
-    sums = spread([diffused], [jnp.concatenate(half, axis=0) for half in zip(*halves)])
+    sums = spread([diffused], split(matrices[: 2 * BCOLS]))
     rows_of(to_far)[...] = sums[:, :BCOLS]
     rows_of(to_near)[...] = sums[:, BCOLS:]
 
 
-def near(step, own, near_in, turned, targets, weights):
+def near(step, own, near_in, turned, matrices):
     one = blocks(own)
     return call(
-        functools.partial(near_kernel, step),
-        (own, near_in, turned, targets, weights),
-        [VMEM] * 5,
+        near_kernel,
+        (own, near_in, turned, matrices),
+        [VMEM] * 4,
         (one, one, one),
         (VMEM,) * 3,
         [pltpu.VMEM(one.shape, F32)],
@@ -325,22 +334,19 @@
     )
 
 
-def far_kernel(step, own, far_in, partial, turned, targets, weights, to_near, diffused, field):
-    block_count = own.shape[0]
-    _, far, target_near, _ = z_blocks(block_count)
-    cols = lanes(far)
+def far_kernel(own, far_in, partial, turned, matrices, to_near, diffused, field):
+    far = z_blocks(own.shape[0])[1]
     field[...] = own[far] + far_in[...]
     diffuse(turned[far], field, diffused)
-    matrix = spread_matrix(targets[step, :, cols], weights[step, :, cols], target_near * BCOLS)
-    rows_of(to_near)[...] = rows_of(partial)[...] + spread([diffused], matrix)
-
-
-def far(step, own, far_in, partial, turned, targets, weights):
+    rows_of(to_near)[...] = rows_of(partial)[...] + spread([diffused], split(matrices[2 * BCOLS :]))
+
+
+def far(step, own, far_in, partial, turned, matrices):
     one = blocks(own)
     return call(
-        functools.partial(far_kernel, step),
-        (own, far_in, partial, turned, targets, weights),
-        [VMEM] * 6,
+        far_kernel,
+        (own, far_in, partial, turned, matrices),
+        [VMEM] * 5,
         (one, one),
         (VMEM,) * 2,
         [pltpu.VMEM(one.shape, F32)],
@@ -558,13 +564,13 @@
     )
     near_in = z_exchange(to_near)
     far_in = z_exchange(to_far)
-    core_diffused, turned, pieces = side(1, fields, targets, merged, inverses)
+    core_diffused, turned, matrices, pieces = side(1, fields, targets, merged, inverses)
     core_in = [core_exchange(piece) for piece in pieces]
     own = inner(1, z_diffused, core_diffused, targets, merged)
 
-    to_far, partial, diffused_near = near(0, own, near_in, turned, targets, merged)
+    to_far, partial, diffused_near = near(0, own, near_in, turned, matrices)
     next_far_in = z_exchange(to_far)
-    to_near, diffused_far = far(0, own, far_in, partial, turned, targets, merged)
+    to_near, diffused_far = far(0, own, far_in, partial, turned, matrices)
     next_near_in = z_exchange(to_near)
     diffused_core, pieces = core(0, own, turned, targets, merged, core_in, to_near)
     next_core_in = [core_exchange(piece) for piece in pieces]

time: 40.4 us -> 40.4 us (level)
  no operation moved by 1% of the time
where the time goes in v10:
time: 40.4 us; the launch traced here: 40 us
  starting transfers between devices  17.6 us (44%)
  Pallas kernels  12.7 us (31%)
  waiting for transfers between devices  8.86 us (22%)
  between operations  0.75 us (2%)
    pallas_call x11, Pallas kernels, call(): pl.pallas_call(kernel, out_shape=outs, in_specs=in_specs, out_specs=out_s...  12.7 us
    ppermute x4, starting transfers between devices, z_exchange(): return lax.ppermute(value, 'col', pairs)  12.2 us
    ppermute x4, waiting for transfers between devices, z_exchange(): return lax.ppermute(value, 'col', pairs)  6.63 us
    ppermute x1, starting transfers between devices, share_out(): beside = lax.ppermute(share, 'col', [(i, i ^ 4) for i in range(count)])  2.94 us
    ppermute x8, starting transfers between devices, core_exchange(): return lax.ppermute(value, 'col', [(i, i ^ 1) for i in range(count)])  2.21 us
    ppermute x8, waiting for transfers between devices, core_exchange(): return lax.ppermute(value, 'col', [(i, i ^ 1) for i in range(count)])  1.58 us
  transfers between devices with their start and end apart: 14, of which 7 were waited for; matrix products, arithmetic and copies ran while one was open for 0% of the time, Pallas kernels for 23%

profile of v10, /device:TPU:0, one launch (start us, length us, event | category | flops | bytes accessed | tf_op | source)
XLA Modules:
  0.0 40.0 jit_solution(6337083236201034222)
XLA Ops:
  0.6 2.2 %first_step1.1 = (f32[137,4,128]{2,1,0:T(4,128)S(1)}, f32[137,4,128]{2,1,0:T(4,128)S(1)}, f32[2,137,4,128]{3,2,1,0:T(4,128)S(1)}, s32[2,4,512]{2,1,0:T(4,128)S(1)}, f32[2,4,512]{2,1,0:T(4,128)S(1)}) custom-call(f32[137,4,512]{2,1,0:T(4,128)} %bitcast.5, f32[2,137,4,137]{3,2,1,0:T(4,128)} %bitcast.7, s32[2,4,5]{2,1,0:T(4,128)} %routes.1, ...), custom_call_target="tpu_custom_call" | custom-call | flops 400000000 | bytes 1000000 | tf_op jit(solution)/shard_map/first_step1/pallas_call | solution.py:122
  2.8 4.6 %collective-permute-start = (f32[137,4,128]{2,1,0:T(4,128)S(1)}, f32[137,4,128]{2,1,0:T(4,128)S(1)}, u32[]{:S(2)}, u32[]{:S(2)}) collective-permute-start(f32[137,4,128]{2,1,0:T(4,128)S(1)} %get-tuple-element.30), channel_id=1, source_target_pairs={{0,7},{1,2},{2,1},{3,4},{4,3},{5,6},{6,5},{7,0},{8,15},{9,10},{10,... | collective-permute-start | bytes 841736 | tf_op jit(solution)/shard_map/ppermute | solution.py:549
  7.3 0.1 collective-permute-start.1
  7.4 2.7 %side_step1.1 = (f32[2,137,4,128]{3,2,1,0:T(4,128)S(1)}, f32[4,137,137]{2,1,0:T(8,128)S(1)}, f32[384,128]{1,0:T(8,128)S(1)}, f32[2,45,4,128]{3,2,1,0:T(4,128)S(1...) custom-call(f32[137,4,512]{2,1,0:T(4,128)} %bitcast.6, s32[2,4,512]{2,1,0:T(4,128)S(1)} %get-tuple-element.27.targets, ...), custom_call_target="tpu_custom_call" | custom-call | flops 2000000000 | bytes 1000000 | tf_op jit(solution)/shard_map/side_step1/pallas_call | solution.py:122
  10.1 0.1 collective-permute-start.2
  10.2 0.5 %collective-permute-start.3 = (f32[2,46,4,128]{3,2,1,0:T(4,128)S(1)}, f32[2,46,4,128]{3,2,1,0:T(4,128)S(1)}, u32[]{:S(2)}, u32[]{:S(2)}) collective-permute-start(f32[2,46,4,128]{3,2,1,0:T(4,128)S(1)} %get-tuple-element.37), channel_id=1, source_target_pairs={{0,1},{1,0},{2,3},{3,2},{4,5},{5,4},{6,7},{7,6},{8,9},{9,8},{10,11... | collective-permute-start | bytes 565256 | tf_op jit(solution)/shard_map/ppermute | solution.py:543
  10.7 0.1 collective-permute-start.4
  10.8 1.3 %inner_step1.1.own = f32[4,137,4,128]{3,2,1,0:T(4,128)S(1)} custom-call(f32[2,137,4,128]{3,2,1,0:T(4,128)S(1)} %get-tuple-element.26.z_diffused, f32[2,137,4,128]{3,2,1,0:T(4,128)S(1)} %get-tuple-element.29.core_diffused, s32[2,4,512]{2,1,0:T(4,128)S(1)} %get-tuple-element.27.targets, f32[2,4,512]{2,1,0:T(4,128)S(1)} %get-tuple-element.28.weights), custom_call_target="tpu_custom_call" | custom-call | flops 2000000000 | bytes 1000000 | tf_op jit(solution)/shard_map/inner_step1/pallas_call | solution.py:122
  12.1 2.4 %collective-permute-done.near_in = f32[137,4,128]{2,1,0:T(4,128)S(1)} collective-permute-done((f32[137,4,128]{2,1,0:T(4,128)S(1)}, f32[137,4,128]{2,1,0:T(4,128)S(1)}, u32[]{:S(2)}, u32[]{:S(2)}) %collective-permute-start) | collective-permute-done | bytes 280608 | tf_op jit(solution)/shard_map/ppermute | solution.py:549
  14.5 0.6 %near_step0.1 = (f32[137,4,128]{2,1,0:T(4,128)S(1)}, f32[137,4,128]{2,1,0:T(4,128)S(1)}, f32[137,4,128]{2,1,0:T(4,128)S(1)}) custom-call(f32[4,137,4,128]{3,2,1,0:T(4,128)S(1)} %inner_step1.1.own, f32[137,4,128]{2,1,0:T(4,128)S(1)} %collective-permute-done.near_in, f32[4,137,137]{2,1,0:T(8,128)S(1)} %get-tuple-element.32.turned, ...), custom_call_target="tpu_custom_call" | custom-call | flops 300000000 | bytes 1000000 | tf_op jit(solution)/shard_map/near_step0/pallas_call | solution.py:122
  15.1 3.8 %collective-permute-start.5 = (f32[137,4,128]{2,1,0:T(4,128)S(1)}, f32[137,4,128]{2,1,0:T(4,128)S(1)}, u32[]{:S(2)}, u32[]{:S(2)}) collective-permute-start(f32[137,4,128]{2,1,0:T(4,128)S(1)} %get-tuple-element.44), channel_id=1, source_target_pairs={{0,7},{1,2},{2,1},{3,4},{4,3},{5,6},{6,5},{7,0},{8,15},{9,10},{10,... | collective-permute-start | bytes 841736 | tf_op jit(solution)/shard_map/ppermute | solution.py:549
  18.9 1.6 %collective-permute-done.1.far_in = f32[137,4,128]{2,1,0:T(4,128)S(1)} collective-permute-done((f32[137,4,128]{2,1,0:T(4,128)S(1)}, f32[137,4,128]{2,1,0:T(4,128)S(1)}, u32[]{:S(2)}, u32[]{:S(2)}) %collective-permute-start.1) | collective-permute-done | bytes 280608 | tf_op jit(solution)/shard_map/ppermute | solution.py:549
  20.5 0.6 %far_step0.1 = (f32[137,4,128]{2,1,0:T(4,128)S(1)}, f32[137,4,128]{2,1,0:T(4,128)S(1)}) custom-call(f32[4,137,4,128]{3,2,1,0:T(4,128)S(1)} %inner_step1.1.own, f32[137,4,128]{2,1,0:T(4,128)S(1)} %collective-permute-done.1.far_in, f32[137,4,128]{2,1,0:T(4,128)S(1)} %get-tuple-element.34.partial, f32[4,137,137]{2,1,0:T(8,128)S(1)} %get-tuple-element.32.turned, ...), custom_call_target="tpu_custom_call" | custom-call | flops 300000000 | bytes 1000000 | tf_op jit(solution)/shard_map/far_step0/pallas_call | solution.py:122
  21.1 3.8 %collective-permute-start.9 = (f32[137,4,128]{2,1,0:T(4,128)S(1)}, f32[137,4,128]{2,1,0:T(4,128)S(1)}, u32[]{:S(2)}, u32[]{:S(2)}) collective-permute-start(f32[137,4,128]{2,1,0:T(4,128)S(1)} %get-tuple-element.35._), channel_id=1, source_target_pairs={{0,7},{1,2},{2,1},{3,4},{4,3},{5,6},{6,5},{7,0},{8,15},{9,10},{10,... | collective-permute-start | bytes 841736 | tf_op jit(solution)/shard_map/ppermute | solution.py:549
  24.9 0.9 %core_step0.1 = (f32[2,137,4,128]{3,2,1,0:T(4,128)S(1)}, f32[2,45,4,128]{3,2,1,0:T(4,128)S(1)}, f32[2,46,4,128]{3,2,1,0:T(4,128)S(1)}, f32[2,46,4,128]{3,2,1,0:T(4,128)S(1)}) custom-call(f32[4,137,4,128]{3,2,1,0:T(4,128)S(1)} %inner_step1.1.own, f32[4,137,137]{2,1,0:T(8,128)S(1)} %get-tuple-element.32.turned, s32[2,4,512]{2,1,0:T(4,128)S(1)} %get-tuple-element.27.targets, ...), custom_call_target="tpu_custom_call" | custom-call | flops 1 | bytes 1 | tf_op jit(solution)/shard_map/core_step0/pallas_call | solution.py:122
  25.8 0.1 collective-permute-start.7
  25.9 0.5 %collective-permute-start.8 = (f32[2,46,4,128]{3,2,1,0:T(4,128)S(1)}, f32[2,46,4,128]{3,2,1,0:T(4,128)S(1)}, u32[]{:S(2)}, u32[]{:S(2)}) collective-permute-start(f32[2,46,4,128]{3,2,1,0:T(4,128)S(1)} %get-tuple-element.47), channel_id=1, source_target_pairs={{0,1},{1,0},{2,3},{3,2},{4,5},{5,4},{6,7},{7,6},{8,9},{9,8},{10,11... | collective-permute-start | bytes 565256 | tf_op jit(solution)/shard_map/ppermute | solution.py:543
  26.4 0.1 collective-permute-start.6
  26.5 2.6 %outer_step0.1 = (f32[4,137,4,128]{3,2,1,0:T(4,128)S(1)}, f32[137,4,512]{2,1,0:T(4,128)}) custom-call(f32[4,137,4,128]{3,2,1,0:T(4,128)S(1)} %inner_step1.1.own, f32[137,4,128]{2,1,0:T(4,128)S(1)} %collective-permute-done.near_in, f32[137,4,128]{2,1,0:T(4,128)S(1)} %collective-permute-done.1.far_in, f32[2,137,4,128]{3,2,1,0:T(4,128)S(1)} %get-tuple-element.39.diffused_core, ...), custom_call_target="tpu_custom_call" | custom-call | flops 1 | bytes 1 | tf_op jit(solution)/shard_map/outer_step0/pallas_call | solution.py:122
  29.1 0.0 collective-permute-done.6.refs_0_
  29.2 0.4 %squares_of_most_blocks.1 = (f32[4,137,4,128]{3,2,1,0:T(4,128)S(1)}, f32[1,128]{1,0:T(1,128)S(1)}) custom-call(f32[4,137,4,128]{3,2,1,0:T(4,128)S(1)} %get-tuple-element.43.own, f32[137,4,128]{2,1,0:T(4,128)S(1)} %collective-permute-done.5.far_in, f32[2,45,4,128]{3,2,1,0:T(4,128)S(1)} %collective-permute-done.6.refs_0_, ...), custom_call_target="tpu_custom_call" | custom-call | flops 1000000 | bytes 1000000 | tf_op jit(solution)/shard_map/squares_of_most_blocks/pallas_call | solution.py:122
  29.6 2.7 %collective-permute-done.9.near_in = f32[137,4,128]{2,1,0:T(4,128)S(1)} collective-permute-done((f32[137,4,128]{2,1,0:T(4,128)S(1)}, f32[137,4,128]{2,1,0:T(4,128)S(1)}, u32[]{:S(2)}, u32[]{:S(2)}) %collective-permute-start.9) | collective-permute-done | bytes 280608 | tf_op jit(solution)/shard_map/ppermute | solution.py:549
  32.3 0.1 squares_of_last_block.1.refs_0_
  32.4 0.1 collective-permute-start.10
  32.4 1.1 %collective-permute-done.10.refs_1_ = f32[1,128]{1,0:T(1,128)S(1)} collective-permute-done((f32[1,128]{1,0:T(1,128)S(1)}, f32[1,128]{1,0:T(1,128)S(1)}, u32[]{:S(2)}, u32[]{:S(2)}) %collective-permute-start.10) | collective-permute-done | bytes 544 | tf_op jit(solution)/shard_map/ppermute | solution.py:543
  33.5 0.3 collective-permute-start.12
  33.8 2.9 %collective-permute-start.11 = (f32[1,128]{1,0:T(1,128)S(1)}, f32[1,128]{1,0:T(1,128)S(1)}, u32[]{:S(2)}, u32[]{:S(2)}) collective-permute-start(f32[1,128]{1,0:T(1,128)S(1)} %add_shares.1.refs_0_), channel_id=1, source_target_pairs={{0,4},{1,5},{2,6},{3,7},{4,0},{5,1},{6,2},{7,3},{8,12},{9,13},{10,... | collective-permute-start | bytes 1544 | tf_op jit(solution)/shard_map/ppermute | solution.py:537
  36.8 0.3 collective-permute-done.12.refs_2_
  37.1 0.9 %collective-permute-start.13 = (f32[1,128]{1,0:T(1,128)S(1)}, f32[1,128]{1,0:T(1,128)S(1)}, u32[]{:S(2)}, u32[]{:S(2)}) collective-permute-start(f32[1,128]{1,0:T(1,128)S(1)} %collective-permute-done.12.refs_2_), channel_id=1, source_target_pairs={{0,1},{1,0},{2,3},{3,2},{4,5},{5,4},{6,7},{7,6},{8,9},{9,8},{10,11... | collective-permute-start | bytes 1544 | tf_op jit(solution)/shard_map/ppermute | solution.py:543
  37.9 0.4 collective-permute-done.11.refs_1_
  38.3 0.5 %collective-permute-done.13.refs_3_ = f32[1,128]{1,0:T(1,128)S(1)} collective-permute-done((f32[1,128]{1,0:T(1,128)S(1)}, f32[1,128]{1,0:T(1,128)S(1)}, u32[]{:S(2)}, u32[]{:S(2)}) %collective-permute-start.13) | collective-permute-done | bytes 544 | tf_op jit(solution)/shard_map/ppermute | solution.py:543
  38.8 1.2 %scale_start.1 = f32[137,4,512]{2,1,0:T(4,128)} custom-call(f32[4,137,4,128]{3,2,1,0:T(4,128)S(1)} %get-tuple-element.48.start, f32[137,4,128]{2,1,0:T(4,128)S(1)} %collective-permute-done.9.near_in, f32[1,128]{1,0:T(1,128)S(1)} %add_shares.1.refs_0_, f32[1,128]{1,0:T(1,128)S(1)} %collective-permute-done.11.refs_1_, ...), custom_call_target="tpu_custom_call" | custom-call | flops 1000000 | bytes 1000000 | tf_op jit(solution)/shard_map/scale_start/pallas_call | solution.py:122
  (7 shorter events, 0.0 us)
Async XLA Ops:
  2.8 11.7 %collective-permute-start = (f32[137,4,128]{2,1,0:T(4,128)S(1)}, f32[137,4,128]{2,1,0:T(4,128)S(1)}, u32[]{:S(2)}, u32[]{:S(2)}) collective-permute-start(f32[137,4,128]{2,1,0:T(4,128)S(1)} %get-tuple-element.30), channel_id=1, source_target_pairs={{0,7},{1,2},{2,1},{3,4},{4,3},{5,6},{6,5},{7,0},{8,15},{9,10},{10,... | collective-permute-start | bytes 841736 | tf_op jit(solution)/shard_map/ppermute | solution.py:549
  7.3 13.2 %collective-permute-start.1 = (f32[137,4,128]{2,1,0:T(4,128)S(1)}, f32[137,4,128]{2,1,0:T(4,128)S(1)}, u32[]{:S(2)}, u32[]{:S(2)}) collective-permute-start(f32[137,4,128]{2,1,0:T(4,128)S(1)} %get-tuple-element.31), channel_id=1, source_target_pairs={{0,7},{1,2},{2,1},{3,4},{4,3},{5,6},{6,5},{7,0},{8,15},{9,10},{10,... | collective-permute-start | bytes 841736 | tf_op jit(solution)/shard_map/ppermute | solution.py:549
  10.1 14.8 %collective-permute-start.2 = (f32[2,45,4,128]{3,2,1,0:T(4,128)S(1)}, f32[2,45,4,128]{3,2,1,0:T(4,128)S(1)}, u32[]{:S(2)}, u32[]{:S(2)}) collective-permute-start(f32[2,45,4,128]{3,2,1,0:T(4,128)S(1)} %get-tuple-element.36), channel_id=1, source_target_pairs={{0,1},{1,0},{2,3},{3,2},{4,5},{5,4},{6,7},{7,6},{8,9},{9,8},{10,11... | collective-permute-start | bytes 552968 | tf_op jit(solution)/shard_map/ppermute | solution.py:543
  10.2 14.7 %collective-permute-start.3 = (f32[2,46,4,128]{3,2,1,0:T(4,128)S(1)}, f32[2,46,4,128]{3,2,1,0:T(4,128)S(1)}, u32[]{:S(2)}, u32[]{:S(2)}) collective-permute-start(f32[2,46,4,128]{3,2,1,0:T(4,128)S(1)} %get-tuple-element.37), channel_id=1, source_target_pairs={{0,1},{1,0},{2,3},{3,2},{4,5},{5,4},{6,7},{7,6},{8,9},{9,8},{10,11... | collective-permute-start | bytes 565256 | tf_op jit(solution)/shard_map/ppermute | solution.py:543
  10.7 14.2 %collective-permute-start.4 = (f32[2,46,4,128]{3,2,1,0:T(4,128)S(1)}, f32[2,46,4,128]{3,2,1,0:T(4,128)S(1)}, u32[]{:S(2)}, u32[]{:S(2)}) collective-permute-start(f32[2,46,4,128]{3,2,1,0:T(4,128)S(1)} %get-tuple-element.38), channel_id=1, source_target_pairs={{0,1},{1,0},{2,3},{3,2},{4,5},{5,4},{6,7},{7,6},{8,9},{9,8},{10,11... | collective-permute-start | bytes 565256 | tf_op jit(solution)/shard_map/ppermute | solution.py:543
  15.1 14.0 %collective-permute-start.5 = (f32[137,4,128]{2,1,0:T(4,128)S(1)}, f32[137,4,128]{2,1,0:T(4,128)S(1)}, u32[]{:S(2)}, u32[]{:S(2)}) collective-permute-start(f32[137,4,128]{2,1,0:T(4,128)S(1)} %get-tuple-element.44), channel_id=1, source_target_pairs={{0,7},{1,2},{2,1},{3,4},{4,3},{5,6},{6,5},{7,0},{8,15},{9,10},{10,... | collective-permute-start | bytes 841736 | tf_op jit(solution)/shard_map/ppermute | solution.py:549
  21.1 11.1 %collective-permute-start.9 = (f32[137,4,128]{2,1,0:T(4,128)S(1)}, f32[137,4,128]{2,1,0:T(4,128)S(1)}, u32[]{:S(2)}, u32[]{:S(2)}) collective-permute-start(f32[137,4,128]{2,1,0:T(4,128)S(1)} %get-tuple-element.35._), channel_id=1, source_target_pairs={{0,7},{1,2},{2,1},{3,4},{4,3},{5,6},{6,5},{7,0},{8,15},{9,10},{10,... | collective-permute-start | bytes 841736 | tf_op jit(solution)/shard_map/ppermute | solution.py:549
  25.8 3.3 %collective-permute-start.7 = (f32[2,46,4,128]{3,2,1,0:T(4,128)S(1)}, f32[2,46,4,128]{3,2,1,0:T(4,128)S(1)}, u32[]{:S(2)}, u32[]{:S(2)}) collective-permute-start(f32[2,46,4,128]{3,2,1,0:T(4,128)S(1)} %get-tuple-element.46), channel_id=1, source_target_pairs={{0,1},{1,0},{2,3},{3,2},{4,5},{5,4},{6,7},{7,6},{8,9},{9,8},{10,11... | collective-permute-start | bytes 565256 | tf_op jit(solution)/shard_map/ppermute | solution.py:543
  25.9 3.2 %collective-permute-start.8 = (f32[2,46,4,128]{3,2,1,0:T(4,128)S(1)}, f32[2,46,4,128]{3,2,1,0:T(4,128)S(1)}, u32[]{:S(2)}, u32[]{:S(2)}) collective-permute-start(f32[2,46,4,128]{3,2,1,0:T(4,128)S(1)} %get-tuple-element.47), channel_id=1, source_target_pairs={{0,1},{1,0},{2,3},{3,2},{4,5},{5,4},{6,7},{7,6},{8,9},{9,8},{10,11... | collective-permute-start | bytes 565256 | tf_op jit(solution)/shard_map/ppermute | solution.py:543
  26.4 2.7 %collective-permute-start.6 = (f32[2,45,4,128]{3,2,1,0:T(4,128)S(1)}, f32[2,45,4,128]{3,2,1,0:T(4,128)S(1)}, u32[]{:S(2)}, u32[]{:S(2)}) collective-permute-start(f32[2,45,4,128]{3,2,1,0:T(4,128)S(1)} %get-tuple-element.45), channel_id=1, source_target_pairs={{0,1},{1,0},{2,3},{3,2},{4,5},{5,4},{6,7},{7,6},{8,9},{9,8},{10,11... | collective-permute-start | bytes 552968 | tf_op jit(solution)/shard_map/ppermute | solution.py:543
  32.4 1.2 %collective-permute-start.10 = (f32[1,128]{1,0:T(1,128)S(1)}, f32[1,128]{1,0:T(1,128)S(1)}, u32[]{:S(2)}, u32[]{:S(2)}) collective-permute-start(f32[1,128]{1,0:T(1,128)S(1)} %squares_of_last_block.1.refs_0_), channel_id=1, source_target_pairs={{0,1},{1,0},{2,3},{3,2},{4,5},{5,4},{6,7},{7,6},{8,9},{9,8},{10,11... | collective-permute-start | bytes 1544 | tf_op jit(solution)/shard_map/ppermute | solution.py:543
  33.5 3.5 %collective-permute-start.12 = (f32[1,128]{1,0:T(1,128)S(1)}, f32[1,128]{1,0:T(1,128)S(1)}, u32[]{:S(2)}, u32[]{:S(2)}) collective-permute-start(f32[1,128]{1,0:T(1,128)S(1)} %add_shares.1.refs_0_), channel_id=1, source_target_pairs={{0,2},{1,7},{2,0},{3,5},{4,6},{5,3},{6,4},{7,1},{8,10},{9,15},{10,... | collective-permute-start | bytes 1544 | tf_op jit(solution)/shard_map/ppermute | solution.py:538
  33.8 4.5 %collective-permute-start.11 = (f32[1,128]{1,0:T(1,128)S(1)}, f32[1,128]{1,0:T(1,128)S(1)}, u32[]{:S(2)}, u32[]{:S(2)}) collective-permute-start(f32[1,128]{1,0:T(1,128)S(1)} %add_shares.1.refs_0_), channel_id=1, source_target_pairs={{0,4},{1,5},{2,6},{3,7},{4,0},{5,1},{6,2},{7,3},{8,12},{9,13},{10,... | collective-permute-start | bytes 1544 | tf_op jit(solution)/shard_map/ppermute | solution.py:537
  37.1 1.7 %collective-permute-start.13 = (f32[1,128]{1,0:T(1,128)S(1)}, f32[1,128]{1,0:T(1,128)S(1)}, u32[]{:S(2)}, u32[]{:S(2)}) collective-permute-start(f32[1,128]{1,0:T(1,128)S(1)} %collective-permute-done.12.refs_2_), channel_id=1, source_target_pairs={{0,1},{1,0},{2,3},{3,2},{4,5},{5,4},{6,7},{7,6},{8,9},{9,8},{10,11... | collective-permute-start | bytes 1544 | tf_op jit(solution)/shard_map/ppermute | solution.py:543
